TPU v7x, 256 devices: a whole 4x4x8 slice. The times are simulated.
256 devices in a mesh: row: 32 (over z, y_hi, core), col: 8 (over x, y_lo).
Axes of the slice: x: 4, y: 4 (y_hi: 2, y_lo: 2; y = y_hi * 2 + y_lo), z: 8, core: 2. Of those that a mesh axis runs over, the one named last changes fastest.
Arguments:
- homolog_embedding: float32 [128, 256, 256], P(None, 'row'), may hold values from -6 to 6
- pair_features: float32 [256, 256, 128], P('row', 'col'), may hold values from -6 to 6
- first_operand_matrix: float32 [256, 32], replicated, may hold values from -0.375 to 0.375
- second_operand_matrix: float32 [256, 32], replicated, may hold values from -0.375 to 0.375
- outer_output_weight: float32 [1024, 128], replicated, may hold values from -2 to 2
- triangle_input_weight: float32 [128, 512], replicated, may hold values from -0.5 to 0.5
- output_gate_weight: float32 [128, 128], replicated, may hold values from -0.5 to 0.5
- triangle_output_weight: float32 [128, 128], replicated, may hold values from -0.5 to 0.5
Outputs:
- pair_out: float32 [256, 256, 128], P('row', 'col')
All inputs are finite; a program needn't handle non-finite values.
Results may differ from a plain program's by a relative error of at most 0.000057.
Values sent between devices are 32-bit elements; how exact they have to be, the bound alone decides.
No kernel may reach another device: no remote copies, remote signals or barrier semaphores. Data moves between devices by JAX's collectives and lax.ppermute only.
A program may use at most 64 MiB of HBM per device.

v0:
```python
import jax
import jax.numpy as jnp
from jax import lax
from jax.sharding import PartitionSpec as P

epsilon = 1e-05
top_precision = lax.Precision.HIGHEST


def broadcast(value, axis, source):
    kept = jnp.where(lax.axis_index(axis) == source, value, 0).astype(value.dtype)
    return lax.psum(kept, axis)


def apply_layer_norm(values):
    average = jnp.mean(values, -1, keepdims=True)
    centred = values - average
    variance = jnp.mean(centred * centred, -1, keepdims=True)
    return centred * lax.rsqrt(variance + epsilon)


def per_device(
    homolog_embedding,
    pair_features,
    first_operand_matrix,
    second_operand_matrix,
    outer_output_weight,
    triangle_input_weight,
    output_gate_weight,
    triangle_output_weight,
):
    sequence_number = homolog_embedding.shape[0]
    row_count = pair_features.shape[0]
    col_count = pair_features.shape[1]
    owner_count = lax.axis_size("row") // lax.axis_size("col")
    column_index = lax.axis_index("col")
    normalized_input = apply_layer_norm(homolog_embedding)
    left_alignment_proj = jnp.einsum(
        "bxp,pg->bxg", normalized_input, first_operand_matrix, precision=top_precision
    )
    right_alignment_proj = jnp.einsum(
        "bxp,pg->bxg", normalized_input, second_operand_matrix, precision=top_precision
    )
    collected_rows = lax.all_gather(right_alignment_proj, "row", axis=1, tiled=True)
    right_factor_columns = lax.dynamic_slice_in_dim(
        collected_rows, column_index * col_count, col_count, 1
    )
    outer_product_total = (
        jnp.einsum(
            "emp,eqk->mqpk", left_alignment_proj, right_factor_columns, precision=top_precision
        )
        / sequence_number
    )
    flattened = outer_product_total.reshape(row_count, col_count, -1)
    pair_mid = pair_features + jnp.einsum(
        "ijf,fz->ijz", flattened, outer_output_weight, precision=top_precision
    )
    normed_pair = apply_layer_norm(pair_mid)
    hidden_width = triangle_output_weight.shape[0]
    projected = jnp.einsum(
        "ijz,zh->ijh", normed_pair, triangle_input_weight, precision=top_precision
    )
    left_edge = (
        jax.nn.sigmoid(projected[..., hidden_width : 2 * hidden_width])
        * projected[..., :hidden_width]
    )
    right_edge = (
        jax.nn.sigmoid(projected[..., 3 * hidden_width :])
        * projected[..., 2 * hidden_width : 3 * hidden_width]
    )
    gate_act = jax.nn.sigmoid(
        jnp.einsum("ijz,zy->ijy", normed_pair, output_gate_weight, precision=top_precision)
    )
    full_left, full_right = (
        lax.all_gather(left_edge, "col", axis=1, tiled=True),
        lax.all_gather(right_edge, "col", axis=1, tiled=True),
    )
    blocks_out = []
    for offset in range(owner_count):
        panel_rows = broadcast(full_right, "row", column_index * owner_count + offset)
        blocks_out.append(
            jnp.einsum("ikc,jkc->ijc", full_left, panel_rows, precision=top_precision)
        )
    mixed_edges = jnp.concatenate(blocks_out, 1)
    return pair_mid + gate_act * jnp.einsum(
        "ijc,cz->ijz",
        apply_layer_norm(mixed_edges),
        triangle_output_weight,
        precision=top_precision,
    )


def solution(mesh):
    placed = (P(None, "row", None), P("row", "col", None), P(), P(), P(), P(), P(), P())
    return jax.shard_map(
        per_device, mesh=mesh, in_specs=placed, out_specs=P("row", "col", None), check_vma=False
    )
```

profile of v0, /device:TPU:2, one launch (start us, length us, event | category | flops | bytes accessed | tf_op | source)
XLA Modules:
  0.0 507.4 jit_solution(2646786040914309708)
XLA Ops:
  6.5 1.6 reduce_sum.54
  8.1 1.6 multiply_reduce_fusion
  9.7 2.2 fusion.6
  12.0 0.9 copy.28
  13.0 1.0 fusion.4
  14.0 0.2 copy.29
  14.2 88.7 %all-gather.4.cloned.1.call-done = f32[128,256,32]{0,2,1:T(8,128)} async-done(((f32[128,8,32]{0,2,1:T(8,128)}), f32[128,256,32]{0,2,1:T(8,128)}) %all-gather.4.cloned.1.call-update) | async-done | bytes 4194320 | tf_op jit(solution)/shard_map/all_gather | solution.py:44
  102.9 6.0 %multiply_bitcast_fusion = f32[8,32,32,32]{2,3,0,1:T(8,128)} fusion(f32[128,256,32]{0,2,1:T(8,128)} %all-gather.4.cloned.1.call-done, s32[]{:T(128)S(6)} %select_n.29, f32[128,8,32]{0,2,1:T(8,128)S(1)} %copy.29), kind=kOutput, calls=%fused_computation | convolution fusion | flops 402915328 | bytes 1703940 | tf_op jit(solution)/shard_map/emp,eqk->mqpk/dot_general | solution.py:49
  108.9 5.6 %copy.30 = f32[8,32,32,32]{3,2,1,0:T(8,128)} copy(f32[8,32,32,32]{2,3,0,1:T(8,128)} %multiply_bitcast_fusion) | data formatting | bytes 2097152 | tf_op jit(solution)/shard_map/div | solution.py:49
  114.5 3.8 reshape.39
  118.3 1.1 fusion.45
  119.4 0.2 multiply_reduce_fusion.2
  119.6 0.6 fusion.17
  120.3 0.8 slice_multiply_fusion
  121.1 0.7 all-gather.8.cloned.1.call-update
  121.8 0.2 all-reduce.3.cloned.1.call-start
  122.0 36.0 %all-gather.6.cloned.1.call-done = f32[8,256,128]{2,1,0:T(8,128)} async-done(((f32[8,32,128]{2,1,0:T(8,128)}), f32[8,256,128]{2,1,0:T(8,128)}) %all-gather.6.cloned.1.call-update) | async-done | bytes 1048592 | tf_op jit(solution)/shard_map/all_gather | solution.py:76
  158.0 3.3 broadcast_select_fusion.3
  161.4 0.3 fusion.2
  161.7 39.4 %all-gather.8.cloned.1.call-done = f32[8,256,128]{2,1,0:T(8,128)} async-done(((f32[8,32,128]{2,1,0:T(8,128)}), f32[8,256,128]{2,1,0:T(8,128)}) %all-gather.8.cloned.1.call-update) | async-done | bytes 1048592 | tf_op jit(solution)/shard_map/all_gather | solution.py:75
  201.1 1.7 copy.32
  202.8 284.1 %all-reduce.3.cloned.1.call-done = (f32[8,256,128]{2,1,0:T(8,128)}, f32[8,256,128]{2,1,0:T(8,128)}, f32[8,256,128]{2,1,0:T(8,128)}, f32[8,256,128]{2,1,0:T(8,128)}) async-done(((f32[8,256,128]{2,1,0:T(8,128)}, f32[8,256,128]{2,1,0:T(8,128)}, f32[8,256,128]{2,1,0:T(8,128)}, f32[8,256,128]{2,1,0:T(8,128)}), (f32[8,256,128]{2,1,0:T(8,128)}, f32[8,256,128]{2,1,0:T(8,128)}, f32[8,256,128]{2,1,0:T(8,128)}, ...) | async-done | bytes 4194320 | tf_op jit(solution)/shard_map/psum | solution.py:12
  486.9 1.7 copy.31
  488.6 1.1 convolution_bitcast_fusion.3
  489.6 0.2 copy.39
  489.8 1.7 copy.33
  491.5 1.1 convolution_bitcast_fusion.2
  492.8 1.7 copy.35
  494.5 1.1 convolution_bitcast_fusion.1
  495.8 1.7 copy.37
  497.5 1.1 convolution_bitcast_fusion
  499.1 1.8 fusion.3
  (29 shorter events, 1.1 us)
Async XLA Ops:
  6.5 111.8 %copy-start = (f32[1024,128]{1,0:T(8,128)S(1)}, f32[1024,128]{1,0:T(8,128)}, u32[]{:S(2)}) copy-start(f32[1024,128]{1,0:T(8,128)} %param.12) | copy-start | bytes 1572868
  6.5 6.4 %copy-start.1 = (f32[128,8,256]{2,1,0:T(8,128)S(1)}, f32[128,8,256]{2,1,0:T(8,128)}, u32[]{:S(2)}) copy-start(f32[128,8,256]{2,1,0:T(8,128)} %param.8) | copy-start | bytes 3145732
  6.5 6.4 %copy-start.5 = (f32[256,32]{0,1:T(8,128)S(1)}, f32[256,32]{0,1:T(8,128)}, u32[]{:S(2)}) copy-start(f32[256,32]{0,1:T(8,128)} %param.10) | copy-start | bytes 98308
  6.5 96.3 %all-gather.4.cloned.1.call-start = ((), (), s32[]{:S(2)}) async-start(), calls=%async_computation | async-start | bytes 4325376 | tf_op jit(solution)/shard_map/all_gather | solution.py:44
  12.9 145.1 %all-gather.6.cloned.1.call-start = ((), (), s32[]{:S(2)}) async-start(), calls=%async_computation.1 | async-start | bytes 1179648 | tf_op jit(solution)/shard_map/all_gather | solution.py:76
  114.5 3.8 copy-start.3
  114.5 5.1 %copy-start.2 = (f32[128,512]{1,0:T(8,128)S(1)}, f32[128,512]{1,0:T(8,128)}, u32[]{:S(2)}) copy-start(f32[128,512]{1,0:T(8,128)} %param.13) | copy-start | bytes 786436
  121.0 80.1 %all-gather.8.cloned.1.call-start = ((), (), s32[]{:S(2)}) async-start(), calls=%async_computation.2 | async-start | bytes 1179648 | tf_op jit(solution)/shard_map/all_gather | solution.py:75
  121.8 365.1 %all-reduce.3.cloned.1.call-start = ((), (), s32[]{:S(2)}) async-start(), calls=%async_computation.3 | async-start | bytes 8388608 | tf_op jit(solution)/shard_map/psum | solution.py:12
  122.0 39.4 %copy-start.4 = (f32[128,128]{1,0:T(8,128)S(1)}, f32[128,128]{1,0:T(8,128)}, u32[]{:S(2)}) copy-start(f32[128,128]{1,0:T(8,128)} %param.14) | copy-start | bytes 196612
Sparse Core Ops, SparseCore 0:
  13.0 89.7 all-gather.3
  121.2 36.8 all-gather.5
  159.8 41.2 all-gather.7
  203.8 282.9 all-reduce.2
where the time goes:
time: 509 us; the launch traced here: 507 us
  waiting for transfers between devices  449 us (88%)
  local copies, waits for them, and re-layouts  19.8 us (4%)
  matrix products  17.4 us (3%)
  between operations  13.4 us (3%)
  other arithmetic  7.77 us (2%)
    psum x1, waiting for transfers between devices, broadcast(): return lax.psum(kept, axis)  284 us
    all_gather x1, waiting for transfers between devices, per_device(): lax.all_gather(right_alignment_proj, 'row', axis=1, tiled=True)  88.7 us
    all_gather x1, waiting for transfers between devices, per_device(): lax.all_gather(left_edge, 'col', axis=1, tiled=True)  39.4 us
    all_gather x1, waiting for transfers between devices, per_device(): lax.all_gather(right_edge, 'col', axis=1, tiled=True)  36 us
  transfers between devices with their start and end apart: 4, of which 4 were waited for; matrix products, arithmetic and copies ran while one was open for 1% of the time, Pallas kernels for 0%

commit v1 on v0

v1 whole, which is shorter than its diff:
```python
import jax
import jax.numpy as jnp
from jax import lax
from jax.sharding import Mesh, PartitionSpec as P

epsilon = 1e-05
top_precision = lax.Precision.HIGHEST

ALL = ("z", "yh", "core", "x", "yl")
ROW = ("z", "yh", "core")
COL = ("x", "yl")
LAYER = ("z", "x", "yl")
QUAD = ("yh", "core")


def apply_layer_norm(values):
    average = jnp.mean(values, -1, keepdims=True)
    centred = values - average
    variance = jnp.mean(centred * centred, -1, keepdims=True)
    return centred * lax.rsqrt(variance + epsilon)


def ring_distance(a, b, n):
    d = (a - b) % n
    return min(d, n - d)


def panel_permutation():
    pairs = []
    for c in range(8):
        targets = sorted(range(8), key=lambda z: -ring_distance(z, c, 8))
        sources = sorted(
            range(8), key=lambda k: ring_distance(k // 2, c // 2, 4) + abs(k % 2 - c % 2)
        )
        for z, k in zip(targets, sources):
            for o in range(4):
                pairs.append(((c * 4 + o) * 8 + k, (z * 4 + o) * 8 + c))
    return pairs


def per_device(homolog, pair, w_first, w_second, w_outer, w_tri, w_gate, w_out):
    normed = apply_layer_norm(homolog)
    right = jnp.einsum("sip,pg->sig", normed, w_second, precision=top_precision)
    moved = lax.ppermute(right, ALL, panel_permutation())
    left = jnp.einsum("sip,pg->sig", normed, w_first, precision=top_precision)
    panel = lax.all_gather(moved, QUAD, axis=1, tiled=True)
    outer = jnp.einsum("sia,sjb->ijab", left, panel, precision=top_precision) / 128.0
    pair_mid = pair.reshape(256, 128) + jnp.dot(
        outer.reshape(256, 1024), w_outer, precision=top_precision
    )
    normed_pair = apply_layer_norm(pair_mid)
    w4 = w_tri.reshape(128, 2, 2, 64, 2)
    w_p = w4[:, :, 0].transpose(2, 1, 3, 0).reshape(256, 128)
    w_g = w4[:, :, 1].transpose(2, 1, 3, 0).reshape(256, 128)
    p_t = jnp.einsum("hz,pz->hp", w_p, normed_pair, precision=top_precision)
    g_t = jnp.einsum("hz,pz->hp", w_g, normed_pair, precision=top_precision)
    edges = jax.nn.sigmoid(g_t) * p_t
    gate = jax.nn.sigmoid(jnp.dot(normed_pair, w_gate, precision=top_precision))
    swapped = lax.all_to_all(edges.reshape(64, 4, 256), LAYER, 0, 0, tiled=True)
    rights = lax.all_gather(swapped[:, 2:], QUAD, axis=0)
    left_e = swapped[:, :2].reshape(8, 8, 2, 8, 32).transpose(2, 0, 3, 1, 4).reshape(2, 64, 256)
    right_e = (
        rights.reshape(4, 8, 8, 2, 8, 32).transpose(3, 1, 0, 4, 2, 5).reshape(2, 256, 256)
    )
    mixed = jnp.einsum("cik,cjk->cij", left_e, right_e, precision=top_precision)
    back = mixed.reshape(2, 8, 8, 8, 32).transpose(1, 3, 0, 2, 4).reshape(64, 2, 256)
    mixed_t = lax.all_to_all(back, LAYER, 0, 0, tiled=True).reshape(128, 256)
    update = jnp.dot(apply_layer_norm(mixed_t.T), w_out, precision=top_precision)
    return (pair_mid + gate * update).reshape(8, 32, 128)


def solution(mesh):
    fine = Mesh(mesh.devices.reshape(8, 2, 2, 4, 2), ALL)
    placed = (P(None, ROW, None), P(ROW, COL, None), P(), P(), P(), P(), P(), P())
    return jax.shard_map(
        per_device, mesh=fine, in_specs=placed, out_specs=P(ROW, COL, None), check_vma=False
    )
```

time: 509 us -> 159 us (0.31)
  waiting for transfers between devices: 449 us -> 31.9 us
  blocking collectives: 0 us -> 70.2 us
  between operations: 13.4 us -> 0.28 us
  starting transfers between devices: 0.3 us -> 12.8 us
  matrix products: 17.4 us -> 22.6 us
    psum x1 -> x0, waiting for transfers between devices: 284 us -> none  [broadcast(): return lax.psum(kept, axis)]
    all_gather x3 -> x0, waiting for transfers between devices: 164 us -> none  [the longest x1 88.7 us: per_device(): lax.all_gather(right_alignment_proj, 'row', axis=1, tiled=True)]
    all_to_all x0 -> x1, blocking collectives: none -> 43.9 us  [per_device(): swapped = lax.all_to_all(edges.reshape(64, 4, 256), LAYER, 0, 0, tiled=True)]
    all_gather x0 -> x2, blocking collectives: none -> 26.3 us  [the longest x1 17.6 us: per_device(): panel = lax.all_gather(moved, QUAD, axis=1, tiled=True)]
    ppermute x0 -> x1, waiting for transfers between devices: none -> 21.9 us  [per_device(): moved = lax.ppermute(right, ALL, panel_permutation())]
    all_to_all x0 -> x1, waiting for transfers between devices: none -> 9.98 us  [per_device(): mixed_t = lax.all_to_all(back, LAYER, 0, 0, tiled=True).reshape(128, 256)]
    reshape x1 -> x13, local copies, waits for them, and re-layouts: 3.8 us -> 10.7 us  [the longest x3 4.94 us: per_device(): rights.reshape(4, 8, 8, 2, 8, 32).transpose(3, 1, 0, 4, 2, 5)]
    psum x4 -> x0, local copies, waits for them, and re-layouts: 6.84 us -> none  [broadcast(): return lax.psum(kept, axis)]
  transfers between devices with their start and end apart: 4 -> 2, of which waited for: 4 -> 2; matrix products, arithmetic and copies ran while one was open for 1% -> 1% of each run, Pallas kernels for 0% -> 0%
where the time goes in v1:
time: 159 us; the launch traced here: 158 us
  blocking collectives  70.2 us (44%)
  waiting for transfers between devices  31.9 us (20%)
  matrix products  22.6 us (14%)
  local copies, waits for them, and re-layouts  16.9 us (11%)
  starting transfers between devices  12.8 us (8%)
  other arithmetic  3.51 us (2%)
    all_to_all x1, blocking collectives, per_device(): swapped = lax.all_to_all(edges.reshape(64, 4, 256), LAYER, 0, 0, tiled=True)  43.9 us
    ppermute x1, waiting for transfers between devices, per_device(): moved = lax.ppermute(right, ALL, panel_permutation())  21.9 us
    all_gather x1, blocking collectives, per_device(): panel = lax.all_gather(moved, QUAD, axis=1, tiled=True)  17.6 us
    dot_general x1, matrix products, per_device(): jnp.einsum('sia,sjb->ijab', left, panel, precision=top_precision) / 128.0  16.5 us
    all_to_all x1, waiting for transfers between devices, per_device(): mixed_t = lax.all_to_all(back, LAYER, 0, 0, tiled=True).reshape(128, 256)  9.98 us
    all_gather x1, blocking collectives, per_device(): rights = lax.all_gather(swapped[:, 2:], QUAD, axis=0)  8.74 us
    ppermute x1, starting transfers between devices, per_device(): moved = lax.ppermute(right, ALL, panel_permutation())  6.8 us
    all_to_all x1, starting transfers between devices, per_device(): mixed_t = lax.all_to_all(back, LAYER, 0, 0, tiled=True).reshape(128, 256)  5.97 us
  transfers between devices with their start and end apart: 2, of which 2 were waited for; matrix products, arithmetic and copies ran while one was open for 1% of the time, Pallas kernels for 0%

profile of v1, /device:TPU:2, one launch (start us, length us, event | category | flops | bytes accessed | tf_op | source)
XLA Modules:
  0.0 158.2 jit_solution(14860706793385623864)
XLA Ops:
  0.0 1.6 reduce_sum.54
  1.6 1.6 %multiply_reduce_fusion = f32[128,8]{1,0:T(8,128)S(1)} fusion(f32[128,8,256]{2,1,0:T(8,128)} %param.8, f32[128,8]{1,0:T(8,128)S(1)} %broadcast_multiply_fusion), kind=kLoop, calls=%fused_computation.16 | loop fusion | flops 785408 | bytes 1056768 | tf_op jit(solution)/shard_map/reduce_sum | solution.py:19
  3.2 1.0 fusion.11
  4.3 6.8 %collective-permute-start = (f32[128,8,32]{2,1,0:T(8,128)S(1)}, f32[128,8,32]{2,1,0:T(8,128)S(1)}, u32[]{:S(2)}, u32[]{:S(2)}) collective-permute-start(f32[128,8,32]{2,1,0:T(8,128)S(1)} %fusion.11), channel_id=1, source_target_pairs={{0,128},{8,136},{16,144},{24,152},{1,96},{9,104},{17,112},{25,120}... | collective-permute-start | bytes 393224 | tf_op jit(solution)/shard_map/ppermute | solution.py:44
  11.1 1.0 fusion.9
  12.1 0.2 copy.29
  12.3 0.1 copy.31
  12.6 21.9 %collective-permute-done = f32[128,8,32]{2,1,0:T(8,128)S(1)} collective-permute-done((f32[128,8,32]{2,1,0:T(8,128)S(1)}, f32[128,8,32]{2,1,0:T(8,128)S(1)}, u32[]{:S(2)}, u32[]{:S(2)}) %collective-permute-start) | collective-permute-done | bytes 131104 | tf_op jit(solution)/shard_map/ppermute | solution.py:44
  34.5 17.6 %all_gather.9 = f32[128,32,32]{2,1,0:T(8,128)S(1)} all-gather(f32[128,8,32]{2,1,0:T(8,128)S(1)} %collective-permute-done), channel_id=1, replica_groups=mesh['z'=8,'yh'=2,'core'=2,'x'=4,'yl'=2] {'yh','core'}, dimensions={1}, use_global_device_ids=true | all-gather | bytes 655360 | tf_op jit(solution)/shard_map/all_gather | solution.py:46
  52.1 16.5 %multiply_bitcast_fusion = f32[8,32,32,32]{2,3,0,1:T(8,128)} fusion(f32[128,32,32,1]{2,1,0,3:T(8,128)S(1)} %bitcast.54, f32[128,8,32]{0,2,1:T(8,128)S(1)} %copy.29), kind=kOutput, calls=%fused_computation | convolution fusion | flops 402915328 | bytes 1703936 | tf_op jit(solution)/shard_map/sia,sjb->ijab/dot_general | solution.py:47
  68.6 5.6 %copy.30 = f32[8,32,32,32]{3,2,1,0:T(8,128)} copy(f32[8,32,32,32]{2,3,0,1:T(8,128)} %multiply_bitcast_fusion) | data formatting | bytes 2097152 | tf_op jit(solution)/shard_map/div | solution.py:47
  74.2 3.8 %reshape.79 = f32[256,1024]{1,0:T(8,128)S(1)} reshape(f32[8,32,32,32]{3,2,1,0:T(8,128)} %copy.30) | data formatting | bytes 2097152 | tf_op jit(solution)/shard_map/reshape | solution.py:49
  78.1 1.1 fusion.33
  79.1 0.2 multiply_reduce_fusion.2
  79.3 0.5 fusion.4
  79.9 0.5 fusion.1
  80.4 43.9 %all_to_all.10 = f32[64,4,256]{2,1,0:T(4,128)S(1)} all-to-all(f32[64,4,256]{2,1,0:T(4,128)S(1)} %reshape.83), channel_id=1, replica_groups=mesh['z'=8,'yh'=2,'core'=2,'x'=4,'yl'=2] {'z','x','yl'}, dimensions={0} | all-to-all | bytes 524288 | tf_op jit(solution)/shard_map/all_to_all | solution.py:59
  124.4 8.7 %all-gather = f32[256,2,256]{2,1,0:T(2,128)S(1)} all-gather(f32[64,2,256]{2,1,0:T(2,128)S(1)} %get-tuple-element.5), channel_id=2, replica_groups=mesh['z'=8,'yh'=2,'core'=2,'x'=4,'yl'=2] {'yh','core'}, dimensions={0}, use_global_device_ids=true | all-gather | bytes 655360 | tf_op jit(solution)/shard_map/all_gather | solution.py:60
  133.2 0.8 reshape.86
  134.0 2.0 %copy.46 = f32[4,8,8,2,8,32]{5,2,4,0,1,3:T(8,128)} copy(f32[4,8,8,2,8,32]{5,4,3,2,1,0:T(8,128)S(1)} %reshape.86) | data formatting | bytes 1048576 | tf_op jit(solution)/shard_map/reshape | solution.py:63
  136.0 2.1 %reshape.87 = f32[2,256,256]{2,1,0:T(8,128)S(1)} reshape(f32[2,8,4,8,8,32]{5,4,3,2,1,0:T(8,128)} %bitcast.55) | data formatting | bytes 1048576 | tf_op jit(solution)/shard_map/reshape | solution.py:63
  138.1 0.2 reshape.84
  138.3 0.2 copy.48
  138.5 0.2 reshape.85
  138.7 0.6 fusion.34
  139.3 0.2 reshape.88
  139.6 0.2 reshape.89
  139.8 0.8 copy.37
  140.5 6.0 %all-to-all-start.1 = ((f32[64,2,256]{2,1,0:T(2,128)}), f32[64,2,256]{2,1,0:T(2,128)S(1)}, u32[]{:S(2)}, u32[]{:S(2)}) async-start(f32[64,2,256]{2,1,0:T(2,128)} %copy.37), calls=%async_computation.1 | async-start | bytes 262144 | tf_op jit(solution)/shard_map/all_to_all | solution.py:67
  146.5 0.3 fusion.7
  146.9 10.0 %all-to-all-done.1 = f32[64,2,256]{2,1,0:T(2,128)S(1)} async-done(((f32[64,2,256]{2,1,0:T(2,128)}), f32[64,2,256]{2,1,0:T(2,128)S(1)}, u32[]{:S(2)}, u32[]{:S(2)}) %all-to-all-start.1) | async-done | bytes 131104 | tf_op jit(solution)/shard_map/all_to_all | solution.py:67
  157.1 1.1 fusion.8
  (31 shorter events, 0.7 us)
Async XLA Ops:
  0.0 78.0 %copy-start = (f32[1024,128]{1,0:T(8,128)S(1)}, f32[1024,128]{1,0:T(8,128)}, u32[]{:S(2)}) copy-start(f32[1024,128]{1,0:T(8,128)} %param.12) | copy-start | bytes 1572868
  0.0 3.2 %copy-start.1 = (f32[128,8,256]{2,1,0:T(8,128)S(1)}, f32[128,8,256]{2,1,0:T(8,128)}, u32[]{:S(2)}) copy-start(f32[128,8,256]{2,1,0:T(8,128)} %param.8) | copy-start | bytes 3145732
  0.0 3.2 %copy-start.6 = (f32[256,32]{0,1:T(8,128)S(1)}, f32[256,32]{0,1:T(8,128)}, u32[]{:S(2)}) copy-start(f32[256,32]{0,1:T(8,128)} %param.11) | copy-start | bytes 98308
  0.0 11.1 %copy-start.7 = (f32[256,32]{0,1:T(8,128)S(1)}, f32[256,32]{0,1:T(8,128)}, u32[]{:S(2)}) copy-start(f32[256,32]{0,1:T(8,128)} %param.10) | copy-start | bytes 98308
  3.2 9.1 %copy-start.2 = (f32[128,512]{1,0:T(8,128)S(1)}, f32[128,512]{1,0:T(8,128)}, u32[]{:S(2)}) copy-start(f32[128,512]{1,0:T(8,128)} %param.13) | copy-start | bytes 786436
  4.3 30.2 %collective-permute-start = (f32[128,8,32]{2,1,0:T(8,128)S(1)}, f32[128,8,32]{2,1,0:T(8,128)S(1)}, u32[]{:S(2)}, u32[]{:S(2)}) collective-permute-start(f32[128,8,32]{2,1,0:T(8,128)S(1)} %fusion.11), channel_id=1, source_target_pairs={{0,128},{8,136},{16,144},{24,152},{1,96},{9,104},{17,112},{25,120}... | collective-permute-start | bytes 393224 | tf_op jit(solution)/shard_map/ppermute | solution.py:44
  74.2 3.8 %copy-start.3 = (f32[8,32,128]{2,1,0:T(8,128)S(1)}, f32[8,32,128]{2,1,0:T(8,128)}, u32[]{:S(2)}) copy-start(f32[8,32,128]{2,1,0:T(8,128)} %param.9) | copy-start | bytes 393220
  138.5 8.0 %copy-start.5 = (f32[128,128]{1,0:T(8,128)S(1)}, f32[128,128]{1,0:T(8,128)}, u32[]{:S(2)}) copy-start(f32[128,128]{1,0:T(8,128)} %param.14) | copy-start | bytes 196612
  139.3 17.8 %copy-start.4 = (f32[128,128]{1,0:T(8,128)S(1)}, f32[128,128]{1,0:T(8,128)}, u32[]{:S(2)}) copy-start(f32[128,128]{1,0:T(8,128)} %param.15) | copy-start | bytes 196612
  140.5 16.3 %all-to-all-start.1 = ((f32[64,2,256]{2,1,0:T(2,128)}), f32[64,2,256]{2,1,0:T(2,128)S(1)}, u32[]{:S(2)}, u32[]{:S(2)}) async-start(f32[64,2,256]{2,1,0:T(2,128)} %copy.37), calls=%async_computation.1 | async-start | bytes 262144 | tf_op jit(solution)/shard_map/all_to_all | solution.py:67

commit v2 on v1

v2 whole, which is shorter than its diff:
```python
import jax
import jax.numpy as jnp
from jax import lax
from jax.experimental import pallas as pl
from jax.experimental.pallas import tpu as pltpu
from jax.sharding import Mesh, PartitionSpec as P

epsilon = 1e-05
top_precision = lax.Precision.HIGHEST

ALL = ("z", "yh", "core", "x", "yl")
ROW = ("z", "yh", "core")
COL = ("x", "yl")
LAYER = ("z", "x", "yl")
QUAD = ("yh", "core")
VMEM_LIMIT = 32 * 1024 * 1024


def ring_distance(a, b, n):
    d = (a - b) % n
    return min(d, n - d)


def panel_permutation():
    pairs = []
    for c in range(8):
        targets = sorted(range(8), key=lambda z: -ring_distance(z, c, 8))
        sources = sorted(
            range(8), key=lambda k: ring_distance(k // 2, c // 2, 4) + abs(k % 2 - c % 2)
        )
        for z, k in zip(targets, sources):
            for o in range(4):
                pairs.append(((c * 4 + o) * 8 + k, (z * 4 + o) * 8 + c))
    return pairs


def dot(a, b):
    return jnp.dot(a, b, precision=top_precision, preferred_element_type=jnp.float32)


def dot_t(a, b):
    return lax.dot_general(
        a, b, (((1,), (1,)), ((), ())), precision=top_precision, preferred_element_type=jnp.float32
    )


def layer_norm(values, axis):
    average = jnp.mean(values, axis, keepdims=True)
    centred = values - average
    variance = jnp.mean(centred * centred, axis, keepdims=True)
    return centred * lax.rsqrt(variance + epsilon)


def sigmoid(x):
    return 1.0 / (1.0 + jnp.exp(-x))


def factor_kernel(msa_ref, w_ref, left_ref, right_ref):
    w = w_ref[...]
    for i in range(8):
        normed = layer_norm(msa_ref[:, i, :], -1)
        both = dot_t(w, normed)
        left_ref[pl.ds(i * 32, 32), :] = both[:32] * (1.0 / 128.0)
        right_ref[pl.ds(i, 32, stride=8), :] = both[32:]


def pair_kernel(
    left_ref, panel_ref, pair_ref, w_outer_ref, w_tri_ref, w_gate_ref,
    edges_ref, mid_ref, gate_ref, outer_ref, flat_ref,
):
    outer_ref[...] = dot_t(panel_ref[...], left_ref[...])
    lane = lax.broadcasted_iota(jnp.int32, (8, 128), 1)
    low_half = lane < 64
    even = (lane // 32) % 2 == 0
    for o in range(4):
        for bh in range(8):
            for ih in range(2):
                v = [
                    outer_ref[pl.ds((o * 32 + bh * 4 + b) * 8, 8), pl.ds(ih * 128, 128)]
                    for b in range(4)
                ]
                for p in range(2):
                    a, c = v[p], v[p + 2]
                    v[p] = jnp.where(low_half, a, pltpu.roll(c, 64, 1))
                    v[p + 2] = jnp.where(low_half, pltpu.roll(a, 64, 1), c)
                for p in (0, 2):
                    a, c = v[p], v[p + 1]
                    v[p] = jnp.where(even, a, pltpu.roll(c, 32, 1))
                    v[p + 1] = jnp.where(even, pltpu.roll(a, 96, 1), c)
                for il in range(4):
                    i = ih * 4 + il
                    flat_ref[pl.ds((i * 4 + o) * 8, 8), pl.ds(bh * 128, 128)] = v[il]
    mid = pair_ref[...] + dot(flat_ref[...], w_outer_ref[...])
    mid_ref[...] = mid
    normed = layer_norm(mid, -1)
    projected = dot_t(w_tri_ref[...], normed)
    for side in range(2):
        plain, gating = projected[side * 256 :][:128], projected[side * 256 + 128 :][:128]
        edge = sigmoid(gating) * plain
        for h in range(2):
            edges_ref[:, pl.ds((side * 2 + h) * 256, 256)] = edge[h * 64 : h * 64 + 64]
    gate_ref[...] = sigmoid(dot(normed, w_gate_ref[...]))


def swap_blocks(x, sub, lane):
    a, b = x[:, :128], x[:, 128:]
    upper = sub >= 4
    a, b = jnp.where(upper, pltpu.roll(b, 4, 0), a), jnp.where(upper, b, pltpu.roll(a, 4, 0))
    out = []
    for v in (a, b):
        for bit, width in ((2, 64), (1, 32)):
            s = (sub // bit) % 2
            l = (lane // width) % 2
            from_below = pltpu.roll(pltpu.roll(v, 8 - bit, 0), width, 1)
            from_above = pltpu.roll(pltpu.roll(v, bit, 0), 128 - width, 1)
            v = jnp.where(s == l, v, jnp.where(s < l, from_below, from_above))
        out.append(v)
    return jnp.concatenate(out, 1)


def triangle_kernel(left_ref, right_ref, out_ref, l_ref, r_ref):
    sub = lax.broadcasted_iota(jnp.int32, (8, 128), 0)
    lane = lax.broadcasted_iota(jnp.int32, (8, 128), 1)
    for h in range(2):
        for z in range(8):
            x = left_ref[pl.ds(z * 8, 8), pl.ds(h * 256, 256)]
            l_ref[pl.ds(z * 8, 8), :] = swap_blocks(x, sub, lane)
            for o in range(4):
                y = right_ref[pl.ds(o * 64 + z * 8, 8), pl.ds(h * 256, 256)]
                r_ref[pl.ds(z * 32 + o * 8, 8), :] = swap_blocks(y, sub, lane)
        mixed = dot_t(l_ref[...], r_ref[...])
        for z in range(8):
            out_ref[pl.ds(z * 8, 8), pl.ds(h * 256, 256)] = swap_blocks(
                mixed[z * 8 : z * 8 + 8], sub, lane
            )


def output_kernel(mixed_ref, mid_ref, gate_ref, w_ref, out_ref):
    mixed = jnp.concatenate([mixed_ref[:, :256], mixed_ref[:, 256:]], 0)
    normed = layer_norm(mixed, 0)
    out_ref[...] = mid_ref[...] + gate_ref[...] * dot(normed.T, w_ref[...])


def call(kernel, out_shapes, scratch, *args):
    shapes = [jax.ShapeDtypeStruct(s, jnp.float32) for s in out_shapes]
    return pl.pallas_call(
        kernel,
        out_shape=shapes if len(shapes) > 1 else shapes[0],
        scratch_shapes=[pltpu.VMEM(s, jnp.float32) for s in scratch],
        compiler_params=pltpu.CompilerParams(vmem_limit_bytes=VMEM_LIMIT),
    )(*args)


def factors(homolog, w_both):
    return call(factor_kernel, [(256, 128), (256, 128)], [], homolog, w_both)


def pair_stage(left, panel, pair, w_outer, w_tri, w_gate):
    return call(
        pair_kernel,
        [(64, 1024), (256, 128), (256, 128)],
        [(1024, 256), (256, 1024)],
        left, panel, pair, w_outer, w_tri, w_gate,
    )


def triangle(left, right):
    return call(triangle_kernel, [(64, 512)], [(64, 256), (256, 256)], left, right)


def output_stage(mixed, mid, gate, w_out):
    return call(output_kernel, [(256, 128)], [], mixed, mid, gate, w_out)


def per_device(homolog, pair, w_first, w_second, w_outer, w_tri, w_gate, w_out):
    w_both = jnp.concatenate([w_first, w_second], 1).T
    left, right = factors(homolog, w_both)
    moved = lax.ppermute(right, ALL, panel_permutation())
    w_outer_ba = w_outer.reshape(32, 32, 128).transpose(1, 0, 2).reshape(1024, 128)
    panel = lax.all_gather(moved, QUAD, axis=0, tiled=True)
    edges, mid, gate = pair_stage(
        left, panel, pair.reshape(256, 128), w_outer_ba, w_tri.T, w_gate
    )
    swapped = lax.all_to_all(edges, LAYER, 0, 0, tiled=True)
    rights = lax.all_gather(swapped[:, 512:], QUAD, axis=0, tiled=True)
    back = triangle(swapped, rights)
    mixed = lax.all_to_all(back, LAYER, 0, 0, tiled=True)
    return output_stage(mixed, mid, gate, w_out).reshape(8, 32, 128)


def solution(mesh):
    fine = Mesh(mesh.devices.reshape(8, 2, 2, 4, 2), ALL)
    placed = (P(None, ROW, None), P(ROW, COL, None), P(), P(), P(), P(), P(), P())
    return jax.shard_map(
        per_device, mesh=fine, in_specs=placed, out_specs=P(ROW, COL, None), check_vma=False
    )
```

time: 159 us -> 87.4 us (0.55)
  waiting for transfers between devices: 31.9 us -> 5.09 us
  matrix products: 22.6 us -> 0 us
  local copies, waits for them, and re-layouts: 16.9 us -> 2.98 us
  Pallas kernels: 0 us -> 9.32 us
  blocking collectives: 70.2 us -> 61.5 us
  starting transfers between devices: 12.8 us -> 6.79 us
  other arithmetic: 3.51 us -> 0.78 us
    dot_general x9 -> x0, matrix products: 22.6 us -> none  [the longest x1 16.5 us: per_device(): jnp.einsum('sia,sjb->ijab', left, panel, precision=top_precision) / 128.0]
    ppermute x1, waiting for transfers between devices: 21.9 us -> 5.09 us  [per_device(): moved = lax.ppermute(right, ALL, panel_permutation())]
    reshape x13 -> x1, local copies, waits for them, and re-layouts: 10.7 us -> 0.31 us  [per_device(): w_outer.reshape(32, 32, 128).transpose(1, 0, 2).reshape(1024, 128)]
    all_to_all x1 -> x0, waiting for transfers between devices: 9.98 us -> none  [per_device(): mixed_t = lax.all_to_all(back, LAYER, 0, 0, tiled=True).reshape(128, 256)]
    pallas_call x0 -> x4, Pallas kernels: none -> 9.32 us  [call(): pl.pallas_call(kernel, out_shape=shapes if len(shapes) > 1 else shapes[0]...]
    all_gather x2, blocking collectives: 26.3 us -> 17.4 us  [the longest x1 8.86 us: per_device(): panel = lax.all_gather(moved, QUAD, axis=0, tiled=True)]
    all_to_all x1 -> x0, starting transfers between devices: 5.97 us -> none  [per_device(): mixed_t = lax.all_to_all(back, LAYER, 0, 0, tiled=True).reshape(128, 256)]
    div x1 -> x0, local copies, waits for them, and re-layouts: 5.63 us -> none  [per_device(): jnp.einsum('sia,sjb->ijab', left, panel, precision=top_precision) / 128.0]
  transfers between devices with their start and end apart: 2 -> 1, of which waited for: 2 -> 1; matrix products, arithmetic and copies ran while one was open for 1% -> 0% of each run, Pallas kernels for 0% -> 0%
where the time goes in v2:
time: 87.4 us; the launch traced here: 86.6 us
  blocking collectives  61.5 us (70%)
  Pallas kernels  9.32 us (11%)
  starting transfers between devices  6.79 us (8%)
  waiting for transfers between devices  5.09 us (6%)
  local copies, waits for them, and re-layouts  2.98 us (3%)
    all_to_all x1, blocking collectives, per_device(): swapped = lax.all_to_all(edges, LAYER, 0, 0, tiled=True)  28.1 us
    all_to_all x1, blocking collectives, per_device(): mixed = lax.all_to_all(back, LAYER, 0, 0, tiled=True)  16.1 us
    pallas_call x4, Pallas kernels, call(): pl.pallas_call(kernel, out_shape=shapes if len(shapes) > 1 else shapes[0]...  9.32 us
    all_gather x1, blocking collectives, per_device(): panel = lax.all_gather(moved, QUAD, axis=0, tiled=True)  8.86 us
    all_gather x1, blocking collectives, per_device(): rights = lax.all_gather(swapped[:, 512:], QUAD, axis=0, tiled=True)  8.51 us
    ppermute x1, starting transfers between devices, per_device(): moved = lax.ppermute(right, ALL, panel_permutation())  6.79 us
    ppermute x1, waiting for transfers between devices, per_device(): moved = lax.ppermute(right, ALL, panel_permutation())  5.09 us
    unnamed x15, local copies, waits for them, and re-layouts  2.25 us
  transfers between devices with their start and end apart: 1, of which 1 were waited for; matrix products, arithmetic and copies ran while one was open for 0% of the time, Pallas kernels for 0%

profile of v2, /device:TPU:2, one launch (start us, length us, event | category | flops | bytes accessed | tf_op | source)
XLA Modules:
  0.0 86.6 jit_solution(13391371405901971569)
XLA Ops:
  0.0 0.8 maximum_bitcast_fusion.w_ref
  0.8 0.0 copy-start
  0.8 1.2 %copy-done = f32[128,8,256]{2,1,0:T(8,128)S(1)} copy-done((f32[128,8,256]{2,1,0:T(8,128)S(1)}, f32[128,8,256]{2,1,0:T(8,128)}, u32[]{:S(2)}) %copy-start) | copy-done | bytes 1048600
  2.0 0.0 copy-start.5
  2.0 1.5 %shard_map.82 = (f32[256,128]{1,0:T(8,128)S(1)}, f32[256,128]{1,0:T(8,128)S(1)}) custom-call(f32[128,8,256]{2,1,0:T(8,128)S(1)} %copy-done, f32[64,256]{1,0:T(8,128)S(1)} %maximum_bitcast_fusion.w_ref), custom_call_target="tpu_custom_call" | custom-call | tf_op jit(solution)/shard_map/pallas_call | solution.py:146
  3.5 0.0 copy-start.4
  3.5 6.8 %collective-permute-start = (f32[256,128]{1,0:T(8,128)S(1)}, f32[256,128]{1,0:T(8,128)S(1)}, u32[]{:S(2)}, u32[]{:S(2)}) collective-permute-start(f32[256,128]{1,0:T(8,128)S(1)} %get-tuple-element.11), channel_id=1, source_target_pairs={{0,128},{8,136},{16,144},{24,152},{1,96},{9,104},{17,112},{25,120}... | collective-permute-start | bytes 393224 | tf_op jit(solution)/shard_map/ppermute | solution.py:178
  10.3 0.0 copy-done.5
  10.3 0.1 copy.12
  10.4 0.0 copy-done.4
  10.4 0.3 copy.11
  10.7 0.0 copy-start.1
  10.7 0.0 copy-start.2
  10.7 5.1 %collective-permute-done = f32[256,128]{1,0:T(8,128)S(1)} collective-permute-done((f32[256,128]{1,0:T(8,128)S(1)}, f32[256,128]{1,0:T(8,128)S(1)}, u32[]{:S(2)}, u32[]{:S(2)}) %collective-permute-start) | collective-permute-done | bytes 131104 | tf_op jit(solution)/shard_map/ppermute | solution.py:178
  15.8 8.9 %all_gather.6.panel_ref = f32[1024,128]{1,0:T(8,128)S(1)} all-gather(f32[256,128]{1,0:T(8,128)S(1)} %collective-permute-done), channel_id=1, replica_groups=mesh['z'=8,'yh'=2,'core'=2,'x'=4,'yl'=2] {'yh','core'}, dimensions={0}, use_global_device_ids=true | all-gather | bytes 655360 | tf_op jit(solution)/shard_map/all_gather | solution.py:180
  24.7 0.0 copy-done.1
  24.7 0.0 copy-done.2
  24.7 4.5 %shard_map.83 = (f32[64,1024]{1,0:T(8,128)S(1)}, f32[256,128]{1,0:T(8,128)S(1)}, f32[256,128]{1,0:T(8,128)S(1)}) custom-call(f32[256,128]{1,0:T(8,128)S(1)} %get-tuple-element.10.left_ref, f32[1024,128]{1,0:T(8,128)S(1)} %all_gather.6.panel_ref, f32[256,128]{1,0:T(8,128)S(1)} %bitcast.24, f32[1024,128]{1,0:T(8,128)S(1)} %bitcast.17, ...), custom_call_target="tpu_custom_call" | custom-call | tf_op jit(solution)/shard_map/pallas_call | solution.py:146
  29.2 0.3 copy.13
  29.4 28.1 %all_to_all.22 = f32[64,1,1024]{2,1,0:T(1,128)S(1)} all-to-all(f32[64,1,1024]{2,1,0:T(1,128)S(1)} %copy.13), channel_id=1, replica_groups=mesh['z'=8,'yh'=2,'core'=2,'x'=4,'yl'=2] {'z','x','yl'}, dimensions={0} | all-to-all | bytes 524288 | tf_op jit(solution)/shard_map/all_to_all | solution.py:184
  57.6 8.5 %all_gather.7.right_ref = f32[256,512]{1,0:T(8,128)S(1)} all-gather(f32[64,512]{1,0:T(8,128)S(1)} %slice.4), channel_id=1, replica_groups=mesh['z'=8,'yh'=2,'core'=2,'x'=4,'yl'=2] {'yh','core'}, dimensions={0}, use_global_device_ids=true | all-gather | bytes 655360 | tf_op jit(solution)/shard_map/all_gather | solution.py:185
  66.1 2.4 %shard_map.84 = f32[64,512]{1,0:T(8,128)S(1)} custom-call(f32[64,1024]{1,0:T(8,128)S(1)} %bitcast.19, f32[256,512]{1,0:T(8,128)S(1)} %all_gather.7.right_ref), custom_call_target="tpu_custom_call" | custom-call | tf_op jit(solution)/shard_map/pallas_call | solution.py:146
  68.5 0.1 copy.14
  68.6 16.1 %all_to_all.23 = f32[64,1,512]{2,1,0:T(1,128)S(1)} all-to-all(f32[64,1,512]{2,1,0:T(1,128)S(1)} %copy.14), channel_id=1, replica_groups=mesh['z'=8,'yh'=2,'core'=2,'x'=4,'yl'=2] {'z','x','yl'}, dimensions={0} | all-to-all | bytes 262144 | tf_op jit(solution)/shard_map/all_to_all | solution.py:187
  84.7 0.0 copy-start.3
  84.7 0.8 copy-done.3
  85.6 1.0 %shard_map.85 = f32[256,128]{1,0:T(8,128)} custom-call(f32[64,512]{1,0:T(8,128)S(1)} %bitcast.22, f32[256,128]{1,0:T(8,128)S(1)} %get-tuple-element.13.mid_ref, f32[256,128]{1,0:T(8,128)S(1)} %get-tuple-element.14.gate_ref, f32[128,128]{1,0:T(8,128)S(1)} %copy-done.3), custom_call_target="tpu_custom_call" | custom-call | tf_op jit(solution)/shard_map/pallas_call | solution.py:146
  (3 shorter events, 0.1 us)
Async XLA Ops:
  0.8 1.2 %copy-start = (f32[128,8,256]{2,1,0:T(8,128)S(1)}, f32[128,8,256]{2,1,0:T(8,128)}, u32[]{:S(2)}) copy-start(f32[128,8,256]{2,1,0:T(8,128)} %msa_ref.1) | copy-start | bytes 3145732
  2.0 8.3 %copy-start.5 = (f32[128,512]{1,0:T(8,128)S(1)}, f32[128,512]{1,0:T(8,128)}, u32[]{:S(2)}) copy-start(f32[128,512]{1,0:T(8,128)} %param.13) | copy-start | bytes 786436
  3.5 6.9 %copy-start.4 = (f32[1024,128]{1,0:T(8,128)S(1)}, f32[1024,128]{1,0:T(8,128)}, u32[]{:S(2)}) copy-start(f32[1024,128]{1,0:T(8,128)} %param.12) | copy-start | bytes 1572868
  3.5 12.4 %collective-permute-start = (f32[256,128]{1,0:T(8,128)S(1)}, f32[256,128]{1,0:T(8,128)S(1)}, u32[]{:S(2)}, u32[]{:S(2)}) collective-permute-start(f32[256,128]{1,0:T(8,128)S(1)} %get-tuple-element.11), channel_id=1, source_target_pairs={{0,128},{8,136},{16,144},{24,152},{1,96},{9,104},{17,112},{25,120}... | collective-permute-start | bytes 393224 | tf_op jit(solution)/shard_map/ppermute | solution.py:178
  10.7 14.0 %copy-start.1 = (f32[8,32,128]{2,1,0:T(8,128)S(1)}, f32[8,32,128]{2,1,0:T(8,128)}, u32[]{:S(2)}) copy-start(f32[8,32,128]{2,1,0:T(8,128)} %param.9) | copy-start | bytes 393220
  10.7 14.0 %copy-start.2 = (f32[128,128]{1,0:T(8,128)S(1)}, f32[128,128]{1,0:T(8,128)}, u32[]{:S(2)}) copy-start(f32[128,128]{1,0:T(8,128)} %w_gate_ref.1) | copy-start | bytes 196612
  84.7 0.8 copy-start.3

commit v3 on v2

v3 whole, which is shorter than its diff:
```python
import jax
import jax.numpy as jnp
from jax import lax
from jax.experimental import pallas as pl
from jax.experimental.pallas import tpu as pltpu
from jax.sharding import Mesh, PartitionSpec as P

epsilon = 1e-05

ALL = ("z", "yh", "core", "x", "yl")
ROW = ("z", "yh", "core")
COL = ("x", "yl")
LAYER = ("z", "x", "yl")
QUAD = ("yh", "core")
VMEM_LIMIT = 32 * 1024 * 1024


def panel_permutation(cross):
    pairs = []
    for z in range(8):
        for yh in range(2):
            for core in range(2):
                for c in range(8):
                    source = ((c * 2 + (yh ^ cross)) * 2 + core) * 8 + (z + c) % 8
                    pairs.append((source, ((z * 2 + yh) * 2 + core) * 8 + c))
    return pairs


def mm(a, b):
    return jnp.dot(a, b, preferred_element_type=jnp.float32)


def mm_t(a, b):
    return lax.dot_general(a, b, (((1,), (1,)), ((), ())), preferred_element_type=jnp.float32)


def split(x):
    high = x.astype(jnp.bfloat16)
    return high, (x - high.astype(jnp.float32)).astype(jnp.bfloat16)


def dot_deep(a, b):
    a_high, a_low = split(a)
    b_high, b_low = split(b)
    both = mm(a_high, jnp.concatenate([b_high, b_low], 1))
    return both[:, :128] + both[:, 128:] + mm(a_low, b_high)


def dot_t(a, b):
    a_high, a_low = split(a)
    b_high, b_low = split(b)
    shared = mm_t(jnp.concatenate([a_high, a_low], 1), jnp.concatenate([b_high, b_high], 1))
    return shared + mm_t(a_high, b_low)


def dot_t_wide(a, b):
    a_high, a_low = split(a)
    b_high, b_low = split(b)
    return mm_t(a_high, b_high) + mm_t(a_low, b_high) + mm_t(a_high, b_low)


def layer_norm(values, axis):
    average = jnp.mean(values, axis, keepdims=True)
    centred = values - average
    variance = jnp.mean(centred * centred, axis, keepdims=True)
    return centred * lax.rsqrt(variance + epsilon)


def sigmoid(x):
    return 1.0 / (1.0 + jnp.exp(-x))


def factor_kernel(msa_ref, first_ref, second_ref, left_ref, right_ref, held, sems, result):
    copies = [
        pltpu.make_async_copy(
            msa_ref.at[pl.ds(k * 32, 32)], held.at[pl.ds(k * 32, 32)], sems.at[k]
        )
        for k in range(4)
    ]
    for copy in copies:
        copy.start()
    w_high, w_low = split(jnp.concatenate([first_ref[...], second_ref[...]], 1))
    w_both = jnp.concatenate([w_high, w_low], 1)
    w_rest = jnp.concatenate([w_high, jnp.zeros_like(w_high)], 1)
    for k in range(4):
        copies[k].wait()
        n_high, n_low = split(layer_norm(held[pl.ds(k * 32, 32)].reshape(256, 256), -1))
        result[pl.ds(k * 256, 256), :] = mm(n_high, w_both) + mm(n_low, w_rest)
    for i in range(8):
        turned = result[pl.ds(i, 128, stride=8), :].T
        both = turned[:64] + turned[64:]
        left_ref[pl.ds(i * 32, 32), :] = both[:32] * (1.0 / 128.0)
        right_ref[pl.ds(i, 32, stride=8), :] = both[32:]


def pair_half(left, panel, pair, w_outer, w_tri, w_gate, outer_ref, flat_ref):
    outer_ref[...] = dot_t(panel, left)
    lane = lax.broadcasted_iota(jnp.int32, (8, 128), 1)
    low_half = lane < 64
    even = (lane // 32) % 2 == 0
    for o in range(2):
        for bh in range(8):
            for ih in range(2):
                v = [
                    outer_ref[pl.ds((o * 32 + bh * 4 + b) * 8, 8), pl.ds(ih * 128, 128)]
                    for b in range(4)
                ]
                for p in range(2):
                    a, c = v[p], v[p + 2]
                    v[p] = jnp.where(low_half, a, pltpu.roll(c, 64, 1))
                    v[p + 2] = jnp.where(low_half, pltpu.roll(a, 64, 1), c)
                for p in (0, 2):
                    a, c = v[p], v[p + 1]
                    v[p] = jnp.where(even, a, pltpu.roll(c, 32, 1))
                    v[p + 1] = jnp.where(even, pltpu.roll(a, 96, 1), c)
                for il in range(4):
                    i = ih * 4 + il
                    flat_ref[pl.ds(((8 - i) % 8 * 2 + o) * 8, 8), pl.ds(bh * 128, 128)] = v[il]
    mid = pair + dot_deep(flat_ref[...], w_outer)
    normed = layer_norm(mid, -1)
    projected = dot_t(w_tri, normed)
    edges = []
    for side in range(2):
        plain, gating = projected[side * 256 :][:128], projected[side * 256 + 128 :][:128]
        edge = sigmoid(gating) * plain
        edges += [edge[:64], edge[64:]]
    return mid, sigmoid(dot_deep(normed, w_gate)), edges


def half_pairs(pair_ref, half):
    return jnp.concatenate([pair_ref[(8 - p) % 8, half] for p in range(8)], 0)


def near_kernel(
    left_ref, panel_ref, pair_ref, w_outer_ref, w_tri_ref, w_gate_ref,
    edges_ref, mid_ref, gate_ref, outer_ref, flat_ref,
):
    yh = lax.axis_index("yh")
    pair = half_pairs(pair_ref, yh)
    mid, gate, edges = pair_half(
        left_ref[...], panel_ref[...], pair, w_outer_ref[...], w_tri_ref[...], w_gate_ref[...],
        outer_ref, flat_ref,
    )
    mid_ref[...] = mid
    gate_ref[...] = gate
    for q in range(4):
        edges_ref[pl.ds(q * 64, 64), :] = edges[q]


def far_kernel(
    left_ref, panel_ref, pair_ref, w_outer_ref, w_tri_ref, w_gate_ref,
    near_edges_ref, near_mid_ref, near_gate_ref,
    edges_ref, mid_ref, gate_ref, outer_ref, flat_ref,
):
    yh = lax.axis_index("yh")
    pair = half_pairs(pair_ref, 1 - yh)
    mid, gate, edges = pair_half(
        left_ref[...], panel_ref[...], pair, w_outer_ref[...], w_tri_ref[...], w_gate_ref[...],
        outer_ref, flat_ref,
    )
    mid_ref[yh] = near_mid_ref[...]
    mid_ref[1 - yh] = mid
    gate_ref[yh] = near_gate_ref[...]
    gate_ref[1 - yh] = gate
    for q in range(4):
        near = near_edges_ref[pl.ds(q * 64, 64), :]
        edges_ref[pl.ds(q * 2, 64, stride=8), :] = jnp.where(yh == 0, near, edges[q])
        edges_ref[pl.ds(q * 2 + 1, 64, stride=8), :] = jnp.where(yh == 0, edges[q], near)


def turn_blocks(x, masks):
    x = pltpu.roll(x, 0, 1, stride=16, stride_axis=0)
    for bit, mask in zip((1, 2, 4), masks):
        x = jnp.where(mask, pltpu.roll(x, 8 - bit, 0), x)
    return pltpu.roll(x, 0, 1, stride=16, stride_axis=0)


def triangle_kernel(left_ref, right_ref, out_ref, l_ref, r_ref):
    lane = lax.broadcasted_iota(jnp.int32, (8, 128), 1)
    masks = [(lane // 16) & bit != 0 for bit in (1, 2, 4)]
    for h in range(2):
        for z in range(8):
            for half in range(2):
                lanes = pl.ds(half * 128, 128)
                x = left_ref[pl.ds(z * 64 + h * 2 + half, 8, stride=8), :]
                l_ref[pl.ds(z * 8, 8), lanes] = turn_blocks(x, masks)
                for o in range(4):
                    y = right_ref[pl.ds(o * 256 + z * 32 + h * 2 + half, 8, stride=4), :]
                    row = (o // 2) * 128 + (8 - z) % 8 * 16 + (o % 2) * 8
                    r_ref[pl.ds(row, 8), lanes] = turn_blocks(y, masks)
        mixed = dot_t_wide(l_ref[...], r_ref[...])
        for z in range(8):
            for half in range(2):
                block = mixed[z * 8 : z * 8 + 8, half * 128 : half * 128 + 128]
                out_ref[pl.ds(z * 32 + h * 2 + half, 8, stride=4), :] = turn_blocks(block, masks)


def output_kernel(mixed_ref, mid_ref, gate_ref, w_ref, out_ref):
    w = w_ref[...]
    for half in range(2):
        mixed = jnp.concatenate(
            [mixed_ref[pl.ds(h * 2 + half, 64, stride=4), :] for h in range(2)], 0
        )
        update = dot_deep(layer_norm(mixed, 0).T, w)
        for i in range(8):
            rows = pl.ds((8 - i) % 8 * 16, 16)
            out_ref[i, half] = (
                mid_ref[half, rows, :] + gate_ref[half, rows, :] * update[i * 16 : i * 16 + 16]
            )


def call(kernel, out_shapes, scratch, *args, specs=None, flops=0):
    shapes = [jax.ShapeDtypeStruct(s, jnp.float32) for s in out_shapes]
    extra = {} if specs is None else {"in_specs": specs}
    return pl.pallas_call(
        kernel,
        out_shape=shapes if len(shapes) > 1 else shapes[0],
        scratch_shapes=scratch,
        compiler_params=pltpu.CompilerParams(vmem_limit_bytes=VMEM_LIMIT),
        cost_estimate=pl.CostEstimate(flops=flops, bytes_accessed=2**20, transcendentals=0),
        **extra,
    )(*args)


def vmem(*shape):
    return pltpu.VMEM(shape, jnp.float32)


def factors(homolog, first, second):
    inside = pl.BlockSpec(memory_space=pltpu.VMEM)
    return call(
        factor_kernel,
        [(256, 128), (256, 128)],
        [vmem(128, 8, 256), pltpu.SemaphoreType.DMA((4,)), vmem(1024, 128)],
        homolog, first, second,
        specs=[pl.BlockSpec(memory_space=pl.ANY), inside, inside],
    )


def pair_stage_near(left, panel, pair, w_outer, w_tri, w_gate):
    return call(
        near_kernel,
        [(256, 128), (128, 128), (128, 128)],
        [vmem(512, 256), vmem(128, 1024)],
        left, panel, pair, w_outer, w_tri, w_gate,
        flops=10**9,
    )


def pair_stage_far(left, panel, pair, w_outer, w_tri, w_gate, edges, mid, gate):
    return call(
        far_kernel,
        [(512, 128), (2, 128, 128), (2, 128, 128)],
        [vmem(512, 256), vmem(128, 1024)],
        left, panel, pair, w_outer, w_tri, w_gate, edges, mid, gate,
        flops=10**9,
    )


def triangle(left, right):
    return call(triangle_kernel, [(256, 128)], [vmem(64, 256), vmem(256, 256)], left, right)


def output_stage(mixed, mid, gate, w_out):
    return call(output_kernel, [(8, 2, 16, 128)], [], mixed, mid, gate, w_out)


def per_device(homolog, pair, w_first, w_second, w_outer, w_tri, w_gate, w_out):
    left, right = factors(homolog, w_first, w_second)
    near = lax.ppermute(right, ALL, panel_permutation(0))
    far = lax.ppermute(right, ALL, panel_permutation(1))
    w_outer_ba = w_outer.reshape(32, 32, 128).transpose(1, 0, 2).reshape(1024, 128)
    pair = pair.reshape(8, 2, 16, 128)
    shared = (pair, w_outer_ba, w_tri.T, w_gate)
    near = lax.all_gather(near, "core", axis=0, tiled=True)
    done = pair_stage_near(left, near, *shared)
    far = lax.all_gather(far, "core", axis=0, tiled=True)
    edges, mid, gate = pair_stage_far(left, far, *shared, *done)
    swapped = lax.all_to_all(edges.reshape(64, 8, 128), LAYER, 0, 0, tiled=True)
    rights = lax.all_gather(swapped[:, 4:], QUAD, axis=0, tiled=True)
    back = triangle(swapped.reshape(512, 128), rights.reshape(1024, 128))
    mixed = lax.all_to_all(back.reshape(64, 4, 128), LAYER, 0, 0, tiled=True)
    return output_stage(mixed.reshape(256, 128), mid, gate, w_out).reshape(8, 32, 128)


def solution(mesh):
    fine = Mesh(mesh.devices.reshape(8, 2, 2, 4, 2), ALL)
    placed = (P(None, ROW, None), P(ROW, COL, None), P(), P(), P(), P(), P(), P())
    return jax.shard_map(
        per_device, mesh=fine, in_specs=placed, out_specs=P(ROW, COL, None), check_vma=False
    )
```

time: 87.4 us -> 80.1 us (0.916)
  starting transfers between devices: 6.79 us -> 14.3 us
  blocking collectives: 61.5 us -> 55.4 us
  waiting for transfers between devices: 5.09 us -> 0.01 us
  Pallas kernels: 9.32 us -> 6.74 us
    ppermute x1 -> x2, starting transfers between devices: 6.79 us -> 14.3 us  [the longest x1 9.03 us: per_device(): far = lax.ppermute(right, ALL, panel_permutation(1))]
    all_gather x2 -> x3, blocking collectives: 17.4 us -> 12.2 us  [the longest x1 8.04 us: per_device(): rights = lax.all_gather(swapped[:, 4:], QUAD, axis=0, tiled=True)]
    ppermute x1 -> x2, waiting for transfers between devices: 5.09 us -> 0.01 us  [the longest x1 0.01 us: per_device(): near = lax.ppermute(right, ALL, panel_permutation(0))]
    pallas_call x4 -> x5, Pallas kernels: 9.32 us -> 6.74 us  [call(): pl.pallas_call(kernel, out_shape=shapes if len(shapes) > 1 else shapes[0]...]
    all_to_all x2, blocking collectives: 44.2 us -> 43.2 us  [the longest x1 27 us: per_device(): swapped = lax.all_to_all(edges.reshape(64, 8, 128), LAYER, 0, 0, tiled=True)]
    unnamed x15 -> x17, local copies, waits for them, and re-layouts: 2.25 us -> 2.33 us
  transfers between devices with their start and end apart: 1 -> 2, of which waited for: 1 -> 0; matrix products, arithmetic and copies ran while one was open for 0% -> 1% of each run, Pallas kernels for 0% -> 2%
where the time goes in v3:
time: 80.1 us; the launch traced here: 79.3 us
  blocking collectives  55.4 us (69%)
  starting transfers between devices  14.3 us (18%)
  Pallas kernels  6.74 us (8%)
  local copies, waits for them, and re-layouts  2.67 us (3%)
    all_to_all x1, blocking collectives, per_device(): swapped = lax.all_to_all(edges.reshape(64, 8, 128), LAYER, 0, 0, tiled=True)  27 us
    all_to_all x1, blocking collectives, per_device(): mixed = lax.all_to_all(back.reshape(64, 4, 128), LAYER, 0, 0, tiled=True)  16.2 us
    ppermute x1, starting transfers between devices, per_device(): far = lax.ppermute(right, ALL, panel_permutation(1))  9.03 us
    all_gather x1, blocking collectives, per_device(): rights = lax.all_gather(swapped[:, 4:], QUAD, axis=0, tiled=True)  8.04 us
    pallas_call x5, Pallas kernels, call(): pl.pallas_call(kernel, out_shape=shapes if len(shapes) > 1 else shapes[0]...  6.74 us
    ppermute x1, starting transfers between devices, per_device(): near = lax.ppermute(right, ALL, panel_permutation(0))  5.28 us
    unnamed x17, local copies, waits for them, and re-layouts  2.33 us
    all_gather x1, blocking collectives, per_device(): near = lax.all_gather(near, 'core', axis=0, tiled=True)  2.13 us
  transfers between devices with their start and end apart: 2, of which 0 were waited for; matrix products, arithmetic and copies ran while one was open for 1% of the time, Pallas kernels for 2%

profile of v3, /device:TPU:2, one launch (start us, length us, event | category | flops | bytes accessed | tf_op | source)
XLA Modules:
  0.0 79.3 jit_solution(10776243070855606351)
XLA Ops:
  0.0 0.0 copy-start.6
  0.0 0.9 %copy.13.first_ref = f32[256,32]{1,0:T(8,128)S(1)} copy(f32[256,32]{0,1:T(8,128)} %param.10) | data formatting | bytes 65536 | tf_op args[2]
  0.9 0.0 copy-done.6
  0.9 0.1 copy.14.second_ref
  1.0 0.0 copy-start
  1.0 1.2 %copy-done = f32[128,8,256]{2,1,0:T(8,128)S(1)} copy-done((f32[128,8,256]{2,1,0:T(8,128)S(1)}, f32[128,8,256]{2,1,0:T(8,128)}, u32[]{:S(2)}) %copy-start) | copy-done | bytes 1048600
  2.2 0.0 copy-start.5
  2.2 2.1 %shard_map.82 = (f32[256,128]{1,0:T(8,128)S(1)}, f32[256,128]{1,0:T(8,128)S(1)}) custom-call(f32[128,8,256]{2,1,0:T(8,128)S(1)} %copy-done, f32[256,32]{1,0:T(8,128)S(1)} %copy.13.first_ref, f32[256,32]{1,0:T(8,128)S(1)} %copy.14.second_ref), custom_call_target="tpu_custom_call" | custom-call | bytes 1048576 | tf_op jit(solution)/shard_map/pallas_call | solution.py:215
  4.3 0.0 copy-start.4
  4.3 5.3 %collective-permute-start.1 = (f32[256,128]{1,0:T(8,128)S(1)}, f32[256,128]{1,0:T(8,128)S(1)}, u32[]{:S(2)}, u32[]{:S(2)}) collective-permute-start(f32[256,128]{1,0:T(8,128)S(1)} %get-tuple-element.14), channel_id=1, source_target_pairs={{0,0},{33,1},{66,2},{99,3},{132,4},{165,5},{198,6},{231,7},{8,8},{... | collective-permute-start | bytes 393224 | tf_op jit(solution)/shard_map/ppermute | solution.py:270
  9.6 9.0 %collective-permute-start = (f32[256,128]{1,0:T(8,128)S(1)}, f32[256,128]{1,0:T(8,128)S(1)}, u32[]{:S(2)}, u32[]{:S(2)}) collective-permute-start(f32[256,128]{1,0:T(8,128)S(1)} %get-tuple-element.14), channel_id=1, source_target_pairs={{16,0},{49,1},{82,2},{115,3},{148,4},{181,5},{214,6},{247,7},{24,8... | collective-permute-start | bytes 393224 | tf_op jit(solution)/shard_map/ppermute | solution.py:271
  18.6 0.0 copy-done.5
  18.6 0.1 copy.16
  18.7 0.0 copy-done.4
  18.7 0.3 copy.15
  19.1 0.0 copy-start.2
  19.1 0.0 copy-start.3
  19.1 0.0 collective-permute-done.1
  19.1 2.1 %all_gather.10.panel_ref = f32[512,128]{1,0:T(8,128)S(1)} all-gather(f32[256,128]{1,0:T(8,128)S(1)} %collective-permute-done.1), channel_id=1, replica_groups=mesh['z'=8,'yh'=2,'core'=2,'x'=4,'yl'=2] {'core'}, dimensions={0}, use_global_device_ids=true | all-gather | bytes 393216 | tf_op jit(solution)/shard_map/all_gather | solution.py:275
  21.2 0.0 copy-done.2
  21.2 0.0 copy-done.3
  21.2 1.4 %shard_map.83 = (f32[256,128]{1,0:T(8,128)S(1)}, f32[128,128]{1,0:T(8,128)S(1)}, f32[128,128]{1,0:T(8,128)S(1)}) custom-call(f32[256,128]{1,0:T(8,128)S(1)} %get-tuple-element.13.left_ref, f32[512,128]{1,0:T(8,128)S(1)} %all_gather.10.panel_ref, f32[8,2,16,128]{3,2,1,0:T(8,128)S(1)} %bitcast.21, f32[1024,128]{1,0:T(8,128)S(1)} %bitcast.15, ...), custom_call_target="tpu_custom_call" | custom-call | flops 1000000000 | bytes 1048576 | tf_op jit(solution)/shard_map/pallas_call | solution.py:215
  22.7 0.0 collective-permute-done
  22.7 2.0 %all_gather.9.panel_ref = f32[512,128]{1,0:T(8,128)S(1)} all-gather(f32[256,128]{1,0:T(8,128)S(1)} %collective-permute-done), channel_id=1, replica_groups=mesh['z'=8,'yh'=2,'core'=2,'x'=4,'yl'=2] {'core'}, dimensions={0}, use_global_device_ids=true | all-gather | bytes 393216 | tf_op jit(solution)/shard_map/all_gather | solution.py:277
  24.7 1.4 %shard_map.84 = (f32[512,128]{1,0:T(8,128)S(1)}, f32[2,128,128]{2,1,0:T(8,128)S(1)}, f32[2,128,128]{2,1,0:T(8,128)S(1)}) custom-call(f32[256,128]{1,0:T(8,128)S(1)} %get-tuple-element.13.left_ref, f32[512,128]{1,0:T(8,128)S(1)} %all_gather.9.panel_ref, f32[8,2,16,128]{3,2,1,0:T(8,128)S(1)} %bitcast.22, f32[1024,128]{1,0:T(8,128)S(1)} %bitcast.16, ...), custom_call_target="tpu_custom_call" | custom-call | flops 1000000000 | bytes 1048576 | tf_op jit(solution)/shard_map/pallas_call | solution.py:215
  26.1 27.0 %all_to_all.10 = f32[64,8,128]{2,1,0:T(8,128)S(1)} all-to-all(f32[64,8,128]{2,1,0:T(8,128)S(1)} %bitcast.20), channel_id=1, replica_groups=mesh['z'=8,'yh'=2,'core'=2,'x'=4,'yl'=2] {'z','x','yl'}, dimensions={0} | all-to-all | bytes 524288 | tf_op jit(solution)/shard_map/all_to_all | solution.py:279
  53.2 8.0 %all_gather.11 = f32[256,4,128]{2,1,0:T(4,128)S(1)} all-gather(f32[64,4,128]{2,1,0:T(4,128)S(1)} %slice.4), channel_id=1, replica_groups=mesh['z'=8,'yh'=2,'core'=2,'x'=4,'yl'=2] {'yh','core'}, dimensions={0}, use_global_device_ids=true | all-gather | bytes 655360 | tf_op jit(solution)/shard_map/all_gather | solution.py:280
  61.2 0.8 %shard_map.85 = f32[256,128]{1,0:T(8,128)S(1)} custom-call(f32[512,128]{1,0:T(8,128)S(1)} %bitcast.13, f32[1024,128]{1,0:T(8,128)S(1)} %bitcast.12), custom_call_target="tpu_custom_call" | custom-call | bytes 1048576 | tf_op jit(solution)/shard_map/pallas_call | solution.py:215
  62.0 0.0 copy-start.1
  62.1 16.2 %all_to_all.11 = f32[64,4,128]{2,1,0:T(4,128)S(1)} all-to-all(f32[64,4,128]{2,1,0:T(4,128)S(1)} %bitcast.14), channel_id=1, replica_groups=mesh['z'=8,'yh'=2,'core'=2,'x'=4,'yl'=2] {'z','x','yl'}, dimensions={0} | all-to-all | bytes 262144 | tf_op jit(solution)/shard_map/all_to_all | solution.py:282
  78.3 0.0 copy-done.1
  78.3 1.0 %shard_map.86 = f32[8,2,16,128]{3,2,1,0:T(8,128)} custom-call(f32[256,128]{1,0:T(8,128)S(1)} %bitcast.17, f32[2,128,128]{2,1,0:T(8,128)S(1)} %get-tuple-element.19.mid_ref, f32[2,128,128]{2,1,0:T(8,128)S(1)} %get-tuple-element.20.gate_ref, f32[128,128]{1,0:T(8,128)S(1)} %copy-done.1), custom_call_target="tpu_custom_call" | custom-call | bytes 1048576 | tf_op jit(solution)/shard_map/pallas_call | solution.py:215
  (1 shorter events, 0.0 us)
Async XLA Ops:
  0.0 0.9 %copy-start.6 = (f32[256,32]{0,1:T(8,128)S(1)}, f32[256,32]{0,1:T(8,128)}, u32[]{:S(2)}) copy-start(f32[256,32]{0,1:T(8,128)} %param.11) | copy-start | bytes 98308
  1.0 1.2 %copy-start = (f32[128,8,256]{2,1,0:T(8,128)S(1)}, f32[128,8,256]{2,1,0:T(8,128)}, u32[]{:S(2)}) copy-start(f32[128,8,256]{2,1,0:T(8,128)} %msa_ref.1) | copy-start | bytes 3145732
  2.2 16.4 %copy-start.5 = (f32[128,512]{1,0:T(8,128)S(1)}, f32[128,512]{1,0:T(8,128)}, u32[]{:S(2)}) copy-start(f32[128,512]{1,0:T(8,128)} %param.13) | copy-start | bytes 786436
  4.3 14.5 %copy-start.4 = (f32[1024,128]{1,0:T(8,128)S(1)}, f32[1024,128]{1,0:T(8,128)}, u32[]{:S(2)}) copy-start(f32[1024,128]{1,0:T(8,128)} %param.12) | copy-start | bytes 1572868
  4.3 14.8 %collective-permute-start.1 = (f32[256,128]{1,0:T(8,128)S(1)}, f32[256,128]{1,0:T(8,128)S(1)}, u32[]{:S(2)}, u32[]{:S(2)}) collective-permute-start(f32[256,128]{1,0:T(8,128)S(1)} %get-tuple-element.14), channel_id=1, source_target_pairs={{0,0},{33,1},{66,2},{99,3},{132,4},{165,5},{198,6},{231,7},{8,8},{... | collective-permute-start | bytes 393224 | tf_op jit(solution)/shard_map/ppermute | solution.py:270
  9.6 13.1 %collective-permute-start = (f32[256,128]{1,0:T(8,128)S(1)}, f32[256,128]{1,0:T(8,128)S(1)}, u32[]{:S(2)}, u32[]{:S(2)}) collective-permute-start(f32[256,128]{1,0:T(8,128)S(1)} %get-tuple-element.14), channel_id=1, source_target_pairs={{16,0},{49,1},{82,2},{115,3},{148,4},{181,5},{214,6},{247,7},{24,8... | collective-permute-start | bytes 393224 | tf_op jit(solution)/shard_map/ppermute | solution.py:271
  19.1 2.2 %copy-start.2 = (f32[8,32,128]{2,1,0:T(8,128)S(1)}, f32[8,32,128]{2,1,0:T(8,128)}, u32[]{:S(2)}) copy-start(f32[8,32,128]{2,1,0:T(8,128)} %param.9) | copy-start | bytes 393220
  19.1 2.2 %copy-start.3 = (f32[128,128]{1,0:T(8,128)S(1)}, f32[128,128]{1,0:T(8,128)}, u32[]{:S(2)}) copy-start(f32[128,128]{1,0:T(8,128)} %w_gate_ref.3) | copy-start | bytes 196612
  62.0 16.2 %copy-start.1 = (f32[128,128]{1,0:T(8,128)S(1)}, f32[128,128]{1,0:T(8,128)}, u32[]{:S(2)}) copy-start(f32[128,128]{1,0:T(8,128)} %w_ref.1) | copy-start | bytes 196612

commit v4 on v3

v4 whole, which is shorter than its diff:
```python
import jax
import jax.numpy as jnp
from jax import lax
from jax.experimental import pallas as pl
from jax.experimental.pallas import tpu as pltpu
from jax.sharding import Mesh, PartitionSpec as P

epsilon = 1e-05

ALL = ("z", "yh", "core", "x", "yl")
ROW = ("z", "yh", "core")
COL = ("x", "yl")
LAYER = ("z", "x", "yl")
CHIPS = ("z", "yh", "x", "yl")
VMEM_LIMIT = 32 * 1024 * 1024


def panel_permutation():
    pairs = []
    for z in range(8):
        for o in range(4):
            for c in range(8):
                pairs.append(((c * 4 + o) * 8 + (z + c + 4) % 8, (z * 4 + o) * 8 + c))
    return pairs


def mm(a, b):
    return jnp.dot(a, b, preferred_element_type=jnp.float32)


def mm_t(a, b):
    return lax.dot_general(a, b, (((1,), (1,)), ((), ())), preferred_element_type=jnp.float32)


def split(x):
    high = x.astype(jnp.bfloat16)
    return high, (x - high.astype(jnp.float32)).astype(jnp.bfloat16)


def dot_deep(a, b):
    a_high, a_low = split(a)
    b_high, b_low = split(b)
    both = mm(a_high, jnp.concatenate([b_high, b_low], 1))
    return both[:, :128] + both[:, 128:] + mm(a_low, b_high)


def dot_t(a, b):
    a_high, a_low = split(a)
    b_high, b_low = split(b)
    shared = mm_t(jnp.concatenate([a_high, a_low], 1), jnp.concatenate([b_high, b_high], 1))
    return shared + mm_t(a_high, b_low)


def layer_norm(values, axis):
    average = jnp.mean(values, axis, keepdims=True)
    centred = values - average
    variance = jnp.mean(centred * centred, axis, keepdims=True)
    return centred * lax.rsqrt(variance + epsilon)


def sigmoid(x):
    return 1.0 / (1.0 + jnp.exp(-x))


def turned_rows(p):
    return (8 - p) % 8


def factor_kernel(msa_ref, first_ref, second_ref, pair_ref, shared_ref, right_ref, held, sems, result):
    copies = [
        pltpu.make_async_copy(
            msa_ref.at[pl.ds(k * 32, 32)], held.at[pl.ds(k * 32, 32)], sems.at[k]
        )
        for k in range(4)
    ]
    for copy in copies:
        copy.start()
    w_high, w_low = split(jnp.concatenate([first_ref[...], second_ref[...]], 0))
    w_both = jnp.concatenate([w_high, w_low], 0)
    w_rest = jnp.concatenate([w_high, jnp.zeros_like(w_high)], 0)
    other = 1 - lax.axis_index("yh")
    for p in range(8):
        shared_ref[pl.ds(256 + p * 16, 16), :] = pair_ref[turned_rows(p), other]
    for k in range(4):
        copies[k].wait()
        n_high, n_low = split(layer_norm(held[pl.ds(k * 32, 32)].reshape(256, 256), -1))
        result[pl.ds(k * 256, 256), :] = mm_t(n_high, w_both) + mm_t(n_low, w_rest)
    for i in range(8):
        turned = result[pl.ds(i, 128, stride=8), :].T
        both = turned[:64] + turned[64:]
        shared_ref[pl.ds(i * 32, 32), :] = both[:32] * (1.0 / 128.0)
        right_ref[pl.ds(i, 32, stride=8), :] = both[32:]


def pair_kernel(
    own_ref, met_ref, panel_ref, pair_ref, w_outer_ref, w_tri_ref, w_gate_ref,
    edges_ref, kept_ref, sent_ref, outer_ref, flat_ref,
):
    yh = lax.axis_index("yh")
    left = jnp.concatenate([own_ref[pl.ds(0, 256), :], met_ref[pl.ds(0, 256), :]], 0)
    outer_ref[...] = dot_t(panel_ref[...], left)
    lane = lax.broadcasted_iota(jnp.int32, (8, 128), 1)
    low_half = lane < 64
    even = (lane // 32) % 2 == 0
    for o in range(2):
        for bh in range(8):
            for ih in range(4):
                v = [
                    outer_ref[pl.ds((o * 32 + bh * 4 + b) * 8, 8), pl.ds(ih * 128, 128)]
                    for b in range(4)
                ]
                for p in range(2):
                    a, c = v[p], v[p + 2]
                    v[p] = jnp.where(low_half, a, pltpu.roll(c, 64, 1))
                    v[p + 2] = jnp.where(low_half, pltpu.roll(a, 64, 1), c)
                for p in (0, 2):
                    a, c = v[p], v[p + 1]
                    v[p] = jnp.where(even, a, pltpu.roll(c, 32, 1))
                    v[p + 1] = jnp.where(even, pltpu.roll(a, 96, 1), c)
                for il in range(4):
                    i = ih % 2 * 4 + il
                    row = ih // 2 * 128 + turned_rows(i) * 16 + o * 8
                    flat_ref[pl.ds(row, 8), pl.ds(bh * 128, 128)] = v[il]
    pair = jnp.concatenate(
        [pair_ref[turned_rows(p), yh] for p in range(8)] + [met_ref[pl.ds(256, 128), :]], 0
    )
    mid = pair + dot_deep(flat_ref[...], w_outer_ref[...])
    normed = layer_norm(mid, -1)
    projected = dot_t(w_tri_ref[...], normed)
    for side in range(2):
        plain, gating = projected[side * 256 :][:128], projected[side * 256 + 128 :][:128]
        edge = sigmoid(gating) * plain
        for h in range(2):
            q = side * 2 + h
            own, met = edge[h * 64 : h * 64 + 64, :128], edge[h * 64 : h * 64 + 64, 128:]
            edges_ref[pl.ds(q * 2, 64, stride=8), :] = jnp.where(yh == 0, own, met)
            edges_ref[pl.ds(q * 2 + 1, 64, stride=8), :] = jnp.where(yh == 0, met, own)
    gate = sigmoid(dot_deep(normed, w_gate_ref[...]))
    kept_ref[0], kept_ref[1] = mid[:128], gate[:128]
    sent_ref[0], sent_ref[1] = mid[128:], gate[128:]


def turn_blocks(x, masks):
    x = pltpu.roll(x, 0, 1, stride=16, stride_axis=0)
    for bit, mask in zip((1, 2, 4), masks):
        x = jnp.where(mask, pltpu.roll(x, 8 - bit, 0), x)
    return pltpu.roll(x, 0, 1, stride=16, stride_axis=0)


def triangle_kernel(left_ref, right_ref, out_ref, l_ref, r_ref):
    lane = lax.broadcasted_iota(jnp.int32, (8, 128), 1)
    masks = [(lane // 16) & bit != 0 for bit in (1, 2, 4)]
    for h in range(2):
        for z in range(8):
            for y in range(2):
                x = left_ref[pl.ds(z * 64 + h * 2 + y, 8, stride=8), :]
                l_ref[pl.ds(y * 64 + z * 8, 8), :] = turn_blocks(x, masks)
                for o in range(2):
                    x = right_ref[pl.ds(o * 256 + z * 32 + h * 2 + y, 8, stride=4), :]
                    row = y * 128 + turned_rows(z) * 16 + o * 8
                    r_ref[pl.ds(row, 8), :] = turn_blocks(x, masks)
        mixed = dot_t(l_ref[...], r_ref[...])
        for z in range(8):
            for y in range(2):
                for half in range(2):
                    block = mixed[y * 64 + z * 8 :, half * 128 :][:8, :128]
                    out_ref[pl.ds((z * 2 + y) * 32 + h * 2 + half, 8, stride=4), :] = turn_blocks(
                        block, masks
                    )


def output_kernel(mixed_ref, kept_ref, met_ref, w_ref, out_ref):
    yh = lax.axis_index("yh")
    w = w_ref[...]
    for half in range(2):
        tiles = []
        for h in range(2):
            for z in range(8):
                parts = [
                    mixed_ref[pl.ds((z * 2 + y) * 32 + h * 2 + half, 8, stride=4), :]
                    for y in range(2)
                ]
                tiles.append(parts[0] + parts[1])
        update = dot_deep(layer_norm(jnp.concatenate(tiles, 0), 0).T, w)
        mid = jnp.where(yh == half, kept_ref[0], met_ref[0])
        gate = jnp.where(yh == half, kept_ref[1], met_ref[1])
        for i in range(8):
            p = turned_rows(i) * 16
            out_ref[i, half] = mid[p : p + 16] + gate[p : p + 16] * update[i * 16 : i * 16 + 16]


def call(kernel, out_shapes, scratch, *args, specs=None, limit=VMEM_LIMIT):
    shapes = [jax.ShapeDtypeStruct(s, jnp.float32) for s in out_shapes]
    extra = {} if specs is None else {"in_specs": specs}
    return pl.pallas_call(
        kernel,
        out_shape=shapes if len(shapes) > 1 else shapes[0],
        scratch_shapes=scratch,
        compiler_params=pltpu.CompilerParams(vmem_limit_bytes=limit),
        **extra,
    )(*args)


def vmem(*shape):
    return pltpu.VMEM(shape, jnp.float32)


def factors(homolog, first, second, pair):
    inside = pl.BlockSpec(memory_space=pltpu.VMEM)
    return call(
        factor_kernel,
        [(384, 128), (256, 128)],
        [vmem(128, 8, 256), pltpu.SemaphoreType.DMA((4,)), vmem(1024, 128)],
        homolog, first, second, pair,
        specs=[pl.BlockSpec(memory_space=pltpu.HBM), inside, inside, inside],
        limit=60 * 1024 * 1024,
    )


def pair_stage(own, met, panel, pair, w_outer, w_tri, w_gate):
    return call(
        pair_kernel,
        [(512, 128), (2, 128, 128), (2, 128, 128)],
        [vmem(512, 512), vmem(256, 1024)],
        own, met, panel, pair, w_outer, w_tri, w_gate,
    )


def triangle(left, right):
    return call(triangle_kernel, [(512, 128)], [vmem(128, 128), vmem(256, 128)], left, right)


def output_stage(mixed, kept, met, w_out):
    return call(output_kernel, [(8, 2, 16, 128)], [], mixed, kept, met, w_out)


def per_device(homolog, pair, w_first, w_second, w_outer, w_tri, w_gate, w_out):
    pair = pair.reshape(8, 2, 16, 128)
    shared, right = factors(homolog, w_first.T, w_second.T, pair)
    swap = [(0, 1), (1, 0)]
    panel = lax.ppermute(right, ALL, panel_permutation())
    met = lax.ppermute(shared, "yh", swap)
    w_outer_ba = w_outer.reshape(32, 32, 128).transpose(1, 0, 2).reshape(1024, 128)
    panel = lax.all_gather(panel, "core", axis=0, tiled=True)
    edges, kept, sent = pair_stage(shared, met, panel, pair, w_outer_ba, w_tri.T, w_gate)
    returned = lax.ppermute(sent, "yh", swap)
    swapped = lax.all_to_all(edges.reshape(64, 8, 128), LAYER, 0, 0, tiled=True)
    rights = lax.all_gather(swapped[:, 4:], "core", axis=0, tiled=True)
    back = triangle(swapped.reshape(512, 128), rights.reshape(512, 128))
    mixed = lax.all_to_all(back.reshape(128, 4, 128), CHIPS, 0, 0, tiled=True)
    return output_stage(mixed.reshape(512, 128), kept, returned, w_out).reshape(8, 32, 128)


def solution(mesh):
    fine = Mesh(mesh.devices.reshape(8, 2, 2, 4, 2), ALL)
    placed = (P(None, ROW, None), P(ROW, COL, None), P(), P(), P(), P(), P(), P())
    return jax.shard_map(
        per_device, mesh=fine, in_specs=placed, out_specs=P(ROW, COL, None), check_vma=False
    )
```

time: 80.1 us -> 74.1 us (0.925)
  blocking collectives: 55.4 us -> 27.6 us
  waiting for transfers between devices: 0.01 us -> 13.8 us
  starting transfers between devices: 14.3 us -> 23 us
  local copies, waits for them, and re-layouts: 2.67 us -> 0.49 us
  Pallas kernels: 6.74 us -> 8.78 us
    all_to_all x1 -> x0, blocking collectives: 16.2 us -> none  [per_device(): mixed = lax.all_to_all(back.reshape(64, 4, 128), LAYER, 0, 0, tiled=True)]
    all_to_all x0 -> x1, starting transfers between devices: none -> 8.33 us  [per_device(): mixed = lax.all_to_all(back.reshape(128, 4, 128), CHIPS, 0, 0, tiled=True)]
    all_gather x3 -> x2, blocking collectives: 12.2 us -> 3.98 us  [the longest x1 1.99 us: per_device(): rights = lax.all_gather(swapped[:, 4:], 'core', axis=0, tiled=True)]
    ppermute x2 -> x3, waiting for transfers between devices: 0.01 us -> 7.09 us  [the longest x1 4.69 us: per_device(): returned = lax.ppermute(sent, 'yh', swap)]
    all_to_all x0 -> x1, waiting for transfers between devices: none -> 6.7 us  [per_device(): mixed = lax.all_to_all(back.reshape(128, 4, 128), CHIPS, 0, 0, tiled=True)]
    all_to_all x1, blocking collectives: 27 us -> 23.7 us  [per_device(): swapped = lax.all_to_all(edges.reshape(64, 8, 128), LAYER, 0, 0, tiled=True)]
    unnamed x17 -> x13, local copies, waits for them, and re-layouts: 2.33 us -> 0.15 us
    pallas_call x5 -> x4, Pallas kernels: 6.74 us -> 8.78 us  [call(): pl.pallas_call(kernel, out_shape=shapes if len(shapes) > 1 else shapes[0]...]
  transfers between devices with their start and end apart: 2 -> 4, of which waited for: 0 -> 4; matrix products, arithmetic and copies ran while one was open for 1% -> 1% of each run, Pallas kernels for 2% -> 0%
where the time goes in v4:
time: 74.1 us; the launch traced here: 73.8 us
  blocking collectives  27.6 us (37%)
  starting transfers between devices  23 us (31%)
  waiting for transfers between devices  13.8 us (19%)
  Pallas kernels  8.78 us (12%)
    all_to_all x1, blocking collectives, per_device(): swapped = lax.all_to_all(edges.reshape(64, 8, 128), LAYER, 0, 0, tiled=True)  23.7 us
    pallas_call x4, Pallas kernels, call(): pl.pallas_call(kernel, out_shape=shapes if len(shapes) > 1 else shapes[0]...  8.78 us
    all_to_all x1, starting transfers between devices, per_device(): mixed = lax.all_to_all(back.reshape(128, 4, 128), CHIPS, 0, 0, tiled=True)  8.33 us
    ppermute x1, starting transfers between devices, per_device(): panel = lax.ppermute(right, ALL, panel_permutation())  8.31 us
    all_to_all x1, waiting for transfers between devices, per_device(): mixed = lax.all_to_all(back.reshape(128, 4, 128), CHIPS, 0, 0, tiled=True)  6.7 us
    ppermute x1, waiting for transfers between devices, per_device(): returned = lax.ppermute(sent, 'yh', swap)  4.69 us
    ppermute x1, starting transfers between devices, per_device(): met = lax.ppermute(shared, 'yh', swap)  3.28 us
    ppermute x1, starting transfers between devices, per_device(): returned = lax.ppermute(sent, 'yh', swap)  3.06 us
  transfers between devices with their start and end apart: 4, of which 4 were waited for; matrix products, arithmetic and copies ran while one was open for 1% of the time, Pallas kernels for 0%

profile of v4, /device:TPU:2, one launch (start us, length us, event | category | flops | bytes accessed | tf_op | source)
XLA Modules:
  0.0 73.8 jit_solution(9080056026989612900)
XLA Ops:
  0.0 0.0 copy-start.5
  0.0 4.7 %shard_map.82 = (f32[384,128]{1,0:T(8,128)}, f32[256,128]{1,0:T(8,128)}) custom-call(f32[128,8,256]{2,1,0:T(8,128)} %msa_ref.1, f32[32,256]{1,0:T(8,128)} %bitcast.23, f32[32,256]{1,0:T(8,128)} %bitcast.24, f32[8,2,16,128]{3,2,1,0:T(8,128)} %bitcast.19), custom_call_target="tpu_custom_call" | custom-call | tf_op jit(solution)/shard_map/pallas_call | solution.py:195
  4.7 0.0 copy-start.4
  4.7 8.3 %collective-permute-start.1 = (f32[256,128]{1,0:T(8,128)}, f32[256,128]{1,0:T(8,128)S(1)}, u32[]{:S(2)}, u32[]{:S(2)}) collective-permute-start(f32[256,128]{1,0:T(8,128)} %get-tuple-element.11), channel_id=1, source_target_pairs={{4,0},{37,1},{70,2},{103,3},{128,4},{161,5},{194,6},{227,7},{12,8}... | collective-permute-start | bytes 393224 | tf_op jit(solution)/shard_map/ppermute | solution.py:241
  13.0 3.3 %collective-permute-start = (f32[384,128]{1,0:T(8,128)}, f32[384,128]{1,0:T(8,128)S(1)}, u32[]{:S(2)}, u32[]{:S(2)}) collective-permute-start(f32[384,128]{1,0:T(8,128)} %get-tuple-element.10.own_ref), channel_id=1, source_target_pairs={{0,16},{16,0},{1,17},{17,1},{2,18},{18,2},{3,19},{19,3},{4,20},{20... | collective-permute-start | bytes 589832 | tf_op jit(solution)/shard_map/ppermute | solution.py:242
  16.3 0.0 copy-done.5
  16.3 0.1 copy.12
  16.4 0.0 copy-done.4
  16.4 0.3 copy.11
  16.8 0.0 copy-start
  16.8 0.0 copy-start.1
  16.8 0.0 copy-start.2
  16.8 2.1 %collective-permute-done.1 = f32[256,128]{1,0:T(8,128)S(1)} collective-permute-done((f32[256,128]{1,0:T(8,128)}, f32[256,128]{1,0:T(8,128)S(1)}, u32[]{:S(2)}, u32[]{:S(2)}) %collective-permute-start.1) | collective-permute-done | bytes 131104 | tf_op jit(solution)/shard_map/ppermute | solution.py:241
  18.9 2.0 %all_gather.6.panel_ref = f32[512,128]{1,0:T(8,128)S(1)} all-gather(f32[256,128]{1,0:T(8,128)S(1)} %collective-permute-done.1), channel_id=1, replica_groups=mesh['z'=8,'yh'=2,'core'=2,'x'=4,'yl'=2] {'core'}, dimensions={0}, use_global_device_ids=true | all-gather | bytes 393216 | tf_op jit(solution)/shard_map/all_gather | solution.py:244
  20.9 0.3 collective-permute-done.met_ref
  21.2 0.0 copy-done
  21.2 0.0 copy-done.1
  21.2 0.0 copy-done.2
  21.2 1.7 %shard_map.83 = (f32[512,128]{1,0:T(8,128)S(1)}, f32[2,128,128]{2,1,0:T(8,128)S(1)}, f32[2,128,128]{2,1,0:T(8,128)S(1)}) custom-call(f32[384,128]{1,0:T(8,128)S(1)} %copy-done.1, f32[384,128]{1,0:T(8,128)S(1)} %collective-permute-done.met_ref, f32[512,128]{1,0:T(8,128)S(1)} %all_gather.6.panel_ref, f32[8,2,16,128]{3,2,1,0:T(8,128)S(1)} %bitcast.20, ...), custom_call_target="tpu_custom_call" | custom-call | tf_op jit(solution)/shard_map/pallas_call | solution.py:195
  22.9 23.7 %all_to_all.10 = f32[64,8,128]{2,1,0:T(8,128)S(1)} all-to-all(f32[64,8,128]{2,1,0:T(8,128)S(1)} %bitcast.21), channel_id=1, replica_groups=mesh['z'=8,'yh'=2,'core'=2,'x'=4,'yl'=2] {'z','x','yl'}, dimensions={0} | all-to-all | bytes 524288 | tf_op jit(solution)/shard_map/all_to_all | solution.py:247
  46.6 2.0 %all_gather.7 = f32[128,4,128]{2,1,0:T(4,128)S(1)} all-gather(f32[64,4,128]{2,1,0:T(4,128)S(1)} %slice.4), channel_id=1, replica_groups=mesh['z'=8,'yh'=2,'core'=2,'x'=4,'yl'=2] {'core'}, dimensions={0}, use_global_device_ids=true | all-gather | bytes 393216 | tf_op jit(solution)/shard_map/all_gather | solution.py:248
  48.6 1.4 %shard_map.84 = f32[512,128]{1,0:T(8,128)} custom-call(f32[512,128]{1,0:T(8,128)S(1)} %bitcast.15, f32[512,128]{1,0:T(8,128)S(1)} %bitcast.17), custom_call_target="tpu_custom_call" | custom-call | tf_op jit(solution)/shard_map/pallas_call | solution.py:195
  50.0 0.0 copy-start.3
  50.0 8.3 %all-to-all-start.1 = ((f32[128,4,128]{2,1,0:T(4,128)}), f32[128,4,128]{2,1,0:T(4,128)S(1)}, u32[]{:S(2)}, u32[]{:S(2)}) async-start(f32[128,4,128]{2,1,0:T(4,128)} %bitcast.10), calls=%async_computation.1 | async-start | bytes 524288 | tf_op jit(solution)/shard_map/all_to_all | solution.py:250
  58.4 3.1 %collective-permute-start.2 = (f32[2,128,128]{2,1,0:T(8,128)S(1)}, f32[2,128,128]{2,1,0:T(8,128)S(1)}, u32[]{:S(2)}, u32[]{:S(2)}) collective-permute-start(f32[2,128,128]{2,1,0:T(8,128)S(1)} %get-tuple-element.14), channel_id=1, source_target_pairs={{0,16},{16,0},{1,17},{17,1},{2,18},{18,2},{3,19},{19,3},{4,20},{20... | collective-permute-start | bytes 393224 | tf_op jit(solution)/shard_map/ppermute | solution.py:246
  61.4 4.7 %collective-permute-done.2.met_ref = f32[2,128,128]{2,1,0:T(8,128)S(1)} collective-permute-done((f32[2,128,128]{2,1,0:T(8,128)S(1)}, f32[2,128,128]{2,1,0:T(8,128)S(1)}, u32[]{:S(2)}, u32[]{:S(2)}) %collective-permute-start.2) | collective-permute-done | bytes 131104 | tf_op jit(solution)/shard_map/ppermute | solution.py:246
  66.1 6.7 %all-to-all-done.1 = f32[128,4,128]{2,1,0:T(4,128)S(1)} async-done(((f32[128,4,128]{2,1,0:T(4,128)}), f32[128,4,128]{2,1,0:T(4,128)S(1)}, u32[]{:S(2)}, u32[]{:S(2)}) %all-to-all-start.1) | async-done | bytes 262176 | tf_op jit(solution)/shard_map/all_to_all | solution.py:250
  72.8 0.0 copy-done.3
  72.8 1.0 %shard_map.85 = f32[8,2,16,128]{3,2,1,0:T(8,128)} custom-call(f32[512,128]{1,0:T(8,128)S(1)} %bitcast.18, f32[2,128,128]{2,1,0:T(8,128)S(1)} %get-tuple-element.13.kept_ref, f32[2,128,128]{2,1,0:T(8,128)S(1)} %collective-permute-done.2.met_ref, f32[128,128]{1,0:T(8,128)S(1)} %copy-done.3), custom_call_target="tpu_custom_call" | custom-call | tf_op jit(solution)/shard_map/pallas_call | solution.py:195
  (1 shorter events, 0.0 us)
Async XLA Ops:
  0.0 16.3 %copy-start.5 = (f32[128,512]{1,0:T(8,128)S(1)}, f32[128,512]{1,0:T(8,128)}, u32[]{:S(2)}) copy-start(f32[128,512]{1,0:T(8,128)} %param.13) | copy-start | bytes 786436
  4.7 11.7 %copy-start.4 = (f32[1024,128]{1,0:T(8,128)S(1)}, f32[1024,128]{1,0:T(8,128)}, u32[]{:S(2)}) copy-start(f32[1024,128]{1,0:T(8,128)} %param.12) | copy-start | bytes 1572868
  4.7 14.2 %collective-permute-start.1 = (f32[256,128]{1,0:T(8,128)}, f32[256,128]{1,0:T(8,128)S(1)}, u32[]{:S(2)}, u32[]{:S(2)}) collective-permute-start(f32[256,128]{1,0:T(8,128)} %get-tuple-element.11), channel_id=1, source_target_pairs={{4,0},{37,1},{70,2},{103,3},{128,4},{161,5},{194,6},{227,7},{12,8}... | collective-permute-start | bytes 393224 | tf_op jit(solution)/shard_map/ppermute | solution.py:241
  13.0 8.2 %collective-permute-start = (f32[384,128]{1,0:T(8,128)}, f32[384,128]{1,0:T(8,128)S(1)}, u32[]{:S(2)}, u32[]{:S(2)}) collective-permute-start(f32[384,128]{1,0:T(8,128)} %get-tuple-element.10.own_ref), channel_id=1, source_target_pairs={{0,16},{16,0},{1,17},{17,1},{2,18},{18,2},{3,19},{19,3},{4,20},{20... | collective-permute-start | bytes 589832 | tf_op jit(solution)/shard_map/ppermute | solution.py:242
  16.8 4.4 %copy-start = (f32[8,32,128]{2,1,0:T(8,128)S(1)}, f32[8,32,128]{2,1,0:T(8,128)}, u32[]{:S(2)}) copy-start(f32[8,32,128]{2,1,0:T(8,128)} %param.9) | copy-start | bytes 393220
  16.8 4.4 %copy-start.1 = (f32[384,128]{1,0:T(8,128)S(1)}, f32[384,128]{1,0:T(8,128)}, u32[]{:S(2)}) copy-start(f32[384,128]{1,0:T(8,128)} %get-tuple-element.10.own_ref) | copy-start | bytes 589828
  16.8 4.4 %copy-start.2 = (f32[128,128]{1,0:T(8,128)S(1)}, f32[128,128]{1,0:T(8,128)}, u32[]{:S(2)}) copy-start(f32[128,128]{1,0:T(8,128)} %w_gate_ref.1) | copy-start | bytes 196612
  50.0 22.8 %copy-start.3 = (f32[128,128]{1,0:T(8,128)S(1)}, f32[128,128]{1,0:T(8,128)}, u32[]{:S(2)}) copy-start(f32[128,128]{1,0:T(8,128)} %w_ref.1) | copy-start | bytes 196612
  50.0 22.8 %all-to-all-start.1 = ((f32[128,4,128]{2,1,0:T(4,128)}), f32[128,4,128]{2,1,0:T(4,128)S(1)}, u32[]{:S(2)}, u32[]{:S(2)}) async-start(f32[128,4,128]{2,1,0:T(4,128)} %bitcast.10), calls=%async_computation.1 | async-start | bytes 524288 | tf_op jit(solution)/shard_map/all_to_all | solution.py:250
  58.4 7.7 %collective-permute-start.2 = (f32[2,128,128]{2,1,0:T(8,128)S(1)}, f32[2,128,128]{2,1,0:T(8,128)S(1)}, u32[]{:S(2)}, u32[]{:S(2)}) collective-permute-start(f32[2,128,128]{2,1,0:T(8,128)S(1)} %get-tuple-element.14), channel_id=1, source_target_pairs={{0,16},{16,0},{1,17},{17,1},{2,18},{18,2},{3,19},{19,3},{4,20},{20... | collective-permute-start | bytes 393224 | tf_op jit(solution)/shard_map/ppermute | solution.py:246

commit v5 on v4

--- a/solution.py
+++ b/solution.py
@@ -15,12 +15,21 @@
 VMEM_LIMIT = 32 * 1024 * 1024
 
 
+PANEL_COLUMNS = (
+    (34570126, 24563107, 1675324, 1674523, 1236754, 1234675, 12467530, 1376452),
+    (34560127, 45673102, 1675423, 1674253, 1237654, 2643175, 12467530, 1376542),
+)
+
+
 def panel_permutation():
     pairs = []
     for z in range(8):
-        for o in range(4):
-            for c in range(8):
-                pairs.append(((c * 4 + o) * 8 + (z + c + 4) % 8, (z * 4 + o) * 8 + c))
+        for yh in range(2):
+            for core in range(2):
+                for c in range(8):
+                    column = PANEL_COLUMNS[yh][c] // 10 ** (7 - z) % 10
+                    source = ((c * 2 + yh) * 2 + core) * 8 + column
+                    pairs.append((source, ((z * 2 + yh) * 2 + core) * 8 + c))
     return pairs
 
 
@@ -66,15 +75,7 @@
     return (8 - p) % 8
 
 
-def factor_kernel(msa_ref, first_ref, second_ref, pair_ref, shared_ref, right_ref, held, sems, result):
-    copies = [
-        pltpu.make_async_copy(
-            msa_ref.at[pl.ds(k * 32, 32)], held.at[pl.ds(k * 32, 32)], sems.at[k]
-        )
-        for k in range(4)
-    ]
-    for copy in copies:
-        copy.start()
+def factor_kernel(msa_ref, first_ref, second_ref, pair_ref, shared_ref, right_ref, result):
     w_high, w_low = split(jnp.concatenate([first_ref[...], second_ref[...]], 0))
     w_both = jnp.concatenate([w_high, w_low], 0)
     w_rest = jnp.concatenate([w_high, jnp.zeros_like(w_high)], 0)
@@ -82,8 +83,7 @@
     for p in range(8):
         shared_ref[pl.ds(256 + p * 16, 16), :] = pair_ref[turned_rows(p), other]
     for k in range(4):
-        copies[k].wait()
-        n_high, n_low = split(layer_norm(held[pl.ds(k * 32, 32)].reshape(256, 256), -1))
+        n_high, n_low = split(layer_norm(msa_ref[pl.ds(k * 32, 32)].reshape(256, 256), -1))
         result[pl.ds(k * 256, 256), :] = mm_t(n_high, w_both) + mm_t(n_low, w_rest)
     for i in range(8):
         turned = result[pl.ds(i, 128, stride=8), :].T
@@ -189,15 +189,13 @@
             out_ref[i, half] = mid[p : p + 16] + gate[p : p + 16] * update[i * 16 : i * 16 + 16]
 
 
-def call(kernel, out_shapes, scratch, *args, specs=None, limit=VMEM_LIMIT):
+def call(kernel, out_shapes, scratch, *args):
     shapes = [jax.ShapeDtypeStruct(s, jnp.float32) for s in out_shapes]
-    extra = {} if specs is None else {"in_specs": specs}
     return pl.pallas_call(
         kernel,
         out_shape=shapes if len(shapes) > 1 else shapes[0],
         scratch_shapes=scratch,
-        compiler_params=pltpu.CompilerParams(vmem_limit_bytes=limit),
-        **extra,
+        compiler_params=pltpu.CompilerParams(vmem_limit_bytes=VMEM_LIMIT),
     )(*args)
 
 
@@ -206,14 +204,8 @@
 
 
 def factors(homolog, first, second, pair):
-    inside = pl.BlockSpec(memory_space=pltpu.VMEM)
     return call(
-        factor_kernel,
-        [(384, 128), (256, 128)],
-        [vmem(128, 8, 256), pltpu.SemaphoreType.DMA((4,)), vmem(1024, 128)],
-        homolog, first, second, pair,
-        specs=[pl.BlockSpec(memory_space=pltpu.HBM), inside, inside, inside],
-        limit=60 * 1024 * 1024,
+        factor_kernel, [(384, 128), (256, 128)], [vmem(1024, 128)], homolog, first, second, pair
     )
 
 
@@ -246,6 +238,7 @@
     returned = lax.ppermute(sent, "yh", swap)
     swapped = lax.all_to_all(edges.reshape(64, 8, 128), LAYER, 0, 0, tiled=True)
     rights = lax.all_gather(swapped[:, 4:], "core", axis=0, tiled=True)
+    rights, returned = lax.optimization_barrier((rights, returned))
     back = triangle(swapped.reshape(512, 128), rights.reshape(512, 128))
     mixed = lax.all_to_all(back.reshape(128, 4, 128), CHIPS, 0, 0, tiled=True)
     return output_stage(mixed.reshape(512, 128), kept, returned, w_out).reshape(8, 32, 128)

time: 74.1 us -> 73.7 us (level)
  Pallas kernels: 8.78 us -> 4.96 us
  local copies, waits for them, and re-layouts: 0.49 us -> 4.13 us
  waiting for transfers between devices: 13.8 us -> 10.6 us
  blocking collectives: 27.6 us -> 29.7 us
    ppermute x1, waiting for transfers between devices: 4.69 us -> 0.01 us  [per_device(): returned = lax.ppermute(sent, 'yh', swap)]
    pallas_call x4, Pallas kernels: 8.78 us -> 4.96 us  [call(): pl.pallas_call(kernel, out_shape=shapes if len(shapes) > 1 else shapes[0]...]
    unnamed x13 -> x19, local copies, waits for them, and re-layouts: 0.15 us -> 3.79 us
    ppermute x1, waiting for transfers between devices: 0.29 us -> 2.67 us  [per_device(): met = lax.ppermute(shared, 'yh', swap)]
    ppermute x1, starting transfers between devices: 3.06 us -> 5.14 us  [per_device(): returned = lax.ppermute(sent, 'yh', swap)]
    all_to_all x1, blocking collectives: 23.7 us -> 25.7 us  [per_device(): mixed = lax.all_to_all(back.reshape(128, 4, 128), CHIPS, 0, 0, tiled=True)]
    ppermute x1, starting transfers between devices: 8.31 us -> 6.35 us  [per_device(): panel = lax.ppermute(right, ALL, panel_permutation())]
    ppermute x1, waiting for transfers between devices: 2.12 us -> 1 us  [per_device(): panel = lax.ppermute(right, ALL, panel_permutation())]
  transfers between devices with their start and end apart: 4 -> 4, of which waited for: 4 -> 3; matrix products, arithmetic and copies ran while one was open for 1% -> 1% of each run, Pallas kernels for 0% -> 0%
where the time goes in v5:
time: 73.7 us; the launch traced here: 73.2 us
  blocking collectives  29.7 us (40%)
  starting transfers between devices  23.7 us (32%)
  waiting for transfers between devices  10.6 us (14%)
  Pallas kernels  4.96 us (7%)
  local copies, waits for them, and re-layouts  4.13 us (6%)
    all_to_all x1, blocking collectives, per_device(): mixed = lax.all_to_all(back.reshape(128, 4, 128), CHIPS, 0, 0, tiled=True)  25.7 us
    all_to_all x1, starting transfers between devices, per_device(): swapped = lax.all_to_all(edges.reshape(64, 8, 128), LAYER, 0, 0, tiled=True)  9.02 us
    all_to_all x1, waiting for transfers between devices, per_device(): swapped = lax.all_to_all(edges.reshape(64, 8, 128), LAYER, 0, 0, tiled=True)  6.97 us
    ppermute x1, starting transfers between devices, per_device(): panel = lax.ppermute(right, ALL, panel_permutation())  6.35 us
    ppermute x1, starting transfers between devices, per_device(): returned = lax.ppermute(sent, 'yh', swap)  5.14 us
    pallas_call x4, Pallas kernels, call(): pl.pallas_call(kernel, out_shape=shapes if len(shapes) > 1 else shapes[0]...  4.96 us
    unnamed x19, local copies, waits for them, and re-layouts  3.79 us
    ppermute x1, starting transfers between devices, per_device(): met = lax.ppermute(shared, 'yh', swap)  3.19 us
  transfers between devices with their start and end apart: 4, of which 3 were waited for; matrix products, arithmetic and copies ran while one was open for 1% of the time, Pallas kernels for 0%

profile of v5, /device:TPU:2, one launch (start us, length us, event | category | flops | bytes accessed | tf_op | source)
XLA Modules:
  0.0 73.2 jit_solution(6307502664791887394)
XLA Ops:
  0.0 0.0 copy-start
  0.0 1.2 %copy-done = f32[128,8,256]{2,1,0:T(8,128)S(1)} copy-done((f32[128,8,256]{2,1,0:T(8,128)S(1)}, f32[128,8,256]{2,1,0:T(8,128)}, u32[]{:S(2)}) %copy-start) | copy-done | bytes 1048600
  1.2 0.0 copy-start.1
  1.2 0.9 %copy-done.1 = f32[8,32,128]{2,1,0:T(8,128)S(1)} copy-done((f32[8,32,128]{2,1,0:T(8,128)S(1)}, f32[8,32,128]{2,1,0:T(8,128)}, u32[]{:S(2)}) %copy-start.1) | copy-done | bytes 131096
  2.1 0.8 %copy-done.5 = f32[256,32]{0,1:T(8,128)S(1)} copy-done((f32[256,32]{0,1:T(8,128)S(1)}, f32[256,32]{0,1:T(8,128)}, u32[]{:S(2)}) %copy-start.5) | copy-done | bytes 32792
  2.9 0.8 %copy-done.6 = f32[256,32]{0,1:T(8,128)S(1)} copy-done((f32[256,32]{0,1:T(8,128)S(1)}, f32[256,32]{0,1:T(8,128)}, u32[]{:S(2)}) %copy-start.6) | copy-done | bytes 32792
  3.6 0.9 %shard_map.82 = (f32[384,128]{1,0:T(8,128)S(1)}, f32[256,128]{1,0:T(8,128)S(1)}) custom-call(f32[128,8,256]{2,1,0:T(8,128)S(1)} %copy-done, f32[32,256]{1,0:T(8,128)S(1)} %bitcast.22, f32[32,256]{1,0:T(8,128)S(1)} %bitcast.23, f32[8,2,16,128]{3,2,1,0:T(8,128)S(1)} %bitcast.20), custom_call_target="tpu_custom_call" | custom-call | tf_op jit(solution)/shard_map/pallas_call | solution.py:194
  4.5 0.0 copy-start.7
  4.6 6.3 %collective-permute-start.1 = (f32[256,128]{1,0:T(8,128)S(1)}, f32[256,128]{1,0:T(8,128)S(1)}, u32[]{:S(2)}, u32[]{:S(2)}) collective-permute-start(f32[256,128]{1,0:T(8,128)S(1)} %get-tuple-element.13), channel_id=1, source_target_pairs={{3,0},{34,1},{64,2},{96,3},{128,4},{160,5},{193,6},{224,7},{11,8},... | collective-permute-start | bytes 393224 | tf_op jit(solution)/shard_map/ppermute | solution.py:233
  10.9 3.2 %collective-permute-start = (f32[384,128]{1,0:T(8,128)S(1)}, f32[384,128]{1,0:T(8,128)S(1)}, u32[]{:S(2)}, u32[]{:S(2)}) collective-permute-start(f32[384,128]{1,0:T(8,128)S(1)} %get-tuple-element.12.own_ref), channel_id=1, source_target_pairs={{0,16},{16,0},{1,17},{17,1},{2,18},{18,2},{3,19},{19,3},{4,20},{20... | collective-permute-start | bytes 589832 | tf_op jit(solution)/shard_map/ppermute | solution.py:234
  14.1 0.0 copy-done.8
  14.1 0.1 copy.12
  14.2 0.0 copy-done.7
  14.2 0.3 copy.11
  14.6 0.0 copy-start.2
  14.6 0.0 copy-start.3
  14.6 1.0 %collective-permute-done.1 = f32[256,128]{1,0:T(8,128)S(1)} collective-permute-done((f32[256,128]{1,0:T(8,128)S(1)}, f32[256,128]{1,0:T(8,128)S(1)}, u32[]{:S(2)}, u32[]{:S(2)}) %collective-permute-start.1) | collective-permute-done | bytes 131104 | tf_op jit(solution)/shard_map/ppermute | solution.py:233
  15.6 2.0 %all_gather.6.panel_ref = f32[512,128]{1,0:T(8,128)S(1)} all-gather(f32[256,128]{1,0:T(8,128)S(1)} %collective-permute-done.1), channel_id=1, replica_groups=mesh['z'=8,'yh'=2,'core'=2,'x'=4,'yl'=2] {'core'}, dimensions={0}, use_global_device_ids=true | all-gather | bytes 393216 | tf_op jit(solution)/shard_map/all_gather | solution.py:236
  17.6 2.7 %collective-permute-done.met_ref = f32[384,128]{1,0:T(8,128)S(1)} collective-permute-done((f32[384,128]{1,0:T(8,128)S(1)}, f32[384,128]{1,0:T(8,128)S(1)}, u32[]{:S(2)}, u32[]{:S(2)}) %collective-permute-start) | collective-permute-done | bytes 196640 | tf_op jit(solution)/shard_map/ppermute | solution.py:234
  20.2 0.0 copy-done.2
  20.2 0.0 copy-done.3
  20.2 2.4 %shard_map.83 = (f32[512,128]{1,0:T(8,128)}, f32[2,128,128]{2,1,0:T(8,128)S(1)}, f32[2,128,128]{2,1,0:T(8,128)S(1)}) custom-call(f32[384,128]{1,0:T(8,128)S(1)} %get-tuple-element.12.own_ref, f32[384,128]{1,0:T(8,128)S(1)} %collective-permute-done.met_ref, f32[512,128]{1,0:T(8,128)S(1)} %all_gather.6.panel_ref, f32[8,2,16,128]{3,2,1,0:T(8,128)S(1)} %bitcast.21, ...), custom_call_target="tpu_custom_call" | custom-call | tf_op jit(solution)/shard_map/pallas_call | solution.py:194
  22.7 9.0 %all-to-all-start = ((f32[64,8,128]{2,1,0:T(8,128)}), f32[64,8,128]{2,1,0:T(8,128)S(1)}, u32[]{:S(2)}, u32[]{:S(2)}) async-start(f32[64,8,128]{2,1,0:T(8,128)} %bitcast.7), calls=%async_computation | async-start | bytes 524288 | tf_op jit(solution)/shard_map/all_to_all | solution.py:239
  31.7 5.1 %collective-permute-start.2 = (f32[2,128,128]{2,1,0:T(8,128)S(1)}, f32[2,128,128]{2,1,0:T(8,128)S(1)}, u32[]{:S(2)}, u32[]{:S(2)}) collective-permute-start(f32[2,128,128]{2,1,0:T(8,128)S(1)} %get-tuple-element.15), channel_id=1, source_target_pairs={{0,16},{16,0},{1,17},{17,1},{2,18},{18,2},{3,19},{19,3},{4,20},{20... | collective-permute-start | bytes 393224 | tf_op jit(solution)/shard_map/ppermute | solution.py:238
  36.8 7.0 %all-to-all-done = f32[64,8,128]{2,1,0:T(8,128)S(1)} async-done(((f32[64,8,128]{2,1,0:T(8,128)}), f32[64,8,128]{2,1,0:T(8,128)S(1)}, u32[]{:S(2)}, u32[]{:S(2)}) %all-to-all-start) | async-done | bytes 262176 | tf_op jit(solution)/shard_map/all_to_all | solution.py:239
  43.8 2.0 %all_gather.7 = f32[128,4,128]{2,1,0:T(4,128)S(1)} all-gather(f32[64,4,128]{2,1,0:T(4,128)S(1)} %slice.4), channel_id=1, replica_groups=mesh['z'=8,'yh'=2,'core'=2,'x'=4,'yl'=2] {'core'}, dimensions={0}, use_global_device_ids=true | all-gather | bytes 393216 | tf_op jit(solution)/shard_map/all_gather | solution.py:240
  45.8 0.0 collective-permute-done.2.met_ref
  45.8 0.7 shard_map.84
  46.5 0.0 copy-start.4
  46.5 25.7 %all_to_all.10 = f32[128,4,128]{2,1,0:T(4,128)S(1)} all-to-all(f32[128,4,128]{2,1,0:T(4,128)S(1)} %bitcast.18), channel_id=1, replica_groups=mesh['z'=8,'yh'=2,'core'=2,'x'=4,'yl'=2] {'z','yh','x','yl'}, dimensions={0} | all-to-all | bytes 524288 | tf_op jit(solution)/shard_map/all_to_all | solution.py:243
  72.2 0.0 copy-done.4
  72.3 1.0 %shard_map.85 = f32[8,2,16,128]{3,2,1,0:T(8,128)} custom-call(f32[512,128]{1,0:T(8,128)S(1)} %bitcast.19, f32[2,128,128]{2,1,0:T(8,128)S(1)} %get-tuple-element.17.kept_ref, f32[2,128,128]{2,1,0:T(8,128)S(1)} %collective-permute-done.2.met_ref, f32[128,128]{1,0:T(8,128)S(1)} %copy-done.4), custom_call_target="tpu_custom_call" | custom-call | tf_op jit(solution)/shard_map/pallas_call | solution.py:194
  (4 shorter events, 0.0 us)
Async XLA Ops:
  0.0 1.2 %copy-start = (f32[128,8,256]{2,1,0:T(8,128)S(1)}, f32[128,8,256]{2,1,0:T(8,128)}, u32[]{:S(2)}) copy-start(f32[128,8,256]{2,1,0:T(8,128)} %msa_ref.1) | copy-start | bytes 3145732
  1.2 0.9 %copy-start.1 = (f32[8,32,128]{2,1,0:T(8,128)S(1)}, f32[8,32,128]{2,1,0:T(8,128)}, u32[]{:S(2)}) copy-start(f32[8,32,128]{2,1,0:T(8,128)} %param.9) | copy-start | bytes 393220
  2.1 0.8 %copy-start.5 = (f32[256,32]{0,1:T(8,128)S(1)}, f32[256,32]{0,1:T(8,128)}, u32[]{:S(2)}) copy-start(f32[256,32]{0,1:T(8,128)} %param.10) | copy-start | bytes 98308
  2.9 0.8 %copy-start.6 = (f32[256,32]{0,1:T(8,128)S(1)}, f32[256,32]{0,1:T(8,128)}, u32[]{:S(2)}) copy-start(f32[256,32]{0,1:T(8,128)} %param.11) | copy-start | bytes 98308
  3.6 10.5 %copy-start.8 = (f32[128,512]{1,0:T(8,128)S(1)}, f32[128,512]{1,0:T(8,128)}, u32[]{:S(2)}) copy-start(f32[128,512]{1,0:T(8,128)} %param.13) | copy-start | bytes 786436
  4.5 9.7 %copy-start.7 = (f32[1024,128]{1,0:T(8,128)S(1)}, f32[1024,128]{1,0:T(8,128)}, u32[]{:S(2)}) copy-start(f32[1024,128]{1,0:T(8,128)} %param.12) | copy-start | bytes 1572868
  4.6 11.0 %collective-permute-start.1 = (f32[256,128]{1,0:T(8,128)S(1)}, f32[256,128]{1,0:T(8,128)S(1)}, u32[]{:S(2)}, u32[]{:S(2)}) collective-permute-start(f32[256,128]{1,0:T(8,128)S(1)} %get-tuple-element.13), channel_id=1, source_target_pairs={{3,0},{34,1},{64,2},{96,3},{128,4},{160,5},{193,6},{224,7},{11,8},... | collective-permute-start | bytes 393224 | tf_op jit(solution)/shard_map/ppermute | solution.py:233
  10.9 9.3 %collective-permute-start = (f32[384,128]{1,0:T(8,128)S(1)}, f32[384,128]{1,0:T(8,128)S(1)}, u32[]{:S(2)}, u32[]{:S(2)}) collective-permute-start(f32[384,128]{1,0:T(8,128)S(1)} %get-tuple-element.12.own_ref), channel_id=1, source_target_pairs={{0,16},{16,0},{1,17},{17,1},{2,18},{18,2},{3,19},{19,3},{4,20},{20... | collective-permute-start | bytes 589832 | tf_op jit(solution)/shard_map/ppermute | solution.py:234
  14.6 5.7 %copy-start.2 = (f32[8,32,128]{2,1,0:T(8,128)S(1)}, f32[8,32,128]{2,1,0:T(8,128)}, u32[]{:S(2)}) copy-start(f32[8,32,128]{2,1,0:T(8,128)} %param.9) | copy-start | bytes 393220
  14.6 5.7 %copy-start.3 = (f32[128,128]{1,0:T(8,128)S(1)}, f32[128,128]{1,0:T(8,128)}, u32[]{:S(2)}) copy-start(f32[128,128]{1,0:T(8,128)} %w_gate_ref.1) | copy-start | bytes 196612
  22.7 21.1 %all-to-all-start = ((f32[64,8,128]{2,1,0:T(8,128)}), f32[64,8,128]{2,1,0:T(8,128)S(1)}, u32[]{:S(2)}, u32[]{:S(2)}) async-start(f32[64,8,128]{2,1,0:T(8,128)} %bitcast.7), calls=%async_computation | async-start | bytes 524288 | tf_op jit(solution)/shard_map/all_to_all | solution.py:239
  31.7 14.1 %collective-permute-start.2 = (f32[2,128,128]{2,1,0:T(8,128)S(1)}, f32[2,128,128]{2,1,0:T(8,128)S(1)}, u32[]{:S(2)}, u32[]{:S(2)}) collective-permute-start(f32[2,128,128]{2,1,0:T(8,128)S(1)} %get-tuple-element.15), channel_id=1, source_target_pairs={{0,16},{16,0},{1,17},{17,1},{2,18},{18,2},{3,19},{19,3},{4,20},{20... | collective-permute-start | bytes 393224 | tf_op jit(solution)/shard_map/ppermute | solution.py:238
  46.5 25.8 %copy-start.4 = (f32[128,128]{1,0:T(8,128)S(1)}, f32[128,128]{1,0:T(8,128)}, u32[]{:S(2)}) copy-start(f32[128,128]{1,0:T(8,128)} %w_ref.1) | copy-start | bytes 196612

commit v6 on v5

--- a/solution.py
+++ b/solution.py
@@ -75,21 +75,41 @@
     return (8 - p) % 8
 
 
-def factor_kernel(msa_ref, first_ref, second_ref, pair_ref, shared_ref, right_ref, result):
-    w_high, w_low = split(jnp.concatenate([first_ref[...], second_ref[...]], 0))
+def factor_kernel(
+    msa_ref, first_ref, second_ref, pair_ref, shared_ref, right_ref,
+    msa, w, pair, result, sems,
+):
+    other = 1 - lax.axis_index("yh")
+    weights = [
+        pltpu.make_async_copy(first_ref, w.at[pl.ds(0, 32)], sems.at[4]),
+        pltpu.make_async_copy(second_ref, w.at[pl.ds(32, 32)], sems.at[5]),
+    ]
+    chunks = [
+        pltpu.make_async_copy(
+            msa_ref.at[pl.ds(k * 32, 32)], msa.at[pl.ds(k * 32, 32)], sems.at[k]
+        )
+        for k in range(4)
+    ]
+    pairs = pltpu.make_async_copy(pair_ref, pair, sems.at[6])
+    for copy in weights + chunks + [pairs]:
+        copy.start()
+    for copy in weights:
+        copy.wait()
+    w_high, w_low = split(w[...])
     w_both = jnp.concatenate([w_high, w_low], 0)
     w_rest = jnp.concatenate([w_high, jnp.zeros_like(w_high)], 0)
-    other = 1 - lax.axis_index("yh")
-    for p in range(8):
-        shared_ref[pl.ds(256 + p * 16, 16), :] = pair_ref[turned_rows(p), other]
     for k in range(4):
-        n_high, n_low = split(layer_norm(msa_ref[pl.ds(k * 32, 32)].reshape(256, 256), -1))
+        chunks[k].wait()
+        n_high, n_low = split(layer_norm(msa[pl.ds(k * 32, 32)].reshape(256, 256), -1))
         result[pl.ds(k * 256, 256), :] = mm_t(n_high, w_both) + mm_t(n_low, w_rest)
     for i in range(8):
         turned = result[pl.ds(i, 128, stride=8), :].T
         both = turned[:64] + turned[64:]
         shared_ref[pl.ds(i * 32, 32), :] = both[:32] * (1.0 / 128.0)
         right_ref[pl.ds(i, 32, stride=8), :] = both[32:]
+    pairs.wait()
+    for p in range(8):
+        shared_ref[pl.ds(256 + p * 16, 16), :] = pair[turned_rows(p), other]
 
 
 def pair_kernel(
@@ -189,13 +209,14 @@
             out_ref[i, half] = mid[p : p + 16] + gate[p : p + 16] * update[i * 16 : i * 16 + 16]
 
 
-def call(kernel, out_shapes, scratch, *args):
+def call(kernel, out_shapes, scratch, *args, limit=VMEM_LIMIT, **more):
     shapes = [jax.ShapeDtypeStruct(s, jnp.float32) for s in out_shapes]
     return pl.pallas_call(
         kernel,
         out_shape=shapes if len(shapes) > 1 else shapes[0],
         scratch_shapes=scratch,
-        compiler_params=pltpu.CompilerParams(vmem_limit_bytes=VMEM_LIMIT),
+        compiler_params=pltpu.CompilerParams(vmem_limit_bytes=limit),
+        **more,
     )(*args)
 
 
@@ -205,7 +226,15 @@
 
 def factors(homolog, first, second, pair):
     return call(
-        factor_kernel, [(384, 128), (256, 128)], [vmem(1024, 128)], homolog, first, second, pair
+        factor_kernel,
+        [(384, 128), (256, 128)],
+        [
+            vmem(128, 8, 256), vmem(64, 256), vmem(8, 2, 16, 128), vmem(1024, 128),
+            pltpu.SemaphoreType.DMA((7,)),
+        ],
+        homolog, first, second, pair,
+        in_specs=[pl.BlockSpec(memory_space=pltpu.HBM)] * 4,
+        limit=53 * 1024 * 1024,
     )
 
 
@@ -235,11 +264,12 @@
     w_outer_ba = w_outer.reshape(32, 32, 128).transpose(1, 0, 2).reshape(1024, 128)
     panel = lax.all_gather(panel, "core", axis=0, tiled=True)
     edges, kept, sent = pair_stage(shared, met, panel, pair, w_outer_ba, w_tri.T, w_gate)
+    swapped = lax.all_to_all(edges.reshape(64, 8, 128), LAYER, 0, 0, tiled=True)
+    sent, swapped = lax.optimization_barrier((sent, swapped))
     returned = lax.ppermute(sent, "yh", swap)
-    swapped = lax.all_to_all(edges.reshape(64, 8, 128), LAYER, 0, 0, tiled=True)
     rights = lax.all_gather(swapped[:, 4:], "core", axis=0, tiled=True)
-    rights, returned = lax.optimization_barrier((rights, returned))
     back = triangle(swapped.reshape(512, 128), rights.reshape(512, 128))
+    back, returned = lax.optimization_barrier((back, returned))
     mixed = lax.all_to_all(back.reshape(128, 4, 128), CHIPS, 0, 0, tiled=True)
     return output_stage(mixed.reshape(512, 128), kept, returned, w_out).reshape(8, 32, 128)
 

time: 73.7 us -> 75.9 us (1.030)
  blocking collectives: 29.7 us -> 47.4 us
  starting transfers between devices: 23.7 us -> 14.7 us
  waiting for transfers between devices: 10.6 us -> 3.91 us
  Pallas kernels: 4.96 us -> 6.48 us
  local copies, waits for them, and re-layouts: 4.13 us -> 2.9 us
    all_to_all x0 -> x1, blocking collectives: none -> 20.9 us  [per_device(): swapped = lax.all_to_all(edges.reshape(64, 8, 128), LAYER, 0, 0, tiled=True)]
    all_to_all x1 -> x0, starting transfers between devices: 9.02 us -> none  [per_device(): swapped = lax.all_to_all(edges.reshape(64, 8, 128), LAYER, 0, 0, tiled=True)]
    all_to_all x1 -> x0, waiting for transfers between devices: 6.97 us -> none  [per_device(): swapped = lax.all_to_all(edges.reshape(64, 8, 128), LAYER, 0, 0, tiled=True)]
    all_to_all x1, blocking collectives: 25.7 us -> 22.5 us  [per_device(): mixed = lax.all_to_all(back.reshape(128, 4, 128), CHIPS, 0, 0, tiled=True)]
    pallas_call x4, Pallas kernels: 4.96 us -> 6.48 us  [call(): pl.pallas_call(kernel, out_shape=shapes if len(shapes) > 1 else shapes[0]...]
    unnamed x19 -> x17, local copies, waits for them, and re-layouts: 3.79 us -> 2.57 us
  transfers between devices with their start and end apart: 4 -> 3, of which waited for: 3 -> 3; matrix products, arithmetic and copies ran while one was open for 1% -> 1% of each run, Pallas kernels for 0% -> 1%
where the time goes in v6:
time: 75.9 us; the launch traced here: 75.5 us
  blocking collectives  47.4 us (62%)
  starting transfers between devices  14.7 us (19%)
  Pallas kernels  6.48 us (9%)
  waiting for transfers between devices  3.91 us (5%)
  local copies, waits for them, and re-layouts  2.9 us (4%)
    all_to_all x1, blocking collectives, per_device(): mixed = lax.all_to_all(back.reshape(128, 4, 128), CHIPS, 0, 0, tiled=True)  22.5 us
    all_to_all x1, blocking collectives, per_device(): swapped = lax.all_to_all(edges.reshape(64, 8, 128), LAYER, 0, 0, tiled=True)  20.9 us
    pallas_call x4, Pallas kernels, call(): pl.pallas_call(kernel, out_shape=shapes if len(shapes) > 1 else shapes[0]...  6.48 us
    ppermute x1, starting transfers between devices, per_device(): panel = lax.ppermute(right, ALL, panel_permutation())  6.35 us
    ppermute x1, starting transfers between devices, per_device(): returned = lax.ppermute(sent, 'yh', swap)  5.18 us
    ppermute x1, starting transfers between devices, per_device(): met = lax.ppermute(shared, 'yh', swap)  3.19 us
    ppermute x1, waiting for transfers between devices, per_device(): met = lax.ppermute(shared, 'yh', swap)  2.67 us
    unnamed x17, local copies, waits for them, and re-layouts  2.57 us
  transfers between devices with their start and end apart: 3, of which 3 were waited for; matrix products, arithmetic and copies ran while one was open for 1% of the time, Pallas kernels for 1%

profile of v6, /device:TPU:2, one launch (start us, length us, event | category | flops | bytes accessed | tf_op | source)
XLA Modules:
  0.0 75.5 jit_solution(12728557724455971233)
XLA Ops:
  0.0 0.0 copy-start
  0.0 0.9 %copy-done = f32[8,32,128]{2,1,0:T(8,128)S(1)} copy-done((f32[8,32,128]{2,1,0:T(8,128)S(1)}, f32[8,32,128]{2,1,0:T(8,128)}, u32[]{:S(2)}) %copy-start) | copy-done | bytes 131096
  0.9 0.0 copy-start.4
  0.9 0.8 %copy-done.4 = f32[256,32]{0,1:T(8,128)S(1)} copy-done((f32[256,32]{0,1:T(8,128)S(1)}, f32[256,32]{0,1:T(8,128)}, u32[]{:S(2)}) %copy-start.4) | copy-done | bytes 32792
  1.7 0.0 copy-start.5
  1.7 0.8 %copy-done.5 = f32[256,32]{0,1:T(8,128)S(1)} copy-done((f32[256,32]{0,1:T(8,128)S(1)}, f32[256,32]{0,1:T(8,128)}, u32[]{:S(2)}) %copy-start.5) | copy-done | bytes 32792
  2.4 0.0 copy-start.7
  2.4 3.1 %shard_map.82 = (f32[384,128]{1,0:T(8,128)S(1)}, f32[256,128]{1,0:T(8,128)S(1)}) custom-call(f32[128,8,256]{2,1,0:T(8,128)} %msa_ref.1, f32[32,256]{1,0:T(8,128)S(1)} %bitcast.23, f32[32,256]{1,0:T(8,128)S(1)} %bitcast.24, f32[8,2,16,128]{3,2,1,0:T(8,128)S(1)} %bitcast.20), custom_call_target="tpu_custom_call" | custom-call | tf_op jit(solution)/shard_map/pallas_call | solution.py:214
  5.5 0.0 copy-start.6
  5.6 6.4 %collective-permute-start.1 = (f32[256,128]{1,0:T(8,128)S(1)}, f32[256,128]{1,0:T(8,128)S(1)}, u32[]{:S(2)}, u32[]{:S(2)}) collective-permute-start(f32[256,128]{1,0:T(8,128)S(1)} %get-tuple-element.15), channel_id=1, source_target_pairs={{3,0},{34,1},{64,2},{96,3},{128,4},{160,5},{193,6},{224,7},{11,8},... | collective-permute-start | bytes 393224 | tf_op jit(solution)/shard_map/ppermute | solution.py:262
  11.9 3.2 %collective-permute-start = (f32[384,128]{1,0:T(8,128)S(1)}, f32[384,128]{1,0:T(8,128)S(1)}, u32[]{:S(2)}, u32[]{:S(2)}) collective-permute-start(f32[384,128]{1,0:T(8,128)S(1)} %get-tuple-element.14.own_ref), channel_id=1, source_target_pairs={{0,16},{16,0},{1,17},{17,1},{2,18},{18,2},{3,19},{19,3},{4,20},{20... | collective-permute-start | bytes 589832 | tf_op jit(solution)/shard_map/ppermute | solution.py:263
  15.1 0.0 copy-done.7
  15.1 0.1 copy.12
  15.2 0.0 copy-done.6
  15.2 0.3 copy.11
  15.6 0.0 copy-start.1
  15.6 0.0 copy-start.2
  15.6 1.0 %collective-permute-done.1 = f32[256,128]{1,0:T(8,128)S(1)} collective-permute-done((f32[256,128]{1,0:T(8,128)S(1)}, f32[256,128]{1,0:T(8,128)S(1)}, u32[]{:S(2)}, u32[]{:S(2)}) %collective-permute-start.1) | collective-permute-done | bytes 131104 | tf_op jit(solution)/shard_map/ppermute | solution.py:262
  16.6 2.0 %all_gather.6.panel_ref = f32[512,128]{1,0:T(8,128)S(1)} all-gather(f32[256,128]{1,0:T(8,128)S(1)} %collective-permute-done.1), channel_id=1, replica_groups=mesh['z'=8,'yh'=2,'core'=2,'x'=4,'yl'=2] {'core'}, dimensions={0}, use_global_device_ids=true | all-gather | bytes 393216 | tf_op jit(solution)/shard_map/all_gather | solution.py:265
  18.6 2.7 %collective-permute-done.met_ref = f32[384,128]{1,0:T(8,128)S(1)} collective-permute-done((f32[384,128]{1,0:T(8,128)S(1)}, f32[384,128]{1,0:T(8,128)S(1)}, u32[]{:S(2)}, u32[]{:S(2)}) %collective-permute-start) | collective-permute-done | bytes 196640 | tf_op jit(solution)/shard_map/ppermute | solution.py:263
  21.2 0.0 copy-done.1
  21.2 0.0 copy-done.2
  21.2 1.7 %shard_map.83 = (f32[512,128]{1,0:T(8,128)S(1)}, f32[2,128,128]{2,1,0:T(8,128)S(1)}, f32[2,128,128]{2,1,0:T(8,128)S(1)}) custom-call(f32[384,128]{1,0:T(8,128)S(1)} %get-tuple-element.14.own_ref, f32[384,128]{1,0:T(8,128)S(1)} %collective-permute-done.met_ref, f32[512,128]{1,0:T(8,128)S(1)} %all_gather.6.panel_ref, f32[8,2,16,128]{3,2,1,0:T(8,128)S(1)} %bitcast.21, ...), custom_call_target="tpu_custom_call" | custom-call | tf_op jit(solution)/shard_map/pallas_call | solution.py:214
  23.0 20.9 %all_to_all.10 = f32[64,8,128]{2,1,0:T(8,128)S(1)} all-to-all(f32[64,8,128]{2,1,0:T(8,128)S(1)} %bitcast.22), channel_id=1, replica_groups=mesh['z'=8,'yh'=2,'core'=2,'x'=4,'yl'=2] {'z','x','yl'}, dimensions={0} | all-to-all | bytes 524288 | tf_op jit(solution)/shard_map/all_to_all | solution.py:267
  43.9 5.2 %collective-permute-start.2 = (f32[2,128,128]{2,1,0:T(8,128)S(1)}, f32[2,128,128]{2,1,0:T(8,128)S(1)}, u32[]{:S(2)}, u32[]{:S(2)}) collective-permute-start(f32[2,128,128]{2,1,0:T(8,128)S(1)} %get-tuple-element.19), channel_id=1, source_target_pairs={{0,16},{16,0},{1,17},{17,1},{2,18},{18,2},{3,19},{19,3},{4,20},{20... | collective-permute-start | bytes 393224 | tf_op jit(solution)/shard_map/ppermute | solution.py:269
  49.1 2.0 %all_gather.7 = f32[128,4,128]{2,1,0:T(4,128)S(1)} all-gather(f32[64,4,128]{2,1,0:T(4,128)S(1)} %slice.3), channel_id=1, replica_groups=mesh['z'=8,'yh'=2,'core'=2,'x'=4,'yl'=2] {'core'}, dimensions={0}, use_global_device_ids=true | all-gather | bytes 393216 | tf_op jit(solution)/shard_map/all_gather | solution.py:270
  51.1 0.7 shard_map.84
  51.8 0.2 collective-permute-done.2.met_ref
  52.0 0.0 copy-start.3
  52.0 22.5 %all_to_all.11 = f32[128,4,128]{2,1,0:T(4,128)S(1)} all-to-all(f32[128,4,128]{2,1,0:T(4,128)S(1)} %bitcast.17), channel_id=1, replica_groups=mesh['z'=8,'yh'=2,'core'=2,'x'=4,'yl'=2] {'z','yh','x','yl'}, dimensions={0} | all-to-all | bytes 524288 | tf_op jit(solution)/shard_map/all_to_all | solution.py:273
  74.5 0.0 copy-done.3
  74.5 1.0 %shard_map.85 = f32[8,2,16,128]{3,2,1,0:T(8,128)} custom-call(f32[512,128]{1,0:T(8,128)S(1)} %bitcast.19, f32[2,128,128]{2,1,0:T(8,128)S(1)} %get-tuple-element.21.kept_ref, f32[2,128,128]{2,1,0:T(8,128)S(1)} %collective-permute-done.2.met_ref, f32[128,128]{1,0:T(8,128)S(1)} %copy-done.3), custom_call_target="tpu_custom_call" | custom-call | tf_op jit(solution)/shard_map/pallas_call | solution.py:214
  (1 shorter events, 0.0 us)
Async XLA Ops:
  0.0 0.9 %copy-start = (f32[8,32,128]{2,1,0:T(8,128)S(1)}, f32[8,32,128]{2,1,0:T(8,128)}, u32[]{:S(2)}) copy-start(f32[8,32,128]{2,1,0:T(8,128)} %param.9) | copy-start | bytes 393220
  0.9 0.8 %copy-start.4 = (f32[256,32]{0,1:T(8,128)S(1)}, f32[256,32]{0,1:T(8,128)}, u32[]{:S(2)}) copy-start(f32[256,32]{0,1:T(8,128)} %param.10) | copy-start | bytes 98308
  1.7 0.8 %copy-start.5 = (f32[256,32]{0,1:T(8,128)S(1)}, f32[256,32]{0,1:T(8,128)}, u32[]{:S(2)}) copy-start(f32[256,32]{0,1:T(8,128)} %param.11) | copy-start | bytes 98308
  2.4 12.7 %copy-start.7 = (f32[128,512]{1,0:T(8,128)S(1)}, f32[128,512]{1,0:T(8,128)}, u32[]{:S(2)}) copy-start(f32[128,512]{1,0:T(8,128)} %param.13) | copy-start | bytes 786436
  5.5 9.7 %copy-start.6 = (f32[1024,128]{1,0:T(8,128)S(1)}, f32[1024,128]{1,0:T(8,128)}, u32[]{:S(2)}) copy-start(f32[1024,128]{1,0:T(8,128)} %param.12) | copy-start | bytes 1572868
  5.6 11.0 %collective-permute-start.1 = (f32[256,128]{1,0:T(8,128)S(1)}, f32[256,128]{1,0:T(8,128)S(1)}, u32[]{:S(2)}, u32[]{:S(2)}) collective-permute-start(f32[256,128]{1,0:T(8,128)S(1)} %get-tuple-element.15), channel_id=1, source_target_pairs={{3,0},{34,1},{64,2},{96,3},{128,4},{160,5},{193,6},{224,7},{11,8},... | collective-permute-start | bytes 393224 | tf_op jit(solution)/shard_map/ppermute | solution.py:262
  11.9 9.3 %collective-permute-start = (f32[384,128]{1,0:T(8,128)S(1)}, f32[384,128]{1,0:T(8,128)S(1)}, u32[]{:S(2)}, u32[]{:S(2)}) collective-permute-start(f32[384,128]{1,0:T(8,128)S(1)} %get-tuple-element.14.own_ref), channel_id=1, source_target_pairs={{0,16},{16,0},{1,17},{17,1},{2,18},{18,2},{3,19},{19,3},{4,20},{20... | collective-permute-start | bytes 589832 | tf_op jit(solution)/shard_map/ppermute | solution.py:263
  15.6 5.7 %copy-start.1 = (f32[8,32,128]{2,1,0:T(8,128)S(1)}, f32[8,32,128]{2,1,0:T(8,128)}, u32[]{:S(2)}) copy-start(f32[8,32,128]{2,1,0:T(8,128)} %param.9) | copy-start | bytes 393220
  15.6 5.7 %copy-start.2 = (f32[128,128]{1,0:T(8,128)S(1)}, f32[128,128]{1,0:T(8,128)}, u32[]{:S(2)}) copy-start(f32[128,128]{1,0:T(8,128)} %w_gate_ref.1) | copy-start | bytes 196612
  43.9 8.1 %collective-permute-start.2 = (f32[2,128,128]{2,1,0:T(8,128)S(1)}, f32[2,128,128]{2,1,0:T(8,128)S(1)}, u32[]{:S(2)}, u32[]{:S(2)}) collective-permute-start(f32[2,128,128]{2,1,0:T(8,128)S(1)} %get-tuple-element.19), channel_id=1, source_target_pairs={{0,16},{16,0},{1,17},{17,1},{2,18},{18,2},{3,19},{19,3},{4,20},{20... | collective-permute-start | bytes 393224 | tf_op jit(solution)/shard_map/ppermute | solution.py:269
  52.0 22.5 %copy-start.3 = (f32[128,128]{1,0:T(8,128)S(1)}, f32[128,128]{1,0:T(8,128)}, u32[]{:S(2)}) copy-start(f32[128,128]{1,0:T(8,128)} %w_ref.1) | copy-start | bytes 196612

commit v7 on v5

--- a/solution.py
+++ b/solution.py
@@ -76,12 +76,10 @@
 
 
 def factor_kernel(msa_ref, first_ref, second_ref, pair_ref, shared_ref, right_ref, result):
+    other = 1 - lax.axis_index("yh")
     w_high, w_low = split(jnp.concatenate([first_ref[...], second_ref[...]], 0))
     w_both = jnp.concatenate([w_high, w_low], 0)
     w_rest = jnp.concatenate([w_high, jnp.zeros_like(w_high)], 0)
-    other = 1 - lax.axis_index("yh")
-    for p in range(8):
-        shared_ref[pl.ds(256 + p * 16, 16), :] = pair_ref[turned_rows(p), other]
     for k in range(4):
         n_high, n_low = split(layer_norm(msa_ref[pl.ds(k * 32, 32)].reshape(256, 256), -1))
         result[pl.ds(k * 256, 256), :] = mm_t(n_high, w_both) + mm_t(n_low, w_rest)
@@ -90,6 +88,8 @@
         both = turned[:64] + turned[64:]
         shared_ref[pl.ds(i * 32, 32), :] = both[:32] * (1.0 / 128.0)
         right_ref[pl.ds(i, 32, stride=8), :] = both[32:]
+    for p in range(8):
+        shared_ref[pl.ds(256 + p * 16, 16), :] = pair_ref[turned_rows(p), other]
 
 
 def pair_kernel(
@@ -189,13 +189,13 @@
             out_ref[i, half] = mid[p : p + 16] + gate[p : p + 16] * update[i * 16 : i * 16 + 16]
 
 
-def call(kernel, out_shapes, scratch, *args):
+def call(kernel, out_shapes, scratch, *args, limit=VMEM_LIMIT):
     shapes = [jax.ShapeDtypeStruct(s, jnp.float32) for s in out_shapes]
     return pl.pallas_call(
         kernel,
         out_shape=shapes if len(shapes) > 1 else shapes[0],
         scratch_shapes=scratch,
-        compiler_params=pltpu.CompilerParams(vmem_limit_bytes=VMEM_LIMIT),
+        compiler_params=pltpu.CompilerParams(vmem_limit_bytes=limit),
     )(*args)
 
 
@@ -205,7 +205,8 @@
 
 def factors(homolog, first, second, pair):
     return call(
-        factor_kernel, [(384, 128), (256, 128)], [vmem(1024, 128)], homolog, first, second, pair
+        factor_kernel, [(384, 128), (256, 128)], [vmem(1024, 128)], homolog, first, second, pair,
+        limit=60 * 1024 * 1024,
     )
 
 
@@ -235,10 +236,9 @@
     w_outer_ba = w_outer.reshape(32, 32, 128).transpose(1, 0, 2).reshape(1024, 128)
     panel = lax.all_gather(panel, "core", axis=0, tiled=True)
     edges, kept, sent = pair_stage(shared, met, panel, pair, w_outer_ba, w_tri.T, w_gate)
+    swapped = lax.all_to_all(edges.reshape(64, 8, 128), LAYER, 0, 0, tiled=True)
     returned = lax.ppermute(sent, "yh", swap)
-    swapped = lax.all_to_all(edges.reshape(64, 8, 128), LAYER, 0, 0, tiled=True)
     rights = lax.all_gather(swapped[:, 4:], "core", axis=0, tiled=True)
-    rights, returned = lax.optimization_barrier((rights, returned))
     back = triangle(swapped.reshape(512, 128), rights.reshape(512, 128))
     mixed = lax.all_to_all(back.reshape(128, 4, 128), CHIPS, 0, 0, tiled=True)
     return output_stage(mixed.reshape(512, 128), kept, returned, w_out).reshape(8, 32, 128)

time: 73.7 us -> 72 us (0.977)
  blocking collectives: 29.7 us -> 24.9 us
  waiting for transfers between devices: 10.6 us -> 15.3 us
  local copies, waits for them, and re-layouts: 4.13 us -> 0.49 us
  Pallas kernels: 4.96 us -> 6.99 us
    all_to_all x1, blocking collectives: 25.7 us -> 20.9 us  [per_device(): swapped = lax.all_to_all(edges.reshape(64, 8, 128), LAYER, 0, 0, tiled=True)]
    ppermute x1, waiting for transfers between devices: 0.01 us -> 4.69 us  [per_device(): returned = lax.ppermute(sent, 'yh', swap)]
    unnamed x19 -> x13, local copies, waits for them, and re-layouts: 3.79 us -> 0.15 us
    all_to_all x1, starting transfers between devices: 9.02 us -> 11.5 us  [per_device(): mixed = lax.all_to_all(back.reshape(128, 4, 128), CHIPS, 0, 0, tiled=True)]
    ppermute x1, starting transfers between devices: 5.14 us -> 3.06 us  [per_device(): returned = lax.ppermute(sent, 'yh', swap)]
    pallas_call x4, Pallas kernels: 4.96 us -> 6.99 us  [call(): pl.pallas_call(kernel, out_shape=shapes if len(shapes) > 1 else shapes[0]...]
  transfers between devices with their start and end apart: 4 -> 4, of which waited for: 3 -> 4; matrix products, arithmetic and copies ran while one was open for 1% -> 1% of each run, Pallas kernels for 0% -> 0%
where the time goes in v7:
time: 72 us; the launch traced here: 71.7 us
  blocking collectives  24.9 us (35%)
  starting transfers between devices  24 us (33%)
  waiting for transfers between devices  15.3 us (21%)
  Pallas kernels  6.99 us (10%)
    all_to_all x1, blocking collectives, per_device(): swapped = lax.all_to_all(edges.reshape(64, 8, 128), LAYER, 0, 0, tiled=True)  20.9 us
    all_to_all x1, starting transfers between devices, per_device(): mixed = lax.all_to_all(back.reshape(128, 4, 128), CHIPS, 0, 0, tiled=True)  11.5 us
    pallas_call x4, Pallas kernels, call(): pl.pallas_call(kernel, out_shape=shapes if len(shapes) > 1 else shapes[0]...  6.99 us
    all_to_all x1, waiting for transfers between devices, per_device(): mixed = lax.all_to_all(back.reshape(128, 4, 128), CHIPS, 0, 0, tiled=True)  6.7 us
    ppermute x1, starting transfers between devices, per_device(): panel = lax.ppermute(right, ALL, panel_permutation())  6.27 us
    ppermute x1, waiting for transfers between devices, per_device(): returned = lax.ppermute(sent, 'yh', swap)  4.69 us
    ppermute x1, starting transfers between devices, per_device(): met = lax.ppermute(shared, 'yh', swap)  3.2 us
    ppermute x1, starting transfers between devices, per_device(): returned = lax.ppermute(sent, 'yh', swap)  3.06 us
  transfers between devices with their start and end apart: 4, of which 4 were waited for; matrix products, arithmetic and copies ran while one was open for 1% of the time, Pallas kernels for 0%

profile of v7, /device:TPU:2, one launch (start us, length us, event | category | flops | bytes accessed | tf_op | source)
XLA Modules:
  0.0 71.7 jit_solution(2916019550528534877)
XLA Ops:
  0.0 0.0 copy-start.5
  0.0 2.9 %shard_map.82 = (f32[384,128]{1,0:T(8,128)}, f32[256,128]{1,0:T(8,128)}) custom-call(f32[128,8,256]{2,1,0:T(8,128)} %msa_ref.1, f32[32,256]{1,0:T(8,128)} %bitcast.23, f32[32,256]{1,0:T(8,128)} %bitcast.24, f32[8,2,16,128]{3,2,1,0:T(8,128)} %bitcast.19), custom_call_target="tpu_custom_call" | custom-call | tf_op jit(solution)/shard_map/pallas_call | solution.py:194
  2.9 0.0 copy-start.4
  2.9 6.3 %collective-permute-start.1 = (f32[256,128]{1,0:T(8,128)}, f32[256,128]{1,0:T(8,128)S(1)}, u32[]{:S(2)}, u32[]{:S(2)}) collective-permute-start(f32[256,128]{1,0:T(8,128)} %get-tuple-element.11), channel_id=1, source_target_pairs={{3,0},{34,1},{64,2},{96,3},{128,4},{160,5},{193,6},{224,7},{11,8},... | collective-permute-start | bytes 393224 | tf_op jit(solution)/shard_map/ppermute | solution.py:234
  9.2 3.2 %collective-permute-start = (f32[384,128]{1,0:T(8,128)}, f32[384,128]{1,0:T(8,128)S(1)}, u32[]{:S(2)}, u32[]{:S(2)}) collective-permute-start(f32[384,128]{1,0:T(8,128)} %get-tuple-element.10.own_ref), channel_id=1, source_target_pairs={{0,16},{16,0},{1,17},{17,1},{2,18},{18,2},{3,19},{19,3},{4,20},{20... | collective-permute-start | bytes 589832 | tf_op jit(solution)/shard_map/ppermute | solution.py:235
  12.4 0.0 copy-done.5
  12.4 0.1 copy.12
  12.5 0.0 copy-done.4
  12.5 0.3 copy.11
  12.8 0.0 copy-start
  12.8 0.0 copy-start.1
  12.9 0.0 copy-start.2
  12.9 1.2 %collective-permute-done.1 = f32[256,128]{1,0:T(8,128)S(1)} collective-permute-done((f32[256,128]{1,0:T(8,128)}, f32[256,128]{1,0:T(8,128)S(1)}, u32[]{:S(2)}, u32[]{:S(2)}) %collective-permute-start.1) | collective-permute-done | bytes 131104 | tf_op jit(solution)/shard_map/ppermute | solution.py:234
  14.1 2.0 %all_gather.6.panel_ref = f32[512,128]{1,0:T(8,128)S(1)} all-gather(f32[256,128]{1,0:T(8,128)S(1)} %collective-permute-done.1), channel_id=1, replica_groups=mesh['z'=8,'yh'=2,'core'=2,'x'=4,'yl'=2] {'core'}, dimensions={0}, use_global_device_ids=true | all-gather | bytes 393216 | tf_op jit(solution)/shard_map/all_gather | solution.py:237
  16.0 2.7 %collective-permute-done.met_ref = f32[384,128]{1,0:T(8,128)S(1)} collective-permute-done((f32[384,128]{1,0:T(8,128)}, f32[384,128]{1,0:T(8,128)S(1)}, u32[]{:S(2)}, u32[]{:S(2)}) %collective-permute-start) | collective-permute-done | bytes 196640 | tf_op jit(solution)/shard_map/ppermute | solution.py:235
  18.7 0.0 copy-done
  18.7 0.0 copy-done.1
  18.7 0.0 copy-done.2
  18.7 1.7 %shard_map.83 = (f32[512,128]{1,0:T(8,128)S(1)}, f32[2,128,128]{2,1,0:T(8,128)S(1)}, f32[2,128,128]{2,1,0:T(8,128)S(1)}) custom-call(f32[384,128]{1,0:T(8,128)S(1)} %copy-done.1, f32[384,128]{1,0:T(8,128)S(1)} %collective-permute-done.met_ref, f32[512,128]{1,0:T(8,128)S(1)} %all_gather.6.panel_ref, f32[8,2,16,128]{3,2,1,0:T(8,128)S(1)} %bitcast.20, ...), custom_call_target="tpu_custom_call" | custom-call | tf_op jit(solution)/shard_map/pallas_call | solution.py:194
  20.5 20.9 %all_to_all.10 = f32[64,8,128]{2,1,0:T(8,128)S(1)} all-to-all(f32[64,8,128]{2,1,0:T(8,128)S(1)} %bitcast.21), channel_id=1, replica_groups=mesh['z'=8,'yh'=2,'core'=2,'x'=4,'yl'=2] {'z','x','yl'}, dimensions={0} | all-to-all | bytes 524288 | tf_op jit(solution)/shard_map/all_to_all | solution.py:239
  41.4 2.0 %all_gather.7 = f32[128,4,128]{2,1,0:T(4,128)S(1)} all-gather(f32[64,4,128]{2,1,0:T(4,128)S(1)} %slice.4), channel_id=1, replica_groups=mesh['z'=8,'yh'=2,'core'=2,'x'=4,'yl'=2] {'core'}, dimensions={0}, use_global_device_ids=true | all-gather | bytes 393216 | tf_op jit(solution)/shard_map/all_gather | solution.py:241
  43.4 1.4 %shard_map.84 = f32[512,128]{1,0:T(8,128)} custom-call(f32[512,128]{1,0:T(8,128)S(1)} %bitcast.15, f32[512,128]{1,0:T(8,128)S(1)} %bitcast.17), custom_call_target="tpu_custom_call" | custom-call | tf_op jit(solution)/shard_map/pallas_call | solution.py:194
  44.8 0.0 copy-start.3
  44.8 11.5 %all-to-all-start.1 = ((f32[128,4,128]{2,1,0:T(4,128)}), f32[128,4,128]{2,1,0:T(4,128)S(1)}, u32[]{:S(2)}, u32[]{:S(2)}) async-start(f32[128,4,128]{2,1,0:T(4,128)} %bitcast.10), calls=%async_computation.1 | async-start | bytes 524288 | tf_op jit(solution)/shard_map/all_to_all | solution.py:243
  56.3 3.1 %collective-permute-start.2 = (f32[2,128,128]{2,1,0:T(8,128)S(1)}, f32[2,128,128]{2,1,0:T(8,128)S(1)}, u32[]{:S(2)}, u32[]{:S(2)}) collective-permute-start(f32[2,128,128]{2,1,0:T(8,128)S(1)} %get-tuple-element.14), channel_id=1, source_target_pairs={{0,16},{16,0},{1,17},{17,1},{2,18},{18,2},{3,19},{19,3},{4,20},{20... | collective-permute-start | bytes 393224 | tf_op jit(solution)/shard_map/ppermute | solution.py:240
  59.4 4.7 %collective-permute-done.2.met_ref = f32[2,128,128]{2,1,0:T(8,128)S(1)} collective-permute-done((f32[2,128,128]{2,1,0:T(8,128)S(1)}, f32[2,128,128]{2,1,0:T(8,128)S(1)}, u32[]{:S(2)}, u32[]{:S(2)}) %collective-permute-start.2) | collective-permute-done | bytes 131104 | tf_op jit(solution)/shard_map/ppermute | solution.py:240
  64.0 6.7 %all-to-all-done.1 = f32[128,4,128]{2,1,0:T(4,128)S(1)} async-done(((f32[128,4,128]{2,1,0:T(4,128)}), f32[128,4,128]{2,1,0:T(4,128)S(1)}, u32[]{:S(2)}, u32[]{:S(2)}) %all-to-all-start.1) | async-done | bytes 262176 | tf_op jit(solution)/shard_map/all_to_all | solution.py:243
  70.7 0.0 copy-done.3
  70.7 1.0 %shard_map.85 = f32[8,2,16,128]{3,2,1,0:T(8,128)} custom-call(f32[512,128]{1,0:T(8,128)S(1)} %bitcast.18, f32[2,128,128]{2,1,0:T(8,128)S(1)} %get-tuple-element.13.kept_ref, f32[2,128,128]{2,1,0:T(8,128)S(1)} %collective-permute-done.2.met_ref, f32[128,128]{1,0:T(8,128)S(1)} %copy-done.3), custom_call_target="tpu_custom_call" | custom-call | tf_op jit(solution)/shard_map/pallas_call | solution.py:194
  (1 shorter events, 0.0 us)
Async XLA Ops:
  0.0 12.4 %copy-start.5 = (f32[128,512]{1,0:T(8,128)S(1)}, f32[128,512]{1,0:T(8,128)}, u32[]{:S(2)}) copy-start(f32[128,512]{1,0:T(8,128)} %param.13) | copy-start | bytes 786436
  2.9 9.6 %copy-start.4 = (f32[1024,128]{1,0:T(8,128)S(1)}, f32[1024,128]{1,0:T(8,128)}, u32[]{:S(2)}) copy-start(f32[1024,128]{1,0:T(8,128)} %param.12) | copy-start | bytes 1572868
  2.9 11.2 %collective-permute-start.1 = (f32[256,128]{1,0:T(8,128)}, f32[256,128]{1,0:T(8,128)S(1)}, u32[]{:S(2)}, u32[]{:S(2)}) collective-permute-start(f32[256,128]{1,0:T(8,128)} %get-tuple-element.11), channel_id=1, source_target_pairs={{3,0},{34,1},{64,2},{96,3},{128,4},{160,5},{193,6},{224,7},{11,8},... | collective-permute-start | bytes 393224 | tf_op jit(solution)/shard_map/ppermute | solution.py:234
  9.2 9.5 %collective-permute-start = (f32[384,128]{1,0:T(8,128)}, f32[384,128]{1,0:T(8,128)S(1)}, u32[]{:S(2)}, u32[]{:S(2)}) collective-permute-start(f32[384,128]{1,0:T(8,128)} %get-tuple-element.10.own_ref), channel_id=1, source_target_pairs={{0,16},{16,0},{1,17},{17,1},{2,18},{18,2},{3,19},{19,3},{4,20},{20... | collective-permute-start | bytes 589832 | tf_op jit(solution)/shard_map/ppermute | solution.py:235
  12.8 5.9 %copy-start = (f32[8,32,128]{2,1,0:T(8,128)S(1)}, f32[8,32,128]{2,1,0:T(8,128)}, u32[]{:S(2)}) copy-start(f32[8,32,128]{2,1,0:T(8,128)} %param.9) | copy-start | bytes 393220
  12.8 5.9 %copy-start.1 = (f32[384,128]{1,0:T(8,128)S(1)}, f32[384,128]{1,0:T(8,128)}, u32[]{:S(2)}) copy-start(f32[384,128]{1,0:T(8,128)} %get-tuple-element.10.own_ref) | copy-start | bytes 589828
  12.9 5.9 %copy-start.2 = (f32[128,128]{1,0:T(8,128)S(1)}, f32[128,128]{1,0:T(8,128)}, u32[]{:S(2)}) copy-start(f32[128,128]{1,0:T(8,128)} %w_gate_ref.1) | copy-start | bytes 196612
  44.8 26.0 %copy-start.3 = (f32[128,128]{1,0:T(8,128)S(1)}, f32[128,128]{1,0:T(8,128)}, u32[]{:S(2)}) copy-start(f32[128,128]{1,0:T(8,128)} %w_ref.1) | copy-start | bytes 196612
  44.8 25.9 %all-to-all-start.1 = ((f32[128,4,128]{2,1,0:T(4,128)}), f32[128,4,128]{2,1,0:T(4,128)S(1)}, u32[]{:S(2)}, u32[]{:S(2)}) async-start(f32[128,4,128]{2,1,0:T(4,128)} %bitcast.10), calls=%async_computation.1 | async-start | bytes 524288 | tf_op jit(solution)/shard_map/all_to_all | solution.py:243
  56.3 7.7 %collective-permute-start.2 = (f32[2,128,128]{2,1,0:T(8,128)S(1)}, f32[2,128,128]{2,1,0:T(8,128)S(1)}, u32[]{:S(2)}, u32[]{:S(2)}) collective-permute-start(f32[2,128,128]{2,1,0:T(8,128)S(1)} %get-tuple-element.14), channel_id=1, source_target_pairs={{0,16},{16,0},{1,17},{17,1},{2,18},{18,2},{3,19},{19,3},{4,20},{20... | collective-permute-start | bytes 393224 | tf_op jit(solution)/shard_map/ppermute | solution.py:240

commit v8 on v7

--- a/solution.py
+++ b/solution.py
@@ -16,8 +16,8 @@
 
 
 PANEL_COLUMNS = (
-    (34570126, 24563107, 1675324, 1674523, 1236754, 1234675, 12467530, 1376452),
-    (34560127, 45673102, 1675423, 1674253, 1237654, 2643175, 12467530, 1376542),
+    (72361054, 54671032, 53160427, 1764253, 74562031, 25647103, 76045231, 5476312),
+    (61053247, 45671032, 30176425, 62347501, 34205176, 50761342, 42635701, 4276513),
 )
 
 
@@ -93,12 +93,17 @@
 
 
 def pair_kernel(
-    own_ref, met_ref, panel_ref, pair_ref, w_outer_ref, w_tri_ref, w_gate_ref,
+    own_ref, met_ref, panel_ref, sibling_ref, pair_ref, w_outer_ref, w_tri_ref, w_gate_ref,
     edges_ref, kept_ref, sent_ref, outer_ref, flat_ref,
 ):
     yh = lax.axis_index("yh")
     left = jnp.concatenate([own_ref[pl.ds(0, 256), :], met_ref[pl.ds(0, 256), :]], 0)
-    outer_ref[...] = dot_t(panel_ref[...], left)
+    first = lax.axis_index("core") == 0
+    panel, sibling = panel_ref[...], sibling_ref[...]
+    panels = jnp.concatenate(
+        [jnp.where(first, panel, sibling), jnp.where(first, sibling, panel)], 0
+    )
+    outer_ref[...] = dot_t(panels, left)
     lane = lax.broadcasted_iota(jnp.int32, (8, 128), 1)
     low_half = lane < 64
     even = (lane // 32) % 2 == 0
@@ -148,6 +153,7 @@
 
 
 def triangle_kernel(left_ref, right_ref, out_ref, l_ref, r_ref):
+    core = lax.axis_index("core")
     lane = lax.broadcasted_iota(jnp.int32, (8, 128), 1)
     masks = [(lane // 16) & bit != 0 for bit in (1, 2, 4)]
     for h in range(2):
@@ -155,10 +161,13 @@
             for y in range(2):
                 x = left_ref[pl.ds(z * 64 + h * 2 + y, 8, stride=8), :]
                 l_ref[pl.ds(y * 64 + z * 8, 8), :] = turn_blocks(x, masks)
-                for o in range(2):
-                    x = right_ref[pl.ds(o * 256 + z * 32 + h * 2 + y, 8, stride=4), :]
-                    row = y * 128 + turned_rows(z) * 16 + o * 8
-                    r_ref[pl.ds(row, 8), :] = turn_blocks(x, masks)
+                x = left_ref[pl.ds(z * 64 + (2 + h) * 2 + y, 8, stride=8), :]
+                own = turn_blocks(x, masks)
+                x = right_ref[pl.ds(z * 32 + h * 2 + y, 8, stride=4), :]
+                other = turn_blocks(x, masks)
+                row = y * 128 + turned_rows(z) * 16
+                r_ref[pl.ds(row, 8), :] = jnp.where(core == 0, own, other)
+                r_ref[pl.ds(row + 8, 8), :] = jnp.where(core == 0, other, own)
         mixed = dot_t(l_ref[...], r_ref[...])
         for z in range(8):
             for y in range(2):
@@ -210,12 +219,12 @@
     )
 
 
-def pair_stage(own, met, panel, pair, w_outer, w_tri, w_gate):
+def pair_stage(own, met, panel, sibling, pair, w_outer, w_tri, w_gate):
     return call(
         pair_kernel,
         [(512, 128), (2, 128, 128), (2, 128, 128)],
         [vmem(512, 512), vmem(256, 1024)],
-        own, met, panel, pair, w_outer, w_tri, w_gate,
+        own, met, panel, sibling, pair, w_outer, w_tri, w_gate,
     )
 
 
@@ -234,12 +243,12 @@
     panel = lax.ppermute(right, ALL, panel_permutation())
     met = lax.ppermute(shared, "yh", swap)
     w_outer_ba = w_outer.reshape(32, 32, 128).transpose(1, 0, 2).reshape(1024, 128)
-    panel = lax.all_gather(panel, "core", axis=0, tiled=True)
-    edges, kept, sent = pair_stage(shared, met, panel, pair, w_outer_ba, w_tri.T, w_gate)
+    sibling = lax.ppermute(panel, "core", swap)
+    edges, kept, sent = pair_stage(shared, met, panel, sibling, pair, w_outer_ba, w_tri.T, w_gate)
     swapped = lax.all_to_all(edges.reshape(64, 8, 128), LAYER, 0, 0, tiled=True)
     returned = lax.ppermute(sent, "yh", swap)
-    rights = lax.all_gather(swapped[:, 4:], "core", axis=0, tiled=True)
-    back = triangle(swapped.reshape(512, 128), rights.reshape(512, 128))
+    rights = lax.ppermute(swapped[:, 4:], "core", swap)
+    back = triangle(swapped.reshape(512, 128), rights.reshape(256, 128))
     mixed = lax.all_to_all(back.reshape(128, 4, 128), CHIPS, 0, 0, tiled=True)
     return output_stage(mixed.reshape(512, 128), kept, returned, w_out).reshape(8, 32, 128)
 

time: 72 us -> 69.2 us (0.961)
  blocking collectives: 24.9 us -> 20 us
  waiting for transfers between devices: 15.3 us -> 19.5 us
  starting transfers between devices: 24 us -> 21.8 us
    ppermute x1, starting transfers between devices: 3.2 us -> 8.02 us  [per_device(): met = lax.ppermute(shared, 'yh', swap)]
    ppermute x1, starting transfers between devices: 6.27 us -> 1.89 us  [per_device(): panel = lax.ppermute(right, ALL, panel_permutation())]
    ppermute x1, waiting for transfers between devices: 2.66 us -> 6.8 us  [per_device(): met = lax.ppermute(shared, 'yh', swap)]
    all_gather x2 -> x0, blocking collectives: 3.98 us -> none  [the longest x1 1.99 us: per_device(): rights = lax.all_gather(swapped[:, 4:], 'core', axis=0, tiled=True)]
    all_to_all x1, starting transfers between devices: 11.5 us -> 8.75 us  [per_device(): mixed = lax.all_to_all(back.reshape(128, 4, 128), CHIPS, 0, 0, tiled=True)]
    ppermute x0 -> x2, waiting for transfers between devices: none -> 1.34 us  [the longest x1 1.33 us: per_device(): rights = lax.ppermute(swapped[:, 4:], 'core', swap)]
    ppermute x1, waiting for transfers between devices: 1.2 us -> 0.01 us  [per_device(): panel = lax.ppermute(right, ALL, panel_permutation())]
    all_to_all x1, blocking collectives: 20.9 us -> 20 us  [per_device(): swapped = lax.all_to_all(edges.reshape(64, 8, 128), LAYER, 0, 0, tiled=True)]
  transfers between devices with their start and end apart: 4 -> 6, of which waited for: 4 -> 4; matrix products, arithmetic and copies ran while one was open for 1% -> 1% of each run, Pallas kernels for 0% -> 0%
where the time goes in v8:
time: 69.2 us; the launch traced here: 69 us
  starting transfers between devices  21.8 us (32%)
  blocking collectives  20 us (29%)
  waiting for transfers between devices  19.5 us (28%)
  Pallas kernels  6.99 us (10%)
    all_to_all x1, blocking collectives, per_device(): swapped = lax.all_to_all(edges.reshape(64, 8, 128), LAYER, 0, 0, tiled=True)  20 us
    all_to_all x1, starting transfers between devices, per_device(): mixed = lax.all_to_all(back.reshape(128, 4, 128), CHIPS, 0, 0, tiled=True)  8.75 us
    ppermute x1, starting transfers between devices, per_device(): met = lax.ppermute(shared, 'yh', swap)  8.02 us
    pallas_call x4, Pallas kernels, call(): pl.pallas_call(kernel, out_shape=shapes if len(shapes) > 1 else shapes[0]...  6.99 us
    ppermute x1, waiting for transfers between devices, per_device(): met = lax.ppermute(shared, 'yh', swap)  6.8 us
    all_to_all x1, waiting for transfers between devices, per_device(): mixed = lax.all_to_all(back.reshape(128, 4, 128), CHIPS, 0, 0, tiled=True)  6.7 us
    ppermute x1, waiting for transfers between devices, per_device(): returned = lax.ppermute(sent, 'yh', swap)  4.69 us
    ppermute x1, starting transfers between devices, per_device(): returned = lax.ppermute(sent, 'yh', swap)  3.06 us
  transfers between devices with their start and end apart: 6, of which 4 were waited for; matrix products, arithmetic and copies ran while one was open for 1% of the time, Pallas kernels for 0%

profile of v8, /device:TPU:2, one launch (start us, length us, event | category | flops | bytes accessed | tf_op | source)
XLA Modules:
  0.0 69.0 jit_solution(10976970885067896131)
XLA Ops:
  0.0 0.0 copy-start.5
  0.0 2.9 %shard_map.82 = (f32[384,128]{1,0:T(8,128)}, f32[256,128]{1,0:T(8,128)}) custom-call(f32[128,8,256]{2,1,0:T(8,128)} %msa_ref.1, f32[32,256]{1,0:T(8,128)} %bitcast.23, f32[32,256]{1,0:T(8,128)} %bitcast.24, f32[8,2,16,128]{3,2,1,0:T(8,128)} %bitcast.18), custom_call_target="tpu_custom_call" | custom-call | tf_op jit(solution)/shard_map/pallas_call | solution.py:203
  2.9 0.0 copy-start.4
  2.9 1.9 %collective-permute-start.1 = (f32[256,128]{1,0:T(8,128)}, f32[256,128]{1,0:T(8,128)S(1)}, u32[]{:S(2)}, u32[]{:S(2)}) collective-permute-start(f32[256,128]{1,0:T(8,128)} %get-tuple-element.11), channel_id=1, source_target_pairs={{7,0},{37,1},{69,2},{96,3},{135,4},{162,5},{199,6},{224,7},{15,8},... | collective-permute-start | bytes 393224 | tf_op jit(solution)/shard_map/ppermute | solution.py:243
  4.8 8.0 %collective-permute-start = (f32[384,128]{1,0:T(8,128)}, f32[384,128]{1,0:T(8,128)S(1)}, u32[]{:S(2)}, u32[]{:S(2)}) collective-permute-start(f32[384,128]{1,0:T(8,128)} %get-tuple-element.10.own_ref), channel_id=1, source_target_pairs={{0,16},{16,0},{1,17},{17,1},{2,18},{18,2},{3,19},{19,3},{4,20},{20... | collective-permute-start | bytes 589832 | tf_op jit(solution)/shard_map/ppermute | solution.py:244
  12.8 0.0 collective-permute-done.1.panel_ref
  12.8 0.0 collective-permute-start.2
  12.8 0.0 copy-done.5
  12.8 0.1 copy.10
  13.0 0.0 copy-done.4
  13.0 0.0 copy-start
  13.0 0.0 copy-start.1
  13.0 0.0 copy-start.2
  13.0 0.3 copy.9
  13.3 6.8 %collective-permute-done.met_ref = f32[384,128]{1,0:T(8,128)S(1)} collective-permute-done((f32[384,128]{1,0:T(8,128)}, f32[384,128]{1,0:T(8,128)S(1)}, u32[]{:S(2)}, u32[]{:S(2)}) %collective-permute-start) | collective-permute-done | bytes 196640 | tf_op jit(solution)/shard_map/ppermute | solution.py:244
  20.1 0.0 collective-permute-done.2.sibling_ref
  20.1 0.0 copy-done
  20.1 0.0 copy-done.1
  20.1 0.0 copy-done.2
  20.1 1.7 %shard_map.83 = (f32[512,128]{1,0:T(8,128)S(1)}, f32[2,128,128]{2,1,0:T(8,128)S(1)}, f32[2,128,128]{2,1,0:T(8,128)S(1)}) custom-call(f32[384,128]{1,0:T(8,128)S(1)} %copy-done.1, f32[384,128]{1,0:T(8,128)S(1)} %collective-permute-done.met_ref, f32[256,128]{1,0:T(8,128)S(1)} %collective-permute-done.1.panel_ref, ...), custom_call_target="tpu_custom_call" | custom-call | tf_op jit(solution)/shard_map/pallas_call | solution.py:203
  21.9 20.0 %all_to_all.10 = f32[64,8,128]{2,1,0:T(8,128)S(1)} all-to-all(f32[64,8,128]{2,1,0:T(8,128)S(1)} %bitcast.20), channel_id=1, replica_groups=mesh['z'=8,'yh'=2,'core'=2,'x'=4,'yl'=2] {'z','x','yl'}, dimensions={0} | all-to-all | bytes 524288 | tf_op jit(solution)/shard_map/all_to_all | solution.py:248
  42.0 0.1 collective-permute-start.3
  42.1 1.3 %collective-permute-done.3 = f32[64,4,128]{2,1,0:T(4,128)S(1)} collective-permute-done((f32[64,4,128]{2,1,0:T(4,128)S(1)}, f32[64,4,128]{2,1,0:T(4,128)S(1)}, u32[]{:S(2)}, u32[]{:S(2)}) %collective-permute-start.3) | collective-permute-done | bytes 131104 | tf_op jit(solution)/shard_map/ppermute | solution.py:250
  43.4 1.4 %shard_map.84 = f32[512,128]{1,0:T(8,128)} custom-call(f32[512,128]{1,0:T(8,128)S(1)} %bitcast.15, f32[256,128]{1,0:T(8,128)S(1)} %bitcast.21), custom_call_target="tpu_custom_call" | custom-call | tf_op jit(solution)/shard_map/pallas_call | solution.py:203
  44.8 0.0 copy-start.3
  44.8 8.8 %all-to-all-start.1 = ((f32[128,4,128]{2,1,0:T(4,128)}), f32[128,4,128]{2,1,0:T(4,128)S(1)}, u32[]{:S(2)}, u32[]{:S(2)}) async-start(f32[128,4,128]{2,1,0:T(4,128)} %bitcast.10), calls=%async_computation.1 | async-start | bytes 524288 | tf_op jit(solution)/shard_map/all_to_all | solution.py:252
  53.5 3.1 %collective-permute-start.4 = (f32[2,128,128]{2,1,0:T(8,128)S(1)}, f32[2,128,128]{2,1,0:T(8,128)S(1)}, u32[]{:S(2)}, u32[]{:S(2)}) collective-permute-start(f32[2,128,128]{2,1,0:T(8,128)S(1)} %get-tuple-element.14), channel_id=1, source_target_pairs={{0,16},{16,0},{1,17},{17,1},{2,18},{18,2},{3,19},{19,3},{4,20},{20... | collective-permute-start | bytes 393224 | tf_op jit(solution)/shard_map/ppermute | solution.py:249
  56.6 4.7 %collective-permute-done.4.met_ref = f32[2,128,128]{2,1,0:T(8,128)S(1)} collective-permute-done((f32[2,128,128]{2,1,0:T(8,128)S(1)}, f32[2,128,128]{2,1,0:T(8,128)S(1)}, u32[]{:S(2)}, u32[]{:S(2)}) %collective-permute-start.4) | collective-permute-done | bytes 131104 | tf_op jit(solution)/shard_map/ppermute | solution.py:249
  61.3 6.7 %all-to-all-done.1 = f32[128,4,128]{2,1,0:T(4,128)S(1)} async-done(((f32[128,4,128]{2,1,0:T(4,128)}), f32[128,4,128]{2,1,0:T(4,128)S(1)}, u32[]{:S(2)}, u32[]{:S(2)}) %all-to-all-start.1) | async-done | bytes 262176 | tf_op jit(solution)/shard_map/all_to_all | solution.py:252
  68.0 0.0 copy-done.3
  68.0 1.0 %shard_map.85 = f32[8,2,16,128]{3,2,1,0:T(8,128)} custom-call(f32[512,128]{1,0:T(8,128)S(1)} %bitcast.17, f32[2,128,128]{2,1,0:T(8,128)S(1)} %get-tuple-element.13.kept_ref, f32[2,128,128]{2,1,0:T(8,128)S(1)} %collective-permute-done.4.met_ref, f32[128,128]{1,0:T(8,128)S(1)} %copy-done.3), custom_call_target="tpu_custom_call" | custom-call | tf_op jit(solution)/shard_map/pallas_call | solution.py:203
  (1 shorter events, 0.0 us)
Async XLA Ops:
  0.0 12.8 %copy-start.5 = (f32[128,512]{1,0:T(8,128)S(1)}, f32[128,512]{1,0:T(8,128)}, u32[]{:S(2)}) copy-start(f32[128,512]{1,0:T(8,128)} %param.13) | copy-start | bytes 786436
  2.9 10.1 %copy-start.4 = (f32[1024,128]{1,0:T(8,128)S(1)}, f32[1024,128]{1,0:T(8,128)}, u32[]{:S(2)}) copy-start(f32[1024,128]{1,0:T(8,128)} %param.12) | copy-start | bytes 1572868
  2.9 9.9 %collective-permute-start.1 = (f32[256,128]{1,0:T(8,128)}, f32[256,128]{1,0:T(8,128)S(1)}, u32[]{:S(2)}, u32[]{:S(2)}) collective-permute-start(f32[256,128]{1,0:T(8,128)} %get-tuple-element.11), channel_id=1, source_target_pairs={{7,0},{37,1},{69,2},{96,3},{135,4},{162,5},{199,6},{224,7},{15,8},... | collective-permute-start | bytes 393224 | tf_op jit(solution)/shard_map/ppermute | solution.py:243
  4.8 15.3 %collective-permute-start = (f32[384,128]{1,0:T(8,128)}, f32[384,128]{1,0:T(8,128)S(1)}, u32[]{:S(2)}, u32[]{:S(2)}) collective-permute-start(f32[384,128]{1,0:T(8,128)} %get-tuple-element.10.own_ref), channel_id=1, source_target_pairs={{0,16},{16,0},{1,17},{17,1},{2,18},{18,2},{3,19},{19,3},{4,20},{20... | collective-permute-start | bytes 589832 | tf_op jit(solution)/shard_map/ppermute | solution.py:244
  12.8 7.3 %collective-permute-start.2 = (f32[256,128]{1,0:T(8,128)S(1)}, f32[256,128]{1,0:T(8,128)S(1)}, u32[]{:S(2)}, u32[]{:S(2)}) collective-permute-start(f32[256,128]{1,0:T(8,128)S(1)} %collective-permute-done.1.panel_ref), channel_id=1, source_target_pairs={{0,8},{8,0},{1,9},{9,1},{2,10},{10,2},{3,11},{11,3},{4,12},{12,4},... | collective-permute-start | bytes 393224 | tf_op jit(solution)/shard_map/ppermute | solution.py:246
  13.0 7.2 %copy-start = (f32[8,32,128]{2,1,0:T(8,128)S(1)}, f32[8,32,128]{2,1,0:T(8,128)}, u32[]{:S(2)}) copy-start(f32[8,32,128]{2,1,0:T(8,128)} %param.9) | copy-start | bytes 393220
  13.0 7.1 %copy-start.1 = (f32[384,128]{1,0:T(8,128)S(1)}, f32[384,128]{1,0:T(8,128)}, u32[]{:S(2)}) copy-start(f32[384,128]{1,0:T(8,128)} %get-tuple-element.10.own_ref) | copy-start | bytes 589828
  13.0 7.1 %copy-start.2 = (f32[128,128]{1,0:T(8,128)S(1)}, f32[128,128]{1,0:T(8,128)}, u32[]{:S(2)}) copy-start(f32[128,128]{1,0:T(8,128)} %w_gate_ref.1) | copy-start | bytes 196612
  42.0 1.4 %collective-permute-start.3 = (f32[64,4,128]{2,1,0:T(4,128)S(1)}, f32[64,4,128]{2,1,0:T(4,128)S(1)}, u32[]{:S(2)}, u32[]{:S(2)}) collective-permute-start(f32[64,4,128]{2,1,0:T(4,128)S(1)} %slice.4), channel_id=1, source_target_pairs={{0,8},{8,0},{1,9},{9,1},{2,10},{10,2},{3,11},{11,3},{4,12},{12,4},... | collective-permute-start | bytes 393224 | tf_op jit(solution)/shard_map/ppermute | solution.py:250
  44.8 23.2 %copy-start.3 = (f32[128,128]{1,0:T(8,128)S(1)}, f32[128,128]{1,0:T(8,128)}, u32[]{:S(2)}) copy-start(f32[128,128]{1,0:T(8,128)} %w_ref.1) | copy-start | bytes 196612
  44.8 23.2 %all-to-all-start.1 = ((f32[128,4,128]{2,1,0:T(4,128)}), f32[128,4,128]{2,1,0:T(4,128)S(1)}, u32[]{:S(2)}, u32[]{:S(2)}) async-start(f32[128,4,128]{2,1,0:T(4,128)} %bitcast.10), calls=%async_computation.1 | async-start | bytes 524288 | tf_op jit(solution)/shard_map/all_to_all | solution.py:252
  53.5 7.7 %collective-permute-start.4 = (f32[2,128,128]{2,1,0:T(8,128)S(1)}, f32[2,128,128]{2,1,0:T(8,128)S(1)}, u32[]{:S(2)}, u32[]{:S(2)}) collective-permute-start(f32[2,128,128]{2,1,0:T(8,128)S(1)} %get-tuple-element.14), channel_id=1, source_target_pairs={{0,16},{16,0},{1,17},{17,1},{2,18},{18,2},{3,19},{19,3},{4,20},{20... | collective-permute-start | bytes 393224 | tf_op jit(solution)/shard_map/ppermute | solution.py:249

commit v9 on v8

--- a/solution.py
+++ b/solution.py
@@ -75,7 +75,9 @@
     return (8 - p) % 8
 
 
-def factor_kernel(msa_ref, first_ref, second_ref, pair_ref, shared_ref, right_ref, result):
+def factor_kernel(
+    msa_ref, first_ref, second_ref, pair_ref, left_ref, right_ref, half_ref, result
+):
     other = 1 - lax.axis_index("yh")
     w_high, w_low = split(jnp.concatenate([first_ref[...], second_ref[...]], 0))
     w_both = jnp.concatenate([w_high, w_low], 0)
@@ -86,18 +88,18 @@
     for i in range(8):
         turned = result[pl.ds(i, 128, stride=8), :].T
         both = turned[:64] + turned[64:]
-        shared_ref[pl.ds(i * 32, 32), :] = both[:32] * (1.0 / 128.0)
+        left_ref[pl.ds(i * 32, 32), :] = both[:32] * (1.0 / 128.0)
         right_ref[pl.ds(i, 32, stride=8), :] = both[32:]
     for p in range(8):
-        shared_ref[pl.ds(256 + p * 16, 16), :] = pair_ref[turned_rows(p), other]
+        half_ref[pl.ds(p * 16, 16), :] = pair_ref[turned_rows(p), other]
 
 
 def pair_kernel(
-    own_ref, met_ref, panel_ref, sibling_ref, pair_ref, w_outer_ref, w_tri_ref, w_gate_ref,
+    own_ref, met_ref, met_pair_ref, panel_ref, sibling_ref, pair_ref, w_outer_ref, w_tri_ref, w_gate_ref,
     edges_ref, kept_ref, sent_ref, outer_ref, flat_ref,
 ):
     yh = lax.axis_index("yh")
-    left = jnp.concatenate([own_ref[pl.ds(0, 256), :], met_ref[pl.ds(0, 256), :]], 0)
+    left = jnp.concatenate([own_ref[...], met_ref[...]], 0)
     first = lax.axis_index("core") == 0
     panel, sibling = panel_ref[...], sibling_ref[...]
     panels = jnp.concatenate(
@@ -127,7 +129,7 @@
                     row = ih // 2 * 128 + turned_rows(i) * 16 + o * 8
                     flat_ref[pl.ds(row, 8), pl.ds(bh * 128, 128)] = v[il]
     pair = jnp.concatenate(
-        [pair_ref[turned_rows(p), yh] for p in range(8)] + [met_ref[pl.ds(256, 128), :]], 0
+        [pair_ref[turned_rows(p), yh] for p in range(8)] + [met_pair_ref[...]], 0
     )
     mid = pair + dot_deep(flat_ref[...], w_outer_ref[...])
     normed = layer_norm(mid, -1)
@@ -214,17 +216,18 @@
 
 def factors(homolog, first, second, pair):
     return call(
-        factor_kernel, [(384, 128), (256, 128)], [vmem(1024, 128)], homolog, first, second, pair,
+        factor_kernel, [(256, 128), (256, 128), (128, 128)], [vmem(1024, 128)],
+        homolog, first, second, pair,
         limit=60 * 1024 * 1024,
     )
 
 
-def pair_stage(own, met, panel, sibling, pair, w_outer, w_tri, w_gate):
+def pair_stage(own, met, met_pair, panel, sibling, pair, w_outer, w_tri, w_gate):
     return call(
         pair_kernel,
         [(512, 128), (2, 128, 128), (2, 128, 128)],
         [vmem(512, 512), vmem(256, 1024)],
-        own, met, panel, sibling, pair, w_outer, w_tri, w_gate,
+        own, met, met_pair, panel, sibling, pair, w_outer, w_tri, w_gate,
     )
 
 
@@ -238,13 +241,16 @@
 
 def per_device(homolog, pair, w_first, w_second, w_outer, w_tri, w_gate, w_out):
     pair = pair.reshape(8, 2, 16, 128)
-    shared, right = factors(homolog, w_first.T, w_second.T, pair)
+    left, right, half = factors(homolog, w_first.T, w_second.T, pair)
     swap = [(0, 1), (1, 0)]
     panel = lax.ppermute(right, ALL, panel_permutation())
-    met = lax.ppermute(shared, "yh", swap)
+    met = lax.ppermute(left, ("yh", "yl"), [(0, 3), (1, 2), (2, 1), (3, 0)])
+    met_pair = lax.ppermute(half, "yh", swap)
     w_outer_ba = w_outer.reshape(32, 32, 128).transpose(1, 0, 2).reshape(1024, 128)
     sibling = lax.ppermute(panel, "core", swap)
-    edges, kept, sent = pair_stage(shared, met, panel, sibling, pair, w_outer_ba, w_tri.T, w_gate)
+    edges, kept, sent = pair_stage(
+        left, met, met_pair, panel, sibling, pair, w_outer_ba, w_tri.T, w_gate
+    )
     swapped = lax.all_to_all(edges.reshape(64, 8, 128), LAYER, 0, 0, tiled=True)
     returned = lax.ppermute(sent, "yh", swap)
     rights = lax.ppermute(swapped[:, 4:], "core", swap)

time: 69.2 us -> 73.2 us (1.058)
  starting transfers between devices: 21.8 us -> 27.4 us
  waiting for transfers between devices: 19.5 us -> 15.2 us
  blocking collectives: 20 us -> 22.8 us
    ppermute x1 -> x2, starting transfers between devices: 8.02 us -> 13.9 us  [the longest x1 8.47 us: per_device(): met = lax.ppermute(left, ('yh', 'yl'), [(0, 3), (1, 2), (2, 1), (3, 0)])]
    ppermute x1 -> x2, waiting for transfers between devices: 6.8 us -> 2.48 us  [the longest x1 2.48 us: per_device(): met_pair = lax.ppermute(half, 'yh', swap)]
    all_to_all x1, blocking collectives: 20 us -> 22.8 us  [per_device(): swapped = lax.all_to_all(edges.reshape(64, 8, 128), LAYER, 0, 0, tiled=True)]
  transfers between devices with their start and end apart: 6 -> 7, of which waited for: 4 -> 4; matrix products, arithmetic and copies ran while one was open for 1% -> 1% of each run, Pallas kernels for 0% -> 0%
where the time goes in v9:
time: 73.2 us; the launch traced here: 73 us
  starting transfers between devices  27.4 us (37%)
  blocking collectives  22.8 us (31%)
  waiting for transfers between devices  15.2 us (21%)
  Pallas kernels  6.97 us (10%)
    all_to_all x1, blocking collectives, per_device(): swapped = lax.all_to_all(edges.reshape(64, 8, 128), LAYER, 0, 0, tiled=True)  22.8 us
    all_to_all x1, starting transfers between devices, per_device(): mixed = lax.all_to_all(back.reshape(128, 4, 128), CHIPS, 0, 0, tiled=True)  8.48 us
    ppermute x1, starting transfers between devices, per_device(): met = lax.ppermute(left, ('yh', 'yl'), [(0, 3), (1, 2), (2, 1), (3, 0)])  8.47 us
    pallas_call x4, Pallas kernels, call(): pl.pallas_call(kernel, out_shape=shapes if len(shapes) > 1 else shapes[0]...  6.97 us
    all_to_all x1, waiting for transfers between devices, per_device(): mixed = lax.all_to_all(back.reshape(128, 4, 128), CHIPS, 0, 0, tiled=True)  6.7 us
    ppermute x1, starting transfers between devices, per_device(): met_pair = lax.ppermute(half, 'yh', swap)  5.43 us
    ppermute x1, waiting for transfers between devices, per_device(): returned = lax.ppermute(sent, 'yh', swap)  4.69 us
    ppermute x1, starting transfers between devices, per_device(): returned = lax.ppermute(sent, 'yh', swap)  3.06 us
  transfers between devices with their start and end apart: 7, of which 4 were waited for; matrix products, arithmetic and copies ran while one was open for 1% of the time, Pallas kernels for 0%

profile of v9, /device:TPU:2, one launch (start us, length us, event | category | flops | bytes accessed | tf_op | source)
XLA Modules:
  0.0 73.0 jit_solution(3980351969753697091)
XLA Ops:
  0.0 0.0 copy-start.5
  0.0 2.9 %shard_map.82 = (f32[256,128]{1,0:T(8,128)}, f32[256,128]{1,0:T(8,128)}, f32[128,128]{1,0:T(8,128)}) custom-call(f32[128,8,256]{2,1,0:T(8,128)} %msa_ref.1, f32[32,256]{1,0:T(8,128)} %bitcast.23, f32[32,256]{1,0:T(8,128)} %bitcast.24, f32[8,2,16,128]{3,2,1,0:T(8,128)} %bitcast.18), custom_call_target="tpu_custom_call" | custom-call | tf_op jit(solution)/shard_map/pallas_call | solution.py:205
  2.9 0.0 copy-start.4
  2.9 1.9 %collective-permute-start.2 = (f32[256,128]{1,0:T(8,128)}, f32[256,128]{1,0:T(8,128)S(1)}, u32[]{:S(2)}, u32[]{:S(2)}) collective-permute-start(f32[256,128]{1,0:T(8,128)} %get-tuple-element.13), channel_id=1, source_target_pairs={{7,0},{37,1},{69,2},{96,3},{135,4},{162,5},{199,6},{224,7},{15,8},... | collective-permute-start | bytes 393224 | tf_op jit(solution)/shard_map/ppermute | solution.py:246
  4.8 8.5 %collective-permute-start = (f32[256,128]{1,0:T(8,128)}, f32[256,128]{1,0:T(8,128)S(1)}, u32[]{:S(2)}, u32[]{:S(2)}) collective-permute-start(f32[256,128]{1,0:T(8,128)} %get-tuple-element.11.own_ref), channel_id=1, source_target_pairs={{0,17},{1,16},{16,1},{17,0},{2,19},{3,18},{18,3},{19,2},{4,21},{5,... | collective-permute-start | bytes 393224 | tf_op jit(solution)/shard_map/ppermute | solution.py:247
  13.2 0.0 collective-permute-done.2.panel_ref
  13.3 0.0 collective-permute-start.3
  13.3 5.4 %collective-permute-start.1 = (f32[128,128]{1,0:T(8,128)}, f32[128,128]{1,0:T(8,128)S(1)}, u32[]{:S(2)}, u32[]{:S(2)}) collective-permute-start(f32[128,128]{1,0:T(8,128)} %get-tuple-element.12), channel_id=1, source_target_pairs={{0,16},{16,0},{1,17},{17,1},{2,18},{18,2},{3,19},{19,3},{4,20},{20... | collective-permute-start | bytes 196616 | tf_op jit(solution)/shard_map/ppermute | solution.py:248
  18.7 0.0 copy-done.5
  18.7 0.1 copy.10
  18.8 0.0 copy-done.4
  18.8 0.0 copy-start
  18.8 0.0 copy-start.1
  18.9 0.0 copy-start.2
  18.9 0.3 copy.9
  19.2 2.5 %collective-permute-done.1.met_pair_ref = f32[128,128]{1,0:T(8,128)S(1)} collective-permute-done((f32[128,128]{1,0:T(8,128)}, f32[128,128]{1,0:T(8,128)S(1)}, u32[]{:S(2)}, u32[]{:S(2)}) %collective-permute-start.1) | collective-permute-done | bytes 65568 | tf_op jit(solution)/shard_map/ppermute | solution.py:248
  21.7 0.0 collective-permute-done.met_ref
  21.7 0.0 collective-permute-done.3.sibling_ref
  21.7 0.0 copy-done
  21.7 0.0 copy-done.1
  21.7 0.0 copy-done.2
  21.7 1.7 %shard_map.83 = (f32[512,128]{1,0:T(8,128)S(1)}, f32[2,128,128]{2,1,0:T(8,128)S(1)}, f32[2,128,128]{2,1,0:T(8,128)S(1)}) custom-call(f32[256,128]{1,0:T(8,128)S(1)} %copy-done.1, f32[256,128]{1,0:T(8,128)S(1)} %collective-permute-done.met_ref, f32[128,128]{1,0:T(8,128)S(1)} %collective-permute-done.1.met_pair_ref, ...), custom_call_target="tpu_custom_call" | custom-call | tf_op jit(solution)/shard_map/pallas_call | solution.py:205
  23.4 22.8 %all_to_all.10 = f32[64,8,128]{2,1,0:T(8,128)S(1)} all-to-all(f32[64,8,128]{2,1,0:T(8,128)S(1)} %bitcast.20), channel_id=1, replica_groups=mesh['z'=8,'yh'=2,'core'=2,'x'=4,'yl'=2] {'z','x','yl'}, dimensions={0} | all-to-all | bytes 524288 | tf_op jit(solution)/shard_map/all_to_all | solution.py:254
  46.3 0.1 collective-permute-start.4
  46.4 1.3 %collective-permute-done.4 = f32[64,4,128]{2,1,0:T(4,128)S(1)} collective-permute-done((f32[64,4,128]{2,1,0:T(4,128)S(1)}, f32[64,4,128]{2,1,0:T(4,128)S(1)}, u32[]{:S(2)}, u32[]{:S(2)}) %collective-permute-start.4) | collective-permute-done | bytes 131104 | tf_op jit(solution)/shard_map/ppermute | solution.py:256
  47.7 1.4 %shard_map.84 = f32[512,128]{1,0:T(8,128)} custom-call(f32[512,128]{1,0:T(8,128)S(1)} %bitcast.15, f32[256,128]{1,0:T(8,128)S(1)} %bitcast.21), custom_call_target="tpu_custom_call" | custom-call | tf_op jit(solution)/shard_map/pallas_call | solution.py:205
  49.1 8.5 %all-to-all-start.1 = ((f32[128,4,128]{2,1,0:T(4,128)}), f32[128,4,128]{2,1,0:T(4,128)S(1)}, u32[]{:S(2)}, u32[]{:S(2)}) async-start(f32[128,4,128]{2,1,0:T(4,128)} %bitcast.10), calls=%async_computation.1 | async-start | bytes 524288 | tf_op jit(solution)/shard_map/all_to_all | solution.py:258
  57.6 3.1 %collective-permute-start.5 = (f32[2,128,128]{2,1,0:T(8,128)S(1)}, f32[2,128,128]{2,1,0:T(8,128)S(1)}, u32[]{:S(2)}, u32[]{:S(2)}) collective-permute-start(f32[2,128,128]{2,1,0:T(8,128)S(1)} %get-tuple-element.16), channel_id=1, source_target_pairs={{0,16},{16,0},{1,17},{17,1},{2,18},{18,2},{3,19},{19,3},{4,20},{20... | collective-permute-start | bytes 393224 | tf_op jit(solution)/shard_map/ppermute | solution.py:255
  60.6 4.7 %collective-permute-done.5.met_ref = f32[2,128,128]{2,1,0:T(8,128)S(1)} collective-permute-done((f32[2,128,128]{2,1,0:T(8,128)S(1)}, f32[2,128,128]{2,1,0:T(8,128)S(1)}, u32[]{:S(2)}, u32[]{:S(2)}) %collective-permute-start.5) | collective-permute-done | bytes 131104 | tf_op jit(solution)/shard_map/ppermute | solution.py:255
  65.3 6.7 %all-to-all-done.1 = f32[128,4,128]{2,1,0:T(4,128)S(1)} async-done(((f32[128,4,128]{2,1,0:T(4,128)}), f32[128,4,128]{2,1,0:T(4,128)S(1)}, u32[]{:S(2)}, u32[]{:S(2)}) %all-to-all-start.1) | async-done | bytes 262176 | tf_op jit(solution)/shard_map/all_to_all | solution.py:258
  72.0 0.0 copy-done.3
  72.0 1.0 %shard_map.85 = f32[8,2,16,128]{3,2,1,0:T(8,128)} custom-call(f32[512,128]{1,0:T(8,128)S(1)} %bitcast.17, f32[2,128,128]{2,1,0:T(8,128)S(1)} %get-tuple-element.15.kept_ref, f32[2,128,128]{2,1,0:T(8,128)S(1)} %collective-permute-done.5.met_ref, f32[128,128]{1,0:T(8,128)S(1)} %copy-done.3), custom_call_target="tpu_custom_call" | custom-call | tf_op jit(solution)/shard_map/pallas_call | solution.py:205
  (2 shorter events, 0.0 us)
Async XLA Ops:
  0.0 18.7 %copy-start.5 = (f32[128,512]{1,0:T(8,128)S(1)}, f32[128,512]{1,0:T(8,128)}, u32[]{:S(2)}) copy-start(f32[128,512]{1,0:T(8,128)} %param.13) | copy-start | bytes 786436
  2.9 15.9 %copy-start.4 = (f32[1024,128]{1,0:T(8,128)S(1)}, f32[1024,128]{1,0:T(8,128)}, u32[]{:S(2)}) copy-start(f32[1024,128]{1,0:T(8,128)} %param.12) | copy-start | bytes 1572868
  2.9 10.4 %collective-permute-start.2 = (f32[256,128]{1,0:T(8,128)}, f32[256,128]{1,0:T(8,128)S(1)}, u32[]{:S(2)}, u32[]{:S(2)}) collective-permute-start(f32[256,128]{1,0:T(8,128)} %get-tuple-element.13), channel_id=1, source_target_pairs={{7,0},{37,1},{69,2},{96,3},{135,4},{162,5},{199,6},{224,7},{15,8},... | collective-permute-start | bytes 393224 | tf_op jit(solution)/shard_map/ppermute | solution.py:246
  4.8 16.9 %collective-permute-start = (f32[256,128]{1,0:T(8,128)}, f32[256,128]{1,0:T(8,128)S(1)}, u32[]{:S(2)}, u32[]{:S(2)}) collective-permute-start(f32[256,128]{1,0:T(8,128)} %get-tuple-element.11.own_ref), channel_id=1, source_target_pairs={{0,17},{1,16},{16,1},{17,0},{2,19},{3,18},{18,3},{19,2},{4,21},{5,... | collective-permute-start | bytes 393224 | tf_op jit(solution)/shard_map/ppermute | solution.py:247
  13.3 8.4 %collective-permute-start.3 = (f32[256,128]{1,0:T(8,128)S(1)}, f32[256,128]{1,0:T(8,128)S(1)}, u32[]{:S(2)}, u32[]{:S(2)}) collective-permute-start(f32[256,128]{1,0:T(8,128)S(1)} %collective-permute-done.2.panel_ref), channel_id=1, source_target_pairs={{0,8},{8,0},{1,9},{9,1},{2,10},{10,2},{3,11},{11,3},{4,12},{12,4},... | collective-permute-start | bytes 393224 | tf_op jit(solution)/shard_map/ppermute | solution.py:250
  13.3 8.4 %collective-permute-start.1 = (f32[128,128]{1,0:T(8,128)}, f32[128,128]{1,0:T(8,128)S(1)}, u32[]{:S(2)}, u32[]{:S(2)}) collective-permute-start(f32[128,128]{1,0:T(8,128)} %get-tuple-element.12), channel_id=1, source_target_pairs={{0,16},{16,0},{1,17},{17,1},{2,18},{18,2},{3,19},{19,3},{4,20},{20... | collective-permute-start | bytes 196616 | tf_op jit(solution)/shard_map/ppermute | solution.py:248
  18.8 2.8 %copy-start = (f32[8,32,128]{2,1,0:T(8,128)S(1)}, f32[8,32,128]{2,1,0:T(8,128)}, u32[]{:S(2)}) copy-start(f32[8,32,128]{2,1,0:T(8,128)} %param.9) | copy-start | bytes 393220
  18.8 2.8 %copy-start.1 = (f32[256,128]{1,0:T(8,128)S(1)}, f32[256,128]{1,0:T(8,128)}, u32[]{:S(2)}) copy-start(f32[256,128]{1,0:T(8,128)} %get-tuple-element.11.own_ref) | copy-start | bytes 393220
  18.9 2.8 %copy-start.2 = (f32[128,128]{1,0:T(8,128)S(1)}, f32[128,128]{1,0:T(8,128)}, u32[]{:S(2)}) copy-start(f32[128,128]{1,0:T(8,128)} %w_gate_ref.1) | copy-start | bytes 196612
  46.3 1.4 %collective-permute-start.4 = (f32[64,4,128]{2,1,0:T(4,128)S(1)}, f32[64,4,128]{2,1,0:T(4,128)S(1)}, u32[]{:S(2)}, u32[]{:S(2)}) collective-permute-start(f32[64,4,128]{2,1,0:T(4,128)S(1)} %slice.4), channel_id=1, source_target_pairs={{0,8},{8,0},{1,9},{9,1},{2,10},{10,2},{3,11},{11,3},{4,12},{12,4},... | collective-permute-start | bytes 393224 | tf_op jit(solution)/shard_map/ppermute | solution.py:256
  49.1 22.9 %copy-start.3 = (f32[128,128]{1,0:T(8,128)S(1)}, f32[128,128]{1,0:T(8,128)}, u32[]{:S(2)}) copy-start(f32[128,128]{1,0:T(8,128)} %w_ref.1) | copy-start | bytes 196612
  49.1 22.9 %all-to-all-start.1 = ((f32[128,4,128]{2,1,0:T(4,128)}), f32[128,4,128]{2,1,0:T(4,128)S(1)}, u32[]{:S(2)}, u32[]{:S(2)}) async-start(f32[128,4,128]{2,1,0:T(4,128)} %bitcast.10), calls=%async_computation.1 | async-start | bytes 524288 | tf_op jit(solution)/shard_map/all_to_all | solution.py:258
  57.6 7.7 %collective-permute-start.5 = (f32[2,128,128]{2,1,0:T(8,128)S(1)}, f32[2,128,128]{2,1,0:T(8,128)S(1)}, u32[]{:S(2)}, u32[]{:S(2)}) collective-permute-start(f32[2,128,128]{2,1,0:T(8,128)S(1)} %get-tuple-element.16), channel_id=1, source_target_pairs={{0,16},{16,0},{1,17},{17,1},{2,18},{18,2},{3,19},{19,3},{4,20},{20... | collective-permute-start | bytes 393224 | tf_op jit(solution)/shard_map/ppermute | solution.py:255

commit v10 on v9

--- a/solution.py
+++ b/solution.py
@@ -247,6 +247,7 @@
     met = lax.ppermute(left, ("yh", "yl"), [(0, 3), (1, 2), (2, 1), (3, 0)])
     met_pair = lax.ppermute(half, "yh", swap)
     w_outer_ba = w_outer.reshape(32, 32, 128).transpose(1, 0, 2).reshape(1024, 128)
+    panel, met_pair = lax.optimization_barrier((panel, met_pair))
     sibling = lax.ppermute(panel, "core", swap)
     edges, kept, sent = pair_stage(
         left, met, met_pair, panel, sibling, pair, w_outer_ba, w_tri.T, w_gate

time: 73.2 us -> 68.9 us (0.941)
  starting transfers between devices: 27.4 us -> 22 us
  waiting for transfers between devices: 15.2 us -> 19.1 us
  blocking collectives: 22.8 us -> 20 us
    ppermute x1, starting transfers between devices: 8.47 us -> 0.45 us  [per_device(): met = lax.ppermute(left, ('yh', 'yl'), [(0, 3), (1, 2), (2, 1), (3, 0)])]
    all_to_all x1, blocking collectives: 22.8 us -> 20 us  [per_device(): swapped = lax.all_to_all(edges.reshape(64, 8, 128), LAYER, 0, 0, tiled=True)]
    ppermute x1, starting transfers between devices: 5.43 us -> 8.02 us  [per_device(): met_pair = lax.ppermute(half, 'yh', swap)]
    ppermute x1, waiting for transfers between devices: 0.01 us -> 2.2 us  [per_device(): met = lax.ppermute(left, ('yh', 'yl'), [(0, 3), (1, 2), (2, 1), (3, 0)])]
    ppermute x1, waiting for transfers between devices: 2.48 us -> 4.15 us  [per_device(): met_pair = lax.ppermute(half, 'yh', swap)]
  transfers between devices with their start and end apart: 7 -> 7, of which waited for: 4 -> 5; matrix products, arithmetic and copies ran while one was open for 1% -> 1% of each run, Pallas kernels for 0% -> 0%
where the time goes in v10:
time: 68.9 us; the launch traced here: 68.6 us
  starting transfers between devices  22 us (32%)
  blocking collectives  20 us (29%)
  waiting for transfers between devices  19.1 us (28%)
  Pallas kernels  6.97 us (10%)
    all_to_all x1, blocking collectives, per_device(): swapped = lax.all_to_all(edges.reshape(64, 8, 128), LAYER, 0, 0, tiled=True)  20 us
    all_to_all x1, starting transfers between devices, per_device(): mixed = lax.all_to_all(back.reshape(128, 4, 128), CHIPS, 0, 0, tiled=True)  8.49 us
    ppermute x1, starting transfers between devices, per_device(): met_pair = lax.ppermute(half, 'yh', swap)  8.02 us
    pallas_call x4, Pallas kernels, call(): pl.pallas_call(kernel, out_shape=shapes if len(shapes) > 1 else shapes[0]...  6.97 us
    all_to_all x1, waiting for transfers between devices, per_device(): mixed = lax.all_to_all(back.reshape(128, 4, 128), CHIPS, 0, 0, tiled=True)  6.7 us
    ppermute x1, waiting for transfers between devices, per_device(): returned = lax.ppermute(sent, 'yh', swap)  4.69 us
    ppermute x1, waiting for transfers between devices, per_device(): met_pair = lax.ppermute(half, 'yh', swap)  4.15 us
    ppermute x1, starting transfers between devices, per_device(): returned = lax.ppermute(sent, 'yh', swap)  3.06 us
  transfers between devices with their start and end apart: 7, of which 5 were waited for; matrix products, arithmetic and copies ran while one was open for 1% of the time, Pallas kernels for 0%

profile of v10, /device:TPU:2, one launch (start us, length us, event | category | flops | bytes accessed | tf_op | source)
XLA Modules:
  0.0 68.6 jit_solution(9571867829678734489)
XLA Ops:
  0.0 0.0 copy-start.5
  0.0 2.9 %shard_map.82 = (f32[256,128]{1,0:T(8,128)}, f32[256,128]{1,0:T(8,128)}, f32[128,128]{1,0:T(8,128)}) custom-call(f32[128,8,256]{2,1,0:T(8,128)} %msa_ref.1, f32[32,256]{1,0:T(8,128)} %bitcast.23, f32[32,256]{1,0:T(8,128)} %bitcast.24, f32[8,2,16,128]{3,2,1,0:T(8,128)} %bitcast.18), custom_call_target="tpu_custom_call" | custom-call | tf_op jit(solution)/shard_map/pallas_call | solution.py:205
  2.9 0.0 copy-start.4
  2.9 1.9 %collective-permute-start.1 = (f32[256,128]{1,0:T(8,128)}, f32[256,128]{1,0:T(8,128)S(1)}, u32[]{:S(2)}, u32[]{:S(2)}) collective-permute-start(f32[256,128]{1,0:T(8,128)} %get-tuple-element.14), channel_id=1, source_target_pairs={{7,0},{37,1},{69,2},{96,3},{135,4},{162,5},{199,6},{224,7},{15,8},... | collective-permute-start | bytes 393224 | tf_op jit(solution)/shard_map/ppermute | solution.py:246
  4.8 8.0 %collective-permute-start.2 = (f32[128,128]{1,0:T(8,128)}, f32[128,128]{1,0:T(8,128)S(1)}, u32[]{:S(2)}, u32[]{:S(2)}) collective-permute-start(f32[128,128]{1,0:T(8,128)} %get-tuple-element.15), channel_id=1, source_target_pairs={{0,16},{16,0},{1,17},{17,1},{2,18},{18,2},{3,19},{19,3},{4,20},{20... | collective-permute-start | bytes 196616 | tf_op jit(solution)/shard_map/ppermute | solution.py:248
  12.8 0.4 collective-permute-start
  13.3 4.1 %collective-permute-done.2.met_pair_ref = f32[128,128]{1,0:T(8,128)S(1)} collective-permute-done((f32[128,128]{1,0:T(8,128)}, f32[128,128]{1,0:T(8,128)S(1)}, u32[]{:S(2)}, u32[]{:S(2)}) %collective-permute-start.2) | collective-permute-done | bytes 65568 | tf_op jit(solution)/shard_map/ppermute | solution.py:248
  17.4 0.0 collective-permute-done.1.panel_ref
  17.4 0.0 collective-permute-start.3
  17.4 0.0 copy-done.5
  17.4 0.1 copy.10
  17.5 0.0 copy-done.4
  17.6 0.0 copy-start
  17.6 0.0 copy-start.1
  17.6 0.0 copy-start.2
  17.6 0.3 copy.9
  17.9 2.2 %collective-permute-done.met_ref = f32[256,128]{1,0:T(8,128)S(1)} collective-permute-done((f32[256,128]{1,0:T(8,128)}, f32[256,128]{1,0:T(8,128)S(1)}, u32[]{:S(2)}, u32[]{:S(2)}) %collective-permute-start) | collective-permute-done | bytes 131104 | tf_op jit(solution)/shard_map/ppermute | solution.py:247
  20.1 0.0 collective-permute-done.3.sibling_ref
  20.1 0.0 copy-done
  20.1 0.0 copy-done.1
  20.1 0.0 copy-done.2
  20.1 1.7 %shard_map.83 = (f32[512,128]{1,0:T(8,128)S(1)}, f32[2,128,128]{2,1,0:T(8,128)S(1)}, f32[2,128,128]{2,1,0:T(8,128)S(1)}) custom-call(f32[256,128]{1,0:T(8,128)S(1)} %copy-done.1, f32[256,128]{1,0:T(8,128)S(1)} %collective-permute-done.met_ref, f32[128,128]{1,0:T(8,128)S(1)} %collective-permute-done.2.met_pair_ref, ...), custom_call_target="tpu_custom_call" | custom-call | tf_op jit(solution)/shard_map/pallas_call | solution.py:205
  21.9 20.0 %all_to_all.10 = f32[64,8,128]{2,1,0:T(8,128)S(1)} all-to-all(f32[64,8,128]{2,1,0:T(8,128)S(1)} %bitcast.20), channel_id=1, replica_groups=mesh['z'=8,'yh'=2,'core'=2,'x'=4,'yl'=2] {'z','x','yl'}, dimensions={0} | all-to-all | bytes 524288 | tf_op jit(solution)/shard_map/all_to_all | solution.py:255
  41.9 0.1 collective-permute-start.4
  42.0 1.3 %collective-permute-done.4 = f32[64,4,128]{2,1,0:T(4,128)S(1)} collective-permute-done((f32[64,4,128]{2,1,0:T(4,128)S(1)}, f32[64,4,128]{2,1,0:T(4,128)S(1)}, u32[]{:S(2)}, u32[]{:S(2)}) %collective-permute-start.4) | collective-permute-done | bytes 131104 | tf_op jit(solution)/shard_map/ppermute | solution.py:257
  43.3 1.4 %shard_map.84 = f32[512,128]{1,0:T(8,128)} custom-call(f32[512,128]{1,0:T(8,128)S(1)} %bitcast.15, f32[256,128]{1,0:T(8,128)S(1)} %bitcast.21), custom_call_target="tpu_custom_call" | custom-call | tf_op jit(solution)/shard_map/pallas_call | solution.py:205
  44.7 8.5 %all-to-all-start.1 = ((f32[128,4,128]{2,1,0:T(4,128)}), f32[128,4,128]{2,1,0:T(4,128)S(1)}, u32[]{:S(2)}, u32[]{:S(2)}) async-start(f32[128,4,128]{2,1,0:T(4,128)} %bitcast.10), calls=%async_computation.1 | async-start | bytes 524288 | tf_op jit(solution)/shard_map/all_to_all | solution.py:259
  53.2 3.1 %collective-permute-start.5 = (f32[2,128,128]{2,1,0:T(8,128)S(1)}, f32[2,128,128]{2,1,0:T(8,128)S(1)}, u32[]{:S(2)}, u32[]{:S(2)}) collective-permute-start(f32[2,128,128]{2,1,0:T(8,128)S(1)} %get-tuple-element.20), channel_id=1, source_target_pairs={{0,16},{16,0},{1,17},{17,1},{2,18},{18,2},{3,19},{19,3},{4,20},{20... | collective-permute-start | bytes 393224 | tf_op jit(solution)/shard_map/ppermute | solution.py:256
  56.3 4.7 %collective-permute-done.5.met_ref = f32[2,128,128]{2,1,0:T(8,128)S(1)} collective-permute-done((f32[2,128,128]{2,1,0:T(8,128)S(1)}, f32[2,128,128]{2,1,0:T(8,128)S(1)}, u32[]{:S(2)}, u32[]{:S(2)}) %collective-permute-start.5) | collective-permute-done | bytes 131104 | tf_op jit(solution)/shard_map/ppermute | solution.py:256
  61.0 6.7 %all-to-all-done.1 = f32[128,4,128]{2,1,0:T(4,128)S(1)} async-done(((f32[128,4,128]{2,1,0:T(4,128)}), f32[128,4,128]{2,1,0:T(4,128)S(1)}, u32[]{:S(2)}, u32[]{:S(2)}) %all-to-all-start.1) | async-done | bytes 262176 | tf_op jit(solution)/shard_map/all_to_all | solution.py:259
  67.7 0.0 copy-done.3
  67.7 1.0 %shard_map.85 = f32[8,2,16,128]{3,2,1,0:T(8,128)} custom-call(f32[512,128]{1,0:T(8,128)S(1)} %bitcast.16, f32[2,128,128]{2,1,0:T(8,128)S(1)} %get-tuple-element.19.kept_ref, f32[2,128,128]{2,1,0:T(8,128)S(1)} %collective-permute-done.5.met_ref, f32[128,128]{1,0:T(8,128)S(1)} %copy-done.3), custom_call_target="tpu_custom_call" | custom-call | tf_op jit(solution)/shard_map/pallas_call | solution.py:205
  (2 shorter events, 0.0 us)
Async XLA Ops:
  0.0 17.4 %copy-start.5 = (f32[128,512]{1,0:T(8,128)S(1)}, f32[128,512]{1,0:T(8,128)}, u32[]{:S(2)}) copy-start(f32[128,512]{1,0:T(8,128)} %param.13) | copy-start | bytes 786436
  2.9 14.7 %copy-start.4 = (f32[1024,128]{1,0:T(8,128)S(1)}, f32[1024,128]{1,0:T(8,128)}, u32[]{:S(2)}) copy-start(f32[1024,128]{1,0:T(8,128)} %param.12) | copy-start | bytes 1572868
  2.9 14.5 %collective-permute-start.1 = (f32[256,128]{1,0:T(8,128)}, f32[256,128]{1,0:T(8,128)S(1)}, u32[]{:S(2)}, u32[]{:S(2)}) collective-permute-start(f32[256,128]{1,0:T(8,128)} %get-tuple-element.14), channel_id=1, source_target_pairs={{7,0},{37,1},{69,2},{96,3},{135,4},{162,5},{199,6},{224,7},{15,8},... | collective-permute-start | bytes 393224 | tf_op jit(solution)/shard_map/ppermute | solution.py:246
  4.8 12.6 %collective-permute-start.2 = (f32[128,128]{1,0:T(8,128)}, f32[128,128]{1,0:T(8,128)S(1)}, u32[]{:S(2)}, u32[]{:S(2)}) collective-permute-start(f32[128,128]{1,0:T(8,128)} %get-tuple-element.15), channel_id=1, source_target_pairs={{0,16},{16,0},{1,17},{17,1},{2,18},{18,2},{3,19},{19,3},{4,20},{20... | collective-permute-start | bytes 196616 | tf_op jit(solution)/shard_map/ppermute | solution.py:248
  12.8 7.3 %collective-permute-start = (f32[256,128]{1,0:T(8,128)}, f32[256,128]{1,0:T(8,128)S(1)}, u32[]{:S(2)}, u32[]{:S(2)}) collective-permute-start(f32[256,128]{1,0:T(8,128)} %get-tuple-element.13.own_ref), channel_id=1, source_target_pairs={{0,17},{1,16},{16,1},{17,0},{2,19},{3,18},{18,3},{19,2},{4,21},{5,... | collective-permute-start | bytes 393224 | tf_op jit(solution)/shard_map/ppermute | solution.py:247
  17.4 2.7 %collective-permute-start.3 = (f32[256,128]{1,0:T(8,128)S(1)}, f32[256,128]{1,0:T(8,128)S(1)}, u32[]{:S(2)}, u32[]{:S(2)}) collective-permute-start(f32[256,128]{1,0:T(8,128)S(1)} %collective-permute-done.1.panel_ref), channel_id=1, source_target_pairs={{0,8},{8,0},{1,9},{9,1},{2,10},{10,2},{3,11},{11,3},{4,12},{12,4},... | collective-permute-start | bytes 393224 | tf_op jit(solution)/shard_map/ppermute | solution.py:251
  17.6 2.6 %copy-start = (f32[8,32,128]{2,1,0:T(8,128)S(1)}, f32[8,32,128]{2,1,0:T(8,128)}, u32[]{:S(2)}) copy-start(f32[8,32,128]{2,1,0:T(8,128)} %param.9) | copy-start | bytes 393220
  17.6 2.5 %copy-start.1 = (f32[256,128]{1,0:T(8,128)S(1)}, f32[256,128]{1,0:T(8,128)}, u32[]{:S(2)}) copy-start(f32[256,128]{1,0:T(8,128)} %get-tuple-element.13.own_ref) | copy-start | bytes 393220
  17.6 2.5 %copy-start.2 = (f32[128,128]{1,0:T(8,128)S(1)}, f32[128,128]{1,0:T(8,128)}, u32[]{:S(2)}) copy-start(f32[128,128]{1,0:T(8,128)} %w_gate_ref.1) | copy-start | bytes 196612
  41.9 1.4 %collective-permute-start.4 = (f32[64,4,128]{2,1,0:T(4,128)S(1)}, f32[64,4,128]{2,1,0:T(4,128)S(1)}, u32[]{:S(2)}, u32[]{:S(2)}) collective-permute-start(f32[64,4,128]{2,1,0:T(4,128)S(1)} %slice.4), channel_id=1, source_target_pairs={{0,8},{8,0},{1,9},{9,1},{2,10},{10,2},{3,11},{11,3},{4,12},{12,4},... | collective-permute-start | bytes 393224 | tf_op jit(solution)/shard_map/ppermute | solution.py:257
  44.7 23.0 %copy-start.3 = (f32[128,128]{1,0:T(8,128)S(1)}, f32[128,128]{1,0:T(8,128)}, u32[]{:S(2)}) copy-start(f32[128,128]{1,0:T(8,128)} %w_ref.1) | copy-start | bytes 196612
  44.7 22.9 %all-to-all-start.1 = ((f32[128,4,128]{2,1,0:T(4,128)}), f32[128,4,128]{2,1,0:T(4,128)S(1)}, u32[]{:S(2)}, u32[]{:S(2)}) async-start(f32[128,4,128]{2,1,0:T(4,128)} %bitcast.10), calls=%async_computation.1 | async-start | bytes 524288 | tf_op jit(solution)/shard_map/all_to_all | solution.py:259
  53.2 7.7 %collective-permute-start.5 = (f32[2,128,128]{2,1,0:T(8,128)S(1)}, f32[2,128,128]{2,1,0:T(8,128)S(1)}, u32[]{:S(2)}, u32[]{:S(2)}) collective-permute-start(f32[2,128,128]{2,1,0:T(8,128)S(1)} %get-tuple-element.20), channel_id=1, source_target_pairs={{0,16},{16,0},{1,17},{17,1},{2,18},{18,2},{3,19},{19,3},{4,20},{20... | collective-permute-start | bytes 393224 | tf_op jit(solution)/shard_map/ppermute | solution.py:256

commit v11 on v10

--- a/solution.py
+++ b/solution.py
@@ -46,18 +46,19 @@
     return high, (x - high.astype(jnp.float32)).astype(jnp.bfloat16)
 
 
+def halves(x):
+    return jnp.concatenate(split(x), 1)
+
+
 def dot_deep(a, b):
     a_high, a_low = split(a)
+    both = mm(a_high, b)
+    return both[:, :128] + both[:, 128:] + mm(a_low, b[:, :128])
+
+
+def dot_t(a, b):
     b_high, b_low = split(b)
-    both = mm(a_high, jnp.concatenate([b_high, b_low], 1))
-    return both[:, :128] + both[:, 128:] + mm(a_low, b_high)
-
-
-def dot_t(a, b):
-    a_high, a_low = split(a)
-    b_high, b_low = split(b)
-    shared = mm_t(jnp.concatenate([a_high, a_low], 1), jnp.concatenate([b_high, b_high], 1))
-    return shared + mm_t(a_high, b_low)
+    return mm_t(a, jnp.concatenate([b_high, b_high], 1)) + mm_t(a[:, :128], b_low)
 
 
 def layer_norm(values, axis):
@@ -94,8 +95,20 @@
         half_ref[pl.ds(p * 16, 16), :] = pair_ref[turned_rows(p), other]
 
 
+def weight_kernel(w_outer_ref, w_tri_ref, outer_ref, tri_ref):
+    for b in range(32):
+        outer_ref[pl.ds(b * 32, 32), :] = halves(w_outer_ref[pl.ds(b, 32, stride=32), :])
+    tri_ref[...] = halves(w_tri_ref[...])
+
+
+def gate_kernel(kept_ref, met_ref, w_ref, out_ref):
+    w = halves(w_ref[...])
+    for at, ref in enumerate((kept_ref, met_ref)):
+        out_ref[at] = sigmoid(dot_deep(layer_norm(ref[...], -1), w))
+
+
 def pair_kernel(
-    own_ref, met_ref, met_pair_ref, panel_ref, sibling_ref, pair_ref, w_outer_ref, w_tri_ref, w_gate_ref,
+    own_ref, met_ref, met_pair_ref, panel_ref, sibling_ref, pair_ref, w_outer_ref, w_tri_ref,
     edges_ref, kept_ref, sent_ref, outer_ref, flat_ref,
 ):
     yh = lax.axis_index("yh")
@@ -105,7 +118,7 @@
     panels = jnp.concatenate(
         [jnp.where(first, panel, sibling), jnp.where(first, sibling, panel)], 0
     )
-    outer_ref[...] = dot_t(panels, left)
+    outer_ref[...] = dot_t(halves(panels), left)
     lane = lax.broadcasted_iota(jnp.int32, (8, 128), 1)
     low_half = lane < 64
     even = (lane // 32) % 2 == 0
@@ -142,9 +155,8 @@
             own, met = edge[h * 64 : h * 64 + 64, :128], edge[h * 64 : h * 64 + 64, 128:]
             edges_ref[pl.ds(q * 2, 64, stride=8), :] = jnp.where(yh == 0, own, met)
             edges_ref[pl.ds(q * 2 + 1, 64, stride=8), :] = jnp.where(yh == 0, met, own)
-    gate = sigmoid(dot_deep(normed, w_gate_ref[...]))
-    kept_ref[0], kept_ref[1] = mid[:128], gate[:128]
-    sent_ref[0], sent_ref[1] = mid[128:], gate[128:]
+    kept_ref[...] = mid[:128]
+    sent_ref[...] = mid[128:]
 
 
 def turn_blocks(x, masks):
@@ -170,7 +182,7 @@
                 row = y * 128 + turned_rows(z) * 16
                 r_ref[pl.ds(row, 8), :] = jnp.where(core == 0, own, other)
                 r_ref[pl.ds(row + 8, 8), :] = jnp.where(core == 0, other, own)
-        mixed = dot_t(l_ref[...], r_ref[...])
+        mixed = dot_t(halves(l_ref[...]), r_ref[...])
         for z in range(8):
             for y in range(2):
                 for half in range(2):
@@ -180,9 +192,9 @@
                     )
 
 
-def output_kernel(mixed_ref, kept_ref, met_ref, w_ref, out_ref):
+def output_kernel(mixed_ref, kept_ref, met_ref, gates_ref, w_ref, out_ref):
     yh = lax.axis_index("yh")
-    w = w_ref[...]
+    w = halves(w_ref[...])
     for half in range(2):
         tiles = []
         for h in range(2):
@@ -193,15 +205,15 @@
                 ]
                 tiles.append(parts[0] + parts[1])
         update = dot_deep(layer_norm(jnp.concatenate(tiles, 0), 0).T, w)
-        mid = jnp.where(yh == half, kept_ref[0], met_ref[0])
-        gate = jnp.where(yh == half, kept_ref[1], met_ref[1])
+        mid = jnp.where(yh == half, kept_ref[...], met_ref[...])
+        gate = jnp.where(yh == half, gates_ref[0], gates_ref[1])
         for i in range(8):
             p = turned_rows(i) * 16
             out_ref[i, half] = mid[p : p + 16] + gate[p : p + 16] * update[i * 16 : i * 16 + 16]
 
 
-def call(kernel, out_shapes, scratch, *args, limit=VMEM_LIMIT):
-    shapes = [jax.ShapeDtypeStruct(s, jnp.float32) for s in out_shapes]
+def call(kernel, out_shapes, scratch, *args, limit=VMEM_LIMIT, kind=jnp.float32):
+    shapes = [jax.ShapeDtypeStruct(s, kind) for s in out_shapes]
     return pl.pallas_call(
         kernel,
         out_shape=shapes if len(shapes) > 1 else shapes[0],
@@ -222,12 +234,12 @@
     )
 
 
-def pair_stage(own, met, met_pair, panel, sibling, pair, w_outer, w_tri, w_gate):
+def pair_stage(*args):
     return call(
         pair_kernel,
-        [(512, 128), (2, 128, 128), (2, 128, 128)],
+        [(512, 128), (128, 128), (128, 128)],
         [vmem(512, 512), vmem(256, 1024)],
-        own, met, met_pair, panel, sibling, pair, w_outer, w_tri, w_gate,
+        *args,
     )
 
 
@@ -235,8 +247,16 @@
     return call(triangle_kernel, [(512, 128)], [vmem(128, 128), vmem(256, 128)], left, right)
 
 
-def output_stage(mixed, kept, met, w_out):
-    return call(output_kernel, [(8, 2, 16, 128)], [], mixed, kept, met, w_out)
+def output_stage(mixed, kept, met, gates, w_out):
+    return call(output_kernel, [(8, 2, 16, 128)], [], mixed, kept, met, gates, w_out)
+
+
+def gates_of(kept, met, w_gate):
+    return call(gate_kernel, [(2, 128, 128)], [], kept, met, w_gate)
+
+
+def prepared(w_outer, w_tri):
+    return call(weight_kernel, [(1024, 256), (512, 256)], [], w_outer, w_tri, kind=jnp.bfloat16)
 
 
 def per_device(homolog, pair, w_first, w_second, w_outer, w_tri, w_gate, w_out):
@@ -246,18 +266,19 @@
     panel = lax.ppermute(right, ALL, panel_permutation())
     met = lax.ppermute(left, ("yh", "yl"), [(0, 3), (1, 2), (2, 1), (3, 0)])
     met_pair = lax.ppermute(half, "yh", swap)
-    w_outer_ba = w_outer.reshape(32, 32, 128).transpose(1, 0, 2).reshape(1024, 128)
+    weights = prepared(w_outer, w_tri.T)
     panel, met_pair = lax.optimization_barrier((panel, met_pair))
     sibling = lax.ppermute(panel, "core", swap)
     edges, kept, sent = pair_stage(
-        left, met, met_pair, panel, sibling, pair, w_outer_ba, w_tri.T, w_gate
+        left, met, met_pair, panel, sibling, pair, *weights
     )
     swapped = lax.all_to_all(edges.reshape(64, 8, 128), LAYER, 0, 0, tiled=True)
     returned = lax.ppermute(sent, "yh", swap)
     rights = lax.ppermute(swapped[:, 4:], "core", swap)
     back = triangle(swapped.reshape(512, 128), rights.reshape(256, 128))
     mixed = lax.all_to_all(back.reshape(128, 4, 128), CHIPS, 0, 0, tiled=True)
-    return output_stage(mixed.reshape(512, 128), kept, returned, w_out).reshape(8, 32, 128)
+    gates = gates_of(kept, returned, w_gate)
+    return output_stage(mixed.reshape(512, 128), kept, returned, gates, w_out).reshape(8, 32, 128)
 
 
 def solution(mesh):

time: 68.9 us -> 68.9 us (level)
  Pallas kernels: 6.97 us -> 7.68 us
    ppermute x1, waiting for transfers between devices: 4.69 us -> 3.34 us  [per_device(): returned = lax.ppermute(sent, 'yh', swap)]
    all_to_all x1, waiting for transfers between devices: 6.7 us -> 7.67 us  [per_device(): mixed = lax.all_to_all(back.reshape(128, 4, 128), CHIPS, 0, 0, tiled=True)]
    pallas_call x4 -> x6, Pallas kernels: 6.97 us -> 7.68 us  [call(): pl.pallas_call(kernel, out_shape=shapes if len(shapes) > 1 else shapes[0]...]
  transfers between devices with their start and end apart: 7 -> 7, of which waited for: 5 -> 5; matrix products, arithmetic and copies ran while one was open for 1% -> 0% of each run, Pallas kernels for 0% -> 1%
where the time goes in v11:
time: 68.9 us; the launch traced here: 68.7 us
  starting transfers between devices  22 us (32%)
  blocking collectives  20 us (29%)
  waiting for transfers between devices  18.7 us (27%)
  Pallas kernels  7.68 us (11%)
    all_to_all x1, blocking collectives, per_device(): swapped = lax.all_to_all(edges.reshape(64, 8, 128), LAYER, 0, 0, tiled=True)  20 us
    all_to_all x1, starting transfers between devices, per_device(): mixed = lax.all_to_all(back.reshape(128, 4, 128), CHIPS, 0, 0, tiled=True)  8.49 us
    ppermute x1, starting transfers between devices, per_device(): met_pair = lax.ppermute(half, 'yh', swap)  8.02 us
    pallas_call x6, Pallas kernels, call(): pl.pallas_call(kernel, out_shape=shapes if len(shapes) > 1 else shapes[0]...  7.68 us
    all_to_all x1, waiting for transfers between devices, per_device(): mixed = lax.all_to_all(back.reshape(128, 4, 128), CHIPS, 0, 0, tiled=True)  7.67 us
    ppermute x1, waiting for transfers between devices, per_device(): met_pair = lax.ppermute(half, 'yh', swap)  4.15 us
    ppermute x1, waiting for transfers between devices, per_device(): returned = lax.ppermute(sent, 'yh', swap)  3.34 us
    ppermute x1, starting transfers between devices, per_device(): returned = lax.ppermute(sent, 'yh', swap)  3.06 us
  transfers between devices with their start and end apart: 7, of which 5 were waited for; matrix products, arithmetic and copies ran while one was open for 0% of the time, Pallas kernels for 1%

profile of v11, /device:TPU:2, one launch (start us, length us, event | category | flops | bytes accessed | tf_op | source)
XLA Modules:
  0.0 68.7 jit_solution(9821749527136336684)
XLA Ops:
  0.0 0.0 copy-start.5
  0.0 2.9 %shard_map.82 = (f32[256,128]{1,0:T(8,128)}, f32[256,128]{1,0:T(8,128)}, f32[128,128]{1,0:T(8,128)}) custom-call(f32[128,8,256]{2,1,0:T(8,128)} %msa_ref.1, f32[32,256]{1,0:T(8,128)} %bitcast.17, f32[32,256]{1,0:T(8,128)} %bitcast.18, f32[8,2,16,128]{3,2,1,0:T(8,128)} %bitcast.13), custom_call_target="tpu_custom_call" | custom-call | tf_op jit(solution)/shard_map/pallas_call | solution.py:217
  2.9 0.0 copy-start.1
  2.9 1.9 %collective-permute-start.1 = (f32[256,128]{1,0:T(8,128)}, f32[256,128]{1,0:T(8,128)S(1)}, u32[]{:S(2)}, u32[]{:S(2)}) collective-permute-start(f32[256,128]{1,0:T(8,128)} %get-tuple-element.16), channel_id=1, source_target_pairs={{7,0},{37,1},{69,2},{96,3},{135,4},{162,5},{199,6},{224,7},{15,8},... | collective-permute-start | bytes 393224 | tf_op jit(solution)/shard_map/ppermute | solution.py:266
  4.8 8.0 %collective-permute-start.2 = (f32[128,128]{1,0:T(8,128)}, f32[128,128]{1,0:T(8,128)S(1)}, u32[]{:S(2)}, u32[]{:S(2)}) collective-permute-start(f32[128,128]{1,0:T(8,128)} %get-tuple-element.17), channel_id=1, source_target_pairs={{0,16},{16,0},{1,17},{17,1},{2,18},{18,2},{3,19},{19,3},{4,20},{20... | collective-permute-start | bytes 196616 | tf_op jit(solution)/shard_map/ppermute | solution.py:268
  12.8 0.4 collective-permute-start
  13.3 4.1 %collective-permute-done.2.met_pair_ref = f32[128,128]{1,0:T(8,128)S(1)} collective-permute-done((f32[128,128]{1,0:T(8,128)}, f32[128,128]{1,0:T(8,128)S(1)}, u32[]{:S(2)}, u32[]{:S(2)}) %collective-permute-start.2) | collective-permute-done | bytes 65568 | tf_op jit(solution)/shard_map/ppermute | solution.py:268
  17.4 0.0 collective-permute-done.1.panel_ref
  17.4 0.0 collective-permute-start.3
  17.4 0.0 copy-done.5
  17.4 0.1 copy.9
  17.5 0.0 copy-done.1
  17.6 0.0 copy-start
  17.6 0.0 copy-start.2
  17.6 0.3 shard_map.83
  17.9 2.2 %collective-permute-done.met_ref = f32[256,128]{1,0:T(8,128)S(1)} collective-permute-done((f32[256,128]{1,0:T(8,128)}, f32[256,128]{1,0:T(8,128)S(1)}, u32[]{:S(2)}, u32[]{:S(2)}) %collective-permute-start) | collective-permute-done | bytes 131104 | tf_op jit(solution)/shard_map/ppermute | solution.py:267
  20.1 0.0 collective-permute-done.3.sibling_ref
  20.1 0.0 copy-done
  20.1 0.0 copy-done.2
  20.1 1.7 %shard_map.84 = (f32[512,128]{1,0:T(8,128)S(1)}, f32[128,128]{1,0:T(8,128)S(1)}, f32[128,128]{1,0:T(8,128)S(1)}) custom-call(f32[256,128]{1,0:T(8,128)S(1)} %copy-done.2, f32[256,128]{1,0:T(8,128)S(1)} %collective-permute-done.met_ref, f32[128,128]{1,0:T(8,128)S(1)} %collective-permute-done.2.met_pair_ref, f32[256,128]{1,0:T(8,128)S(1)} %collective-permute-done.1.panel_ref, ...), custom_call_target="tpu_custom_call" | custom-call | tf_op jit(solution)/shard_map/pallas_call | solution.py:217
  21.9 20.0 %all_to_all.10 = f32[64,8,128]{2,1,0:T(8,128)S(1)} all-to-all(f32[64,8,128]{2,1,0:T(8,128)S(1)} %bitcast.15), channel_id=1, replica_groups=mesh['z'=8,'yh'=2,'core'=2,'x'=4,'yl'=2] {'z','x','yl'}, dimensions={0} | all-to-all | bytes 524288 | tf_op jit(solution)/shard_map/all_to_all | solution.py:275
  41.9 0.1 collective-permute-start.4
  42.0 1.3 %collective-permute-done.4 = f32[64,4,128]{2,1,0:T(4,128)S(1)} collective-permute-done((f32[64,4,128]{2,1,0:T(4,128)S(1)}, f32[64,4,128]{2,1,0:T(4,128)S(1)}, u32[]{:S(2)}, u32[]{:S(2)}) %collective-permute-start.4) | collective-permute-done | bytes 131104 | tf_op jit(solution)/shard_map/ppermute | solution.py:277
  43.4 1.4 %shard_map.85 = f32[512,128]{1,0:T(8,128)} custom-call(f32[512,128]{1,0:T(8,128)S(1)} %bitcast.10, f32[256,128]{1,0:T(8,128)S(1)} %bitcast.16), custom_call_target="tpu_custom_call" | custom-call | tf_op jit(solution)/shard_map/pallas_call | solution.py:217
  44.7 8.5 %all-to-all-start.1 = ((f32[128,4,128]{2,1,0:T(4,128)}), f32[128,4,128]{2,1,0:T(4,128)S(1)}, u32[]{:S(2)}, u32[]{:S(2)}) async-start(f32[128,4,128]{2,1,0:T(4,128)} %bitcast.7), calls=%async_computation.1 | async-start | bytes 524288 | tf_op jit(solution)/shard_map/all_to_all | solution.py:279
  53.2 3.1 %collective-permute-start.5 = (f32[128,128]{1,0:T(8,128)S(1)}, f32[128,128]{1,0:T(8,128)S(1)}, u32[]{:S(2)}, u32[]{:S(2)}) collective-permute-start(f32[128,128]{1,0:T(8,128)S(1)} %get-tuple-element.24), channel_id=1, source_target_pairs={{0,16},{16,0},{1,17},{17,1},{2,18},{18,2},{3,19},{19,3},{4,20},{20... | collective-permute-start | bytes 196616 | tf_op jit(solution)/shard_map/ppermute | solution.py:276
  56.3 3.3 %collective-permute-done.5.met_ref = f32[128,128]{1,0:T(8,128)S(1)} collective-permute-done((f32[128,128]{1,0:T(8,128)S(1)}, f32[128,128]{1,0:T(8,128)S(1)}, u32[]{:S(2)}, u32[]{:S(2)}) %collective-permute-start.5) | collective-permute-done | bytes 65568 | tf_op jit(solution)/shard_map/ppermute | solution.py:276
  59.6 0.0 copy-done.3
  59.6 0.4 shard_map.86.gates_ref
  60.0 7.7 %all-to-all-done.1 = f32[128,4,128]{2,1,0:T(4,128)S(1)} async-done(((f32[128,4,128]{2,1,0:T(4,128)}), f32[128,4,128]{2,1,0:T(4,128)S(1)}, u32[]{:S(2)}, u32[]{:S(2)}) %all-to-all-start.1) | async-done | bytes 262176 | tf_op jit(solution)/shard_map/all_to_all | solution.py:279
  67.7 0.0 copy-done.4
  67.7 1.0 %shard_map.87 = f32[8,2,16,128]{3,2,1,0:T(8,128)} custom-call(f32[512,128]{1,0:T(8,128)S(1)} %bitcast.12, f32[128,128]{1,0:T(8,128)S(1)} %get-tuple-element.23.kept_ref, f32[128,128]{1,0:T(8,128)S(1)} %collective-permute-done.5.met_ref, f32[2,128,128]{2,1,0:T(8,128)S(1)} %shard_map.86.gates_ref, f32[128,128]{1,0:T(8,128)S(1)} %copy-done.4), custom_call_target="tpu_custom_call" | custom-call | tf_op jit(solution)/shard_map/pallas_call | solution.py:217
  (3 shorter events, 0.0 us)
Async XLA Ops:
  0.0 17.4 %copy-start.5 = (f32[128,512]{1,0:T(8,128)S(1)}, f32[128,512]{1,0:T(8,128)}, u32[]{:S(2)}) copy-start(f32[128,512]{1,0:T(8,128)} %param.13) | copy-start | bytes 786436
  2.9 14.7 %copy-start.1 = (f32[1024,128]{1,0:T(8,128)S(1)}, f32[1024,128]{1,0:T(8,128)}, u32[]{:S(2)}) copy-start(f32[1024,128]{1,0:T(8,128)} %w_outer_ref.1) | copy-start | bytes 1572868
  2.9 14.5 %collective-permute-start.1 = (f32[256,128]{1,0:T(8,128)}, f32[256,128]{1,0:T(8,128)S(1)}, u32[]{:S(2)}, u32[]{:S(2)}) collective-permute-start(f32[256,128]{1,0:T(8,128)} %get-tuple-element.16), channel_id=1, source_target_pairs={{7,0},{37,1},{69,2},{96,3},{135,4},{162,5},{199,6},{224,7},{15,8},... | collective-permute-start | bytes 393224 | tf_op jit(solution)/shard_map/ppermute | solution.py:266
  4.8 12.6 %collective-permute-start.2 = (f32[128,128]{1,0:T(8,128)}, f32[128,128]{1,0:T(8,128)S(1)}, u32[]{:S(2)}, u32[]{:S(2)}) collective-permute-start(f32[128,128]{1,0:T(8,128)} %get-tuple-element.17), channel_id=1, source_target_pairs={{0,16},{16,0},{1,17},{17,1},{2,18},{18,2},{3,19},{19,3},{4,20},{20... | collective-permute-start | bytes 196616 | tf_op jit(solution)/shard_map/ppermute | solution.py:268
  12.8 7.3 %collective-permute-start = (f32[256,128]{1,0:T(8,128)}, f32[256,128]{1,0:T(8,128)S(1)}, u32[]{:S(2)}, u32[]{:S(2)}) collective-permute-start(f32[256,128]{1,0:T(8,128)} %get-tuple-element.15.own_ref), channel_id=1, source_target_pairs={{0,17},{1,16},{16,1},{17,0},{2,19},{3,18},{18,3},{19,2},{4,21},{5,... | collective-permute-start | bytes 393224 | tf_op jit(solution)/shard_map/ppermute | solution.py:267
  17.4 2.7 %collective-permute-start.3 = (f32[256,128]{1,0:T(8,128)S(1)}, f32[256,128]{1,0:T(8,128)S(1)}, u32[]{:S(2)}, u32[]{:S(2)}) collective-permute-start(f32[256,128]{1,0:T(8,128)S(1)} %collective-permute-done.1.panel_ref), channel_id=1, source_target_pairs={{0,8},{8,0},{1,9},{9,1},{2,10},{10,2},{3,11},{11,3},{4,12},{12,4},... | collective-permute-start | bytes 393224 | tf_op jit(solution)/shard_map/ppermute | solution.py:271
  17.6 2.6 %copy-start = (f32[8,32,128]{2,1,0:T(8,128)S(1)}, f32[8,32,128]{2,1,0:T(8,128)}, u32[]{:S(2)}) copy-start(f32[8,32,128]{2,1,0:T(8,128)} %param.9) | copy-start | bytes 393220
  17.6 2.5 %copy-start.2 = (f32[256,128]{1,0:T(8,128)S(1)}, f32[256,128]{1,0:T(8,128)}, u32[]{:S(2)}) copy-start(f32[256,128]{1,0:T(8,128)} %get-tuple-element.15.own_ref) | copy-start | bytes 393220
  41.9 1.4 %collective-permute-start.4 = (f32[64,4,128]{2,1,0:T(4,128)S(1)}, f32[64,4,128]{2,1,0:T(4,128)S(1)}, u32[]{:S(2)}, u32[]{:S(2)}) collective-permute-start(f32[64,4,128]{2,1,0:T(4,128)S(1)} %slice.4), channel_id=1, source_target_pairs={{0,8},{8,0},{1,9},{9,1},{2,10},{10,2},{3,11},{11,3},{4,12},{12,4},... | collective-permute-start | bytes 393224 | tf_op jit(solution)/shard_map/ppermute | solution.py:277
  44.7 14.9 %copy-start.3 = (f32[128,128]{1,0:T(8,128)S(1)}, f32[128,128]{1,0:T(8,128)}, u32[]{:S(2)}) copy-start(f32[128,128]{1,0:T(8,128)} %w_ref.2) | copy-start | bytes 196612
  44.7 22.9 %all-to-all-start.1 = ((f32[128,4,128]{2,1,0:T(4,128)}), f32[128,4,128]{2,1,0:T(4,128)S(1)}, u32[]{:S(2)}, u32[]{:S(2)}) async-start(f32[128,4,128]{2,1,0:T(4,128)} %bitcast.7), calls=%async_computation.1 | async-start | bytes 524288 | tf_op jit(solution)/shard_map/all_to_all | solution.py:279
  53.2 6.4 %collective-permute-start.5 = (f32[128,128]{1,0:T(8,128)S(1)}, f32[128,128]{1,0:T(8,128)S(1)}, u32[]{:S(2)}, u32[]{:S(2)}) collective-permute-start(f32[128,128]{1,0:T(8,128)S(1)} %get-tuple-element.24), channel_id=1, source_target_pairs={{0,16},{16,0},{1,17},{17,1},{2,18},{18,2},{3,19},{19,3},{4,20},{20... | collective-permute-start | bytes 196616 | tf_op jit(solution)/shard_map/ppermute | solution.py:276
  59.6 8.0 %copy-start.4 = (f32[128,128]{1,0:T(8,128)S(1)}, f32[128,128]{1,0:T(8,128)}, u32[]{:S(2)}) copy-start(f32[128,128]{1,0:T(8,128)} %w_ref.3) | copy-start | bytes 196612

commit v12 on v11

--- a/solution.py
+++ b/solution.py
@@ -10,8 +10,8 @@
 ALL = ("z", "yh", "core", "x", "yl")
 ROW = ("z", "yh", "core")
 COL = ("x", "yl")
-LAYER = ("z", "x", "yl")
-CHIPS = ("z", "yh", "x", "yl")
+LAYER = ("x", "yl", "z")
+CHIPS = ("x", "yl", "z", "yh")
 VMEM_LIMIT = 32 * 1024 * 1024
 
 
@@ -173,11 +173,11 @@
     for h in range(2):
         for z in range(8):
             for y in range(2):
-                x = left_ref[pl.ds(z * 64 + h * 2 + y, 8, stride=8), :]
+                x = left_ref[pl.ds(z * 8 + h * 2 + y, 8, stride=64), :]
                 l_ref[pl.ds(y * 64 + z * 8, 8), :] = turn_blocks(x, masks)
-                x = left_ref[pl.ds(z * 64 + (2 + h) * 2 + y, 8, stride=8), :]
+                x = left_ref[pl.ds(z * 8 + (2 + h) * 2 + y, 8, stride=64), :]
                 own = turn_blocks(x, masks)
-                x = right_ref[pl.ds(z * 32 + h * 2 + y, 8, stride=4), :]
+                x = right_ref[pl.ds(z * 4 + h * 2 + y, 8, stride=32), :]
                 other = turn_blocks(x, masks)
                 row = y * 128 + turned_rows(z) * 16
                 r_ref[pl.ds(row, 8), :] = jnp.where(core == 0, own, other)
@@ -187,7 +187,7 @@
             for y in range(2):
                 for half in range(2):
                     block = mixed[y * 64 + z * 8 :, half * 128 :][:8, :128]
-                    out_ref[pl.ds((z * 2 + y) * 32 + h * 2 + half, 8, stride=4), :] = turn_blocks(
+                    out_ref[pl.ds((z * 2 + y) * 4 + h * 2 + half, 8, stride=64), :] = turn_blocks(
                         block, masks
                     )
 
@@ -198,9 +198,9 @@
     for half in range(2):
         tiles = []
         for h in range(2):
-            for z in range(8):
+            for c in range(8):
                 parts = [
-                    mixed_ref[pl.ds((z * 2 + y) * 32 + h * 2 + half, 8, stride=4), :]
+                    mixed_ref[pl.ds(c * 64 + y * 4 + h * 2 + half, 8, stride=8), :]
                     for y in range(2)
                 ]
                 tiles.append(parts[0] + parts[1])

time: 68.9 us -> 69.1 us (level)
  no operation moved by 1% of the time
where the time goes in v12:
time: 69.1 us; the launch traced here: 68.8 us
  starting transfers between devices  22.4 us (32%)
  blocking collectives  19.9 us (29%)
  waiting for transfers between devices  18.4 us (27%)
  Pallas kernels  7.8 us (11%)
    all_to_all x1, blocking collectives, per_device(): swapped = lax.all_to_all(edges.reshape(64, 8, 128), LAYER, 0, 0, tiled=True)  19.9 us
    all_to_all x1, starting transfers between devices, per_device(): mixed = lax.all_to_all(back.reshape(128, 4, 128), CHIPS, 0, 0, tiled=True)  8.92 us
    ppermute x1, starting transfers between devices, per_device(): met_pair = lax.ppermute(half, 'yh', swap)  8.02 us
    pallas_call x6, Pallas kernels, call(): pl.pallas_call(kernel, out_shape=shapes if len(shapes) > 1 else shapes[0]...  7.8 us
    all_to_all x1, waiting for transfers between devices, per_device(): mixed = lax.all_to_all(back.reshape(128, 4, 128), CHIPS, 0, 0, tiled=True)  7.58 us
    ppermute x1, waiting for transfers between devices, per_device(): met_pair = lax.ppermute(half, 'yh', swap)  4.15 us
    ppermute x1, waiting for transfers between devices, per_device(): returned = lax.ppermute(sent, 'yh', swap)  3.17 us
    ppermute x1, starting transfers between devices, per_device(): returned = lax.ppermute(sent, 'yh', swap)  3.06 us
  transfers between devices with their start and end apart: 7, of which 5 were waited for; matrix products, arithmetic and copies ran while one was open for 0% of the time, Pallas kernels for 1%

profile of v12, /device:TPU:2, one launch (start us, length us, event | category | flops | bytes accessed | tf_op | source)
XLA Modules:
  0.0 68.8 jit_solution(17857940986688487005)
XLA Ops:
  0.0 0.0 copy-start.5
  0.0 2.9 %shard_map.82 = (f32[256,128]{1,0:T(8,128)}, f32[256,128]{1,0:T(8,128)}, f32[128,128]{1,0:T(8,128)}) custom-call(f32[128,8,256]{2,1,0:T(8,128)} %msa_ref.1, f32[32,256]{1,0:T(8,128)} %bitcast.17, f32[32,256]{1,0:T(8,128)} %bitcast.18, f32[8,2,16,128]{3,2,1,0:T(8,128)} %bitcast.13), custom_call_target="tpu_custom_call" | custom-call | tf_op jit(solution)/shard_map/pallas_call | solution.py:217
  2.9 0.0 copy-start.1
  2.9 1.9 %collective-permute-start.1 = (f32[256,128]{1,0:T(8,128)}, f32[256,128]{1,0:T(8,128)S(1)}, u32[]{:S(2)}, u32[]{:S(2)}) collective-permute-start(f32[256,128]{1,0:T(8,128)} %get-tuple-element.16), channel_id=1, source_target_pairs={{7,0},{37,1},{69,2},{96,3},{135,4},{162,5},{199,6},{224,7},{15,8},... | collective-permute-start | bytes 393224 | tf_op jit(solution)/shard_map/ppermute | solution.py:266
  4.8 8.0 %collective-permute-start.2 = (f32[128,128]{1,0:T(8,128)}, f32[128,128]{1,0:T(8,128)S(1)}, u32[]{:S(2)}, u32[]{:S(2)}) collective-permute-start(f32[128,128]{1,0:T(8,128)} %get-tuple-element.17), channel_id=1, source_target_pairs={{0,16},{16,0},{1,17},{17,1},{2,18},{18,2},{3,19},{19,3},{4,20},{20... | collective-permute-start | bytes 196616 | tf_op jit(solution)/shard_map/ppermute | solution.py:268
  12.8 0.4 collective-permute-start
  13.3 4.1 %collective-permute-done.2.met_pair_ref = f32[128,128]{1,0:T(8,128)S(1)} collective-permute-done((f32[128,128]{1,0:T(8,128)}, f32[128,128]{1,0:T(8,128)S(1)}, u32[]{:S(2)}, u32[]{:S(2)}) %collective-permute-start.2) | collective-permute-done | bytes 65568 | tf_op jit(solution)/shard_map/ppermute | solution.py:268
  17.4 0.0 collective-permute-done.1.panel_ref
  17.4 0.0 collective-permute-start.3
  17.4 0.0 copy-done.5
  17.4 0.1 copy.9
  17.5 0.0 copy-done.1
  17.6 0.0 copy-start
  17.6 0.0 copy-start.2
  17.6 0.3 shard_map.83
  17.9 2.2 %collective-permute-done.met_ref = f32[256,128]{1,0:T(8,128)S(1)} collective-permute-done((f32[256,128]{1,0:T(8,128)}, f32[256,128]{1,0:T(8,128)S(1)}, u32[]{:S(2)}, u32[]{:S(2)}) %collective-permute-start) | collective-permute-done | bytes 131104 | tf_op jit(solution)/shard_map/ppermute | solution.py:267
  20.1 0.0 collective-permute-done.3.sibling_ref
  20.1 0.0 copy-done
  20.1 0.0 copy-done.2
  20.1 1.7 %shard_map.84 = (f32[512,128]{1,0:T(8,128)S(1)}, f32[128,128]{1,0:T(8,128)S(1)}, f32[128,128]{1,0:T(8,128)S(1)}) custom-call(f32[256,128]{1,0:T(8,128)S(1)} %copy-done.2, f32[256,128]{1,0:T(8,128)S(1)} %collective-permute-done.met_ref, f32[128,128]{1,0:T(8,128)S(1)} %collective-permute-done.2.met_pair_ref, f32[256,128]{1,0:T(8,128)S(1)} %collective-permute-done.1.panel_ref, ...), custom_call_target="tpu_custom_call" | custom-call | tf_op jit(solution)/shard_map/pallas_call | solution.py:217
  21.9 19.9 %all_to_all.10 = f32[64,8,128]{2,1,0:T(8,128)S(1)} all-to-all(f32[64,8,128]{2,1,0:T(8,128)S(1)} %bitcast.15), channel_id=1, replica_groups=mesh['z'=8,'yh'=2,'core'=2,'x'=4,'yl'=2] {'x','yl','z'}, dimensions={0} | all-to-all | bytes 524288 | tf_op jit(solution)/shard_map/all_to_all | solution.py:275
  41.8 0.1 collective-permute-start.4
  41.9 1.3 %collective-permute-done.4 = f32[64,4,128]{2,1,0:T(4,128)S(1)} collective-permute-done((f32[64,4,128]{2,1,0:T(4,128)S(1)}, f32[64,4,128]{2,1,0:T(4,128)S(1)}, u32[]{:S(2)}, u32[]{:S(2)}) %collective-permute-start.4) | collective-permute-done | bytes 131104 | tf_op jit(solution)/shard_map/ppermute | solution.py:277
  43.2 1.5 %shard_map.85 = f32[512,128]{1,0:T(8,128)} custom-call(f32[512,128]{1,0:T(8,128)S(1)} %bitcast.10, f32[256,128]{1,0:T(8,128)S(1)} %bitcast.16), custom_call_target="tpu_custom_call" | custom-call | tf_op jit(solution)/shard_map/pallas_call | solution.py:217
  44.7 8.9 %all-to-all-start.1 = ((f32[128,4,128]{2,1,0:T(4,128)}), f32[128,4,128]{2,1,0:T(4,128)S(1)}, u32[]{:S(2)}, u32[]{:S(2)}) async-start(f32[128,4,128]{2,1,0:T(4,128)} %bitcast.7), calls=%async_computation.1 | async-start | bytes 524288 | tf_op jit(solution)/shard_map/all_to_all | solution.py:279
  53.6 3.1 %collective-permute-start.5 = (f32[128,128]{1,0:T(8,128)S(1)}, f32[128,128]{1,0:T(8,128)S(1)}, u32[]{:S(2)}, u32[]{:S(2)}) collective-permute-start(f32[128,128]{1,0:T(8,128)S(1)} %get-tuple-element.24), channel_id=1, source_target_pairs={{0,16},{16,0},{1,17},{17,1},{2,18},{18,2},{3,19},{19,3},{4,20},{20... | collective-permute-start | bytes 196616 | tf_op jit(solution)/shard_map/ppermute | solution.py:276
  56.7 3.2 %collective-permute-done.5.met_ref = f32[128,128]{1,0:T(8,128)S(1)} collective-permute-done((f32[128,128]{1,0:T(8,128)S(1)}, f32[128,128]{1,0:T(8,128)S(1)}, u32[]{:S(2)}, u32[]{:S(2)}) %collective-permute-start.5) | collective-permute-done | bytes 65568 | tf_op jit(solution)/shard_map/ppermute | solution.py:276
  59.9 0.0 copy-done.3
  59.9 0.4 shard_map.86.gates_ref
  60.3 7.6 %all-to-all-done.1 = f32[128,4,128]{2,1,0:T(4,128)S(1)} async-done(((f32[128,4,128]{2,1,0:T(4,128)}), f32[128,4,128]{2,1,0:T(4,128)S(1)}, u32[]{:S(2)}, u32[]{:S(2)}) %all-to-all-start.1) | async-done | bytes 262176 | tf_op jit(solution)/shard_map/all_to_all | solution.py:279
  67.8 0.0 copy-done.4
  67.8 1.0 %shard_map.87 = f32[8,2,16,128]{3,2,1,0:T(8,128)} custom-call(f32[512,128]{1,0:T(8,128)S(1)} %bitcast.12, f32[128,128]{1,0:T(8,128)S(1)} %get-tuple-element.23.kept_ref, f32[128,128]{1,0:T(8,128)S(1)} %collective-permute-done.5.met_ref, f32[2,128,128]{2,1,0:T(8,128)S(1)} %shard_map.86.gates_ref, f32[128,128]{1,0:T(8,128)S(1)} %copy-done.4), custom_call_target="tpu_custom_call" | custom-call | tf_op jit(solution)/shard_map/pallas_call | solution.py:217
  (3 shorter events, 0.0 us)
Async XLA Ops:
  0.0 17.4 %copy-start.5 = (f32[128,512]{1,0:T(8,128)S(1)}, f32[128,512]{1,0:T(8,128)}, u32[]{:S(2)}) copy-start(f32[128,512]{1,0:T(8,128)} %param.13) | copy-start | bytes 786436
  2.9 14.7 %copy-start.1 = (f32[1024,128]{1,0:T(8,128)S(1)}, f32[1024,128]{1,0:T(8,128)}, u32[]{:S(2)}) copy-start(f32[1024,128]{1,0:T(8,128)} %w_outer_ref.1) | copy-start | bytes 1572868
  2.9 14.5 %collective-permute-start.1 = (f32[256,128]{1,0:T(8,128)}, f32[256,128]{1,0:T(8,128)S(1)}, u32[]{:S(2)}, u32[]{:S(2)}) collective-permute-start(f32[256,128]{1,0:T(8,128)} %get-tuple-element.16), channel_id=1, source_target_pairs={{7,0},{37,1},{69,2},{96,3},{135,4},{162,5},{199,6},{224,7},{15,8},... | collective-permute-start | bytes 393224 | tf_op jit(solution)/shard_map/ppermute | solution.py:266
  4.8 12.6 %collective-permute-start.2 = (f32[128,128]{1,0:T(8,128)}, f32[128,128]{1,0:T(8,128)S(1)}, u32[]{:S(2)}, u32[]{:S(2)}) collective-permute-start(f32[128,128]{1,0:T(8,128)} %get-tuple-element.17), channel_id=1, source_target_pairs={{0,16},{16,0},{1,17},{17,1},{2,18},{18,2},{3,19},{19,3},{4,20},{20... | collective-permute-start | bytes 196616 | tf_op jit(solution)/shard_map/ppermute | solution.py:268
  12.8 7.3 %collective-permute-start = (f32[256,128]{1,0:T(8,128)}, f32[256,128]{1,0:T(8,128)S(1)}, u32[]{:S(2)}, u32[]{:S(2)}) collective-permute-start(f32[256,128]{1,0:T(8,128)} %get-tuple-element.15.own_ref), channel_id=1, source_target_pairs={{0,17},{1,16},{16,1},{17,0},{2,19},{3,18},{18,3},{19,2},{4,21},{5,... | collective-permute-start | bytes 393224 | tf_op jit(solution)/shard_map/ppermute | solution.py:267
  17.4 2.7 %collective-permute-start.3 = (f32[256,128]{1,0:T(8,128)S(1)}, f32[256,128]{1,0:T(8,128)S(1)}, u32[]{:S(2)}, u32[]{:S(2)}) collective-permute-start(f32[256,128]{1,0:T(8,128)S(1)} %collective-permute-done.1.panel_ref), channel_id=1, source_target_pairs={{0,8},{8,0},{1,9},{9,1},{2,10},{10,2},{3,11},{11,3},{4,12},{12,4},... | collective-permute-start | bytes 393224 | tf_op jit(solution)/shard_map/ppermute | solution.py:271
  17.6 2.6 %copy-start = (f32[8,32,128]{2,1,0:T(8,128)S(1)}, f32[8,32,128]{2,1,0:T(8,128)}, u32[]{:S(2)}) copy-start(f32[8,32,128]{2,1,0:T(8,128)} %param.9) | copy-start | bytes 393220
  17.6 2.5 %copy-start.2 = (f32[256,128]{1,0:T(8,128)S(1)}, f32[256,128]{1,0:T(8,128)}, u32[]{:S(2)}) copy-start(f32[256,128]{1,0:T(8,128)} %get-tuple-element.15.own_ref) | copy-start | bytes 393220
  41.8 1.4 %collective-permute-start.4 = (f32[64,4,128]{2,1,0:T(4,128)S(1)}, f32[64,4,128]{2,1,0:T(4,128)S(1)}, u32[]{:S(2)}, u32[]{:S(2)}) collective-permute-start(f32[64,4,128]{2,1,0:T(4,128)S(1)} %slice.4), channel_id=1, source_target_pairs={{0,8},{8,0},{1,9},{9,1},{2,10},{10,2},{3,11},{11,3},{4,12},{12,4},... | collective-permute-start | bytes 393224 | tf_op jit(solution)/shard_map/ppermute | solution.py:277
  44.7 15.2 %copy-start.3 = (f32[128,128]{1,0:T(8,128)S(1)}, f32[128,128]{1,0:T(8,128)}, u32[]{:S(2)}) copy-start(f32[128,128]{1,0:T(8,128)} %w_ref.2) | copy-start | bytes 196612
  44.7 23.1 %all-to-all-start.1 = ((f32[128,4,128]{2,1,0:T(4,128)}), f32[128,4,128]{2,1,0:T(4,128)S(1)}, u32[]{:S(2)}, u32[]{:S(2)}) async-start(f32[128,4,128]{2,1,0:T(4,128)} %bitcast.7), calls=%async_computation.1 | async-start | bytes 524288 | tf_op jit(solution)/shard_map/all_to_all | solution.py:279
  53.6 6.2 %collective-permute-start.5 = (f32[128,128]{1,0:T(8,128)S(1)}, f32[128,128]{1,0:T(8,128)S(1)}, u32[]{:S(2)}, u32[]{:S(2)}) collective-permute-start(f32[128,128]{1,0:T(8,128)S(1)} %get-tuple-element.24), channel_id=1, source_target_pairs={{0,16},{16,0},{1,17},{17,1},{2,18},{18,2},{3,19},{19,3},{4,20},{20... | collective-permute-start | bytes 196616 | tf_op jit(solution)/shard_map/ppermute | solution.py:276
  59.9 8.0 %copy-start.4 = (f32[128,128]{1,0:T(8,128)S(1)}, f32[128,128]{1,0:T(8,128)}, u32[]{:S(2)}) copy-start(f32[128,128]{1,0:T(8,128)} %w_ref.3) | copy-start | bytes 196612

commit v13 on v12

--- a/solution.py
+++ b/solution.py
@@ -99,12 +99,6 @@
     for b in range(32):
         outer_ref[pl.ds(b * 32, 32), :] = halves(w_outer_ref[pl.ds(b, 32, stride=32), :])
     tri_ref[...] = halves(w_tri_ref[...])
-
-
-def gate_kernel(kept_ref, met_ref, w_ref, out_ref):
-    w = halves(w_ref[...])
-    for at, ref in enumerate((kept_ref, met_ref)):
-        out_ref[at] = sigmoid(dot_deep(layer_norm(ref[...], -1), w))
 
 
 def pair_kernel(
@@ -192,9 +186,9 @@
                     )
 
 
-def output_kernel(mixed_ref, kept_ref, met_ref, gates_ref, w_ref, out_ref):
+def output_kernel(mixed_ref, kept_ref, met_ref, w_gate_ref, w_ref, out_ref):
     yh = lax.axis_index("yh")
-    w = halves(w_ref[...])
+    w, w_gate = halves(w_ref[...]), halves(w_gate_ref[...])
     for half in range(2):
         tiles = []
         for h in range(2):
@@ -206,7 +200,7 @@
                 tiles.append(parts[0] + parts[1])
         update = dot_deep(layer_norm(jnp.concatenate(tiles, 0), 0).T, w)
         mid = jnp.where(yh == half, kept_ref[...], met_ref[...])
-        gate = jnp.where(yh == half, gates_ref[0], gates_ref[1])
+        gate = sigmoid(dot_deep(layer_norm(mid, -1), w_gate))
         for i in range(8):
             p = turned_rows(i) * 16
             out_ref[i, half] = mid[p : p + 16] + gate[p : p + 16] * update[i * 16 : i * 16 + 16]
@@ -247,12 +241,8 @@
     return call(triangle_kernel, [(512, 128)], [vmem(128, 128), vmem(256, 128)], left, right)
 
 
-def output_stage(mixed, kept, met, gates, w_out):
-    return call(output_kernel, [(8, 2, 16, 128)], [], mixed, kept, met, gates, w_out)
-
-
-def gates_of(kept, met, w_gate):
-    return call(gate_kernel, [(2, 128, 128)], [], kept, met, w_gate)
+def output_stage(*args):
+    return call(output_kernel, [(8, 2, 16, 128)], [], *args)
 
 
 def prepared(w_outer, w_tri):
@@ -273,12 +263,14 @@
         left, met, met_pair, panel, sibling, pair, *weights
     )
     swapped = lax.all_to_all(edges.reshape(64, 8, 128), LAYER, 0, 0, tiled=True)
+    sent, swapped = lax.optimization_barrier((sent, swapped))
+    rights = lax.ppermute(swapped[:, 4:], "core", swap)
     returned = lax.ppermute(sent, "yh", swap)
-    rights = lax.ppermute(swapped[:, 4:], "core", swap)
     back = triangle(swapped.reshape(512, 128), rights.reshape(256, 128))
+    back, returned = lax.optimization_barrier((back, returned))
     mixed = lax.all_to_all(back.reshape(128, 4, 128), CHIPS, 0, 0, tiled=True)
-    gates = gates_of(kept, returned, w_gate)
-    return output_stage(mixed.reshape(512, 128), kept, returned, gates, w_out).reshape(8, 32, 128)
+    out = output_stage(mixed.reshape(512, 128), kept, returned, w_gate, w_out)
+    return out.reshape(8, 32, 128)
 
 
 def solution(mesh):

time: 69.1 us -> 71.6 us (1.036)
  blocking collectives: 19.9 us -> 42.2 us
  starting transfers between devices: 22.4 us -> 12.7 us
  waiting for transfers between devices: 18.4 us -> 9.26 us
  Pallas kernels: 7.8 us -> 6.94 us
    all_to_all x0 -> x1, blocking collectives: none -> 22.3 us  [per_device(): mixed = lax.all_to_all(back.reshape(128, 4, 128), CHIPS, 0, 0, tiled=True)]
    all_to_all x1 -> x0, starting transfers between devices: 8.92 us -> none  [per_device(): mixed = lax.all_to_all(back.reshape(128, 4, 128), CHIPS, 0, 0, tiled=True)]
    all_to_all x1 -> x0, waiting for transfers between devices: 7.58 us -> none  [per_device(): mixed = lax.all_to_all(back.reshape(128, 4, 128), CHIPS, 0, 0, tiled=True)]
    ppermute x1, waiting for transfers between devices: 1.33 us -> 0.01 us  [per_device(): rights = lax.ppermute(swapped[:, 4:], 'core', swap)]
    pallas_call x6 -> x5, Pallas kernels: 7.8 us -> 6.94 us  [call(): pl.pallas_call(kernel, out_shape=shapes if len(shapes) > 1 else shapes[0]...]
    ppermute x1, starting transfers between devices: 3.06 us -> 2.28 us  [per_device(): returned = lax.ppermute(sent, 'yh', swap)]
  transfers between devices with their start and end apart: 7 -> 6, of which waited for: 5 -> 3; matrix products, arithmetic and copies ran while one was open for 0% -> 0% of each run, Pallas kernels for 1% -> 2%
where the time goes in v13:
time: 71.6 us; the launch traced here: 71.4 us
  blocking collectives  42.2 us (59%)
  starting transfers between devices  12.7 us (18%)
  waiting for transfers between devices  9.26 us (13%)
  Pallas kernels  6.94 us (10%)
    all_to_all x1, blocking collectives, per_device(): mixed = lax.all_to_all(back.reshape(128, 4, 128), CHIPS, 0, 0, tiled=True)  22.3 us
    all_to_all x1, blocking collectives, per_device(): swapped = lax.all_to_all(edges.reshape(64, 8, 128), LAYER, 0, 0, tiled=True)  19.9 us
    ppermute x1, starting transfers between devices, per_device(): met_pair = lax.ppermute(half, 'yh', swap)  8.02 us
    pallas_call x5, Pallas kernels, call(): pl.pallas_call(kernel, out_shape=shapes if len(shapes) > 1 else shapes[0]...  6.94 us
    ppermute x1, waiting for transfers between devices, per_device(): met_pair = lax.ppermute(half, 'yh', swap)  4.15 us
    ppermute x1, waiting for transfers between devices, per_device(): returned = lax.ppermute(sent, 'yh', swap)  2.91 us
    ppermute x1, starting transfers between devices, per_device(): returned = lax.ppermute(sent, 'yh', swap)  2.28 us
    ppermute x1, waiting for transfers between devices, per_device(): met = lax.ppermute(left, ('yh', 'yl'), [(0, 3), (1, 2), (2, 1), (3, 0)])  2.2 us
  transfers between devices with their start and end apart: 6, of which 3 were waited for; matrix products, arithmetic and copies ran while one was open for 0% of the time, Pallas kernels for 2%

profile of v13, /device:TPU:2, one launch (start us, length us, event | category | flops | bytes accessed | tf_op | source)
XLA Modules:
  0.0 71.4 jit_solution(16492018204849936868)
XLA Ops:
  0.0 0.0 copy-start.5
  0.0 2.9 %shard_map.82 = (f32[256,128]{1,0:T(8,128)}, f32[256,128]{1,0:T(8,128)}, f32[128,128]{1,0:T(8,128)}) custom-call(f32[128,8,256]{2,1,0:T(8,128)} %msa_ref.1, f32[32,256]{1,0:T(8,128)} %bitcast.18, f32[32,256]{1,0:T(8,128)} %bitcast.19, f32[8,2,16,128]{3,2,1,0:T(8,128)} %bitcast.14), custom_call_target="tpu_custom_call" | custom-call | tf_op jit(solution)/shard_map/pallas_call | solution.py:211
  2.9 0.0 copy-start.1
  2.9 1.9 %collective-permute-start.1 = (f32[256,128]{1,0:T(8,128)}, f32[256,128]{1,0:T(8,128)S(1)}, u32[]{:S(2)}, u32[]{:S(2)}) collective-permute-start(f32[256,128]{1,0:T(8,128)} %get-tuple-element.20), channel_id=1, source_target_pairs={{7,0},{37,1},{69,2},{96,3},{135,4},{162,5},{199,6},{224,7},{15,8},... | collective-permute-start | bytes 393224 | tf_op jit(solution)/shard_map/ppermute | solution.py:256
  4.8 8.0 %collective-permute-start.2 = (f32[128,128]{1,0:T(8,128)}, f32[128,128]{1,0:T(8,128)S(1)}, u32[]{:S(2)}, u32[]{:S(2)}) collective-permute-start(f32[128,128]{1,0:T(8,128)} %get-tuple-element.21), channel_id=1, source_target_pairs={{0,16},{16,0},{1,17},{17,1},{2,18},{18,2},{3,19},{19,3},{4,20},{20... | collective-permute-start | bytes 196616 | tf_op jit(solution)/shard_map/ppermute | solution.py:258
  12.8 0.4 collective-permute-start
  13.3 4.1 %collective-permute-done.2.met_pair_ref = f32[128,128]{1,0:T(8,128)S(1)} collective-permute-done((f32[128,128]{1,0:T(8,128)}, f32[128,128]{1,0:T(8,128)S(1)}, u32[]{:S(2)}, u32[]{:S(2)}) %collective-permute-start.2) | collective-permute-done | bytes 65568 | tf_op jit(solution)/shard_map/ppermute | solution.py:258
  17.4 0.0 collective-permute-done.1.panel_ref
  17.4 0.0 collective-permute-start.3
  17.4 0.0 copy-done.5
  17.4 0.1 copy.9
  17.5 0.0 copy-done.1
  17.6 0.0 copy-start
  17.6 0.0 copy-start.2
  17.6 0.3 shard_map.83
  17.9 2.2 %collective-permute-done.met_ref = f32[256,128]{1,0:T(8,128)S(1)} collective-permute-done((f32[256,128]{1,0:T(8,128)}, f32[256,128]{1,0:T(8,128)S(1)}, u32[]{:S(2)}, u32[]{:S(2)}) %collective-permute-start) | collective-permute-done | bytes 131104 | tf_op jit(solution)/shard_map/ppermute | solution.py:257
  20.1 0.0 collective-permute-done.3.sibling_ref
  20.1 0.0 copy-done
  20.1 0.0 copy-done.2
  20.1 1.7 %shard_map.84 = (f32[512,128]{1,0:T(8,128)S(1)}, f32[128,128]{1,0:T(8,128)S(1)}, f32[128,128]{1,0:T(8,128)S(1)}) custom-call(f32[256,128]{1,0:T(8,128)S(1)} %copy-done.2, f32[256,128]{1,0:T(8,128)S(1)} %collective-permute-done.met_ref, f32[128,128]{1,0:T(8,128)S(1)} %collective-permute-done.2.met_pair_ref, f32[256,128]{1,0:T(8,128)S(1)} %collective-permute-done.1.panel_ref, ...), custom_call_target="tpu_custom_call" | custom-call | tf_op jit(solution)/shard_map/pallas_call | solution.py:211
  21.9 19.9 %all_to_all.10 = f32[64,8,128]{2,1,0:T(8,128)S(1)} all-to-all(f32[64,8,128]{2,1,0:T(8,128)S(1)} %bitcast.16), channel_id=1, replica_groups=mesh['z'=8,'yh'=2,'core'=2,'x'=4,'yl'=2] {'x','yl','z'}, dimensions={0} | all-to-all | bytes 524288 | tf_op jit(solution)/shard_map/all_to_all | solution.py:265
  41.8 0.1 collective-permute-start.4
  41.9 2.3 %collective-permute-start.5 = (f32[128,128]{1,0:T(8,128)S(1)}, f32[128,128]{1,0:T(8,128)S(1)}, u32[]{:S(2)}, u32[]{:S(2)}) collective-permute-start(f32[128,128]{1,0:T(8,128)S(1)} %get-tuple-element.29), channel_id=1, source_target_pairs={{0,16},{16,0},{1,17},{17,1},{2,18},{18,2},{3,19},{19,3},{4,20},{20... | collective-permute-start | bytes 196616 | tf_op jit(solution)/shard_map/ppermute | solution.py:268
  44.2 0.0 collective-permute-done.4
  44.2 0.8 %shard_map.85 = f32[512,128]{1,0:T(8,128)S(1)} custom-call(f32[512,128]{1,0:T(8,128)S(1)} %bitcast.10, f32[256,128]{1,0:T(8,128)S(1)} %bitcast.17), custom_call_target="tpu_custom_call" | custom-call | tf_op jit(solution)/shard_map/pallas_call | solution.py:211
  45.0 2.9 %collective-permute-done.5.met_ref = f32[128,128]{1,0:T(8,128)S(1)} collective-permute-done((f32[128,128]{1,0:T(8,128)S(1)}, f32[128,128]{1,0:T(8,128)S(1)}, u32[]{:S(2)}, u32[]{:S(2)}) %collective-permute-start.5) | collective-permute-done | bytes 65568 | tf_op jit(solution)/shard_map/ppermute | solution.py:268
  47.9 0.0 copy-start.3
  47.9 0.0 copy-start.4
  47.9 22.3 %all_to_all.11 = f32[128,4,128]{2,1,0:T(4,128)S(1)} all-to-all(f32[128,4,128]{2,1,0:T(4,128)S(1)} %bitcast.12), channel_id=1, replica_groups=mesh['z'=8,'yh'=2,'core'=2,'x'=4,'yl'=2] {'x','yl','z','yh'}, dimensions={0} | all-to-all | bytes 524288 | tf_op jit(solution)/shard_map/all_to_all | solution.py:271
  70.2 0.0 copy-done.3
  70.2 0.0 copy-done.4
  70.2 1.2 %shard_map.86 = f32[8,2,16,128]{3,2,1,0:T(8,128)} custom-call(f32[512,128]{1,0:T(8,128)S(1)} %bitcast.13, f32[128,128]{1,0:T(8,128)S(1)} %get-tuple-element.31.kept_ref, f32[128,128]{1,0:T(8,128)S(1)} %collective-permute-done.5.met_ref, f32[128,128]{1,0:T(8,128)S(1)} %copy-done.3, f32[128,128]{1,0:T(8,128)S(1)} %copy-done.4), custom_call_target="tpu_custom_call" | custom-call | tf_op jit(solution)/shard_map/pallas_call | solution.py:211
  (1 shorter events, 0.0 us)
Async XLA Ops:
  0.0 17.4 %copy-start.5 = (f32[128,512]{1,0:T(8,128)S(1)}, f32[128,512]{1,0:T(8,128)}, u32[]{:S(2)}) copy-start(f32[128,512]{1,0:T(8,128)} %param.13) | copy-start | bytes 786436
  2.9 14.7 %copy-start.1 = (f32[1024,128]{1,0:T(8,128)S(1)}, f32[1024,128]{1,0:T(8,128)}, u32[]{:S(2)}) copy-start(f32[1024,128]{1,0:T(8,128)} %w_outer_ref.1) | copy-start | bytes 1572868
  2.9 14.5 %collective-permute-start.1 = (f32[256,128]{1,0:T(8,128)}, f32[256,128]{1,0:T(8,128)S(1)}, u32[]{:S(2)}, u32[]{:S(2)}) collective-permute-start(f32[256,128]{1,0:T(8,128)} %get-tuple-element.20), channel_id=1, source_target_pairs={{7,0},{37,1},{69,2},{96,3},{135,4},{162,5},{199,6},{224,7},{15,8},... | collective-permute-start | bytes 393224 | tf_op jit(solution)/shard_map/ppermute | solution.py:256
  4.8 12.6 %collective-permute-start.2 = (f32[128,128]{1,0:T(8,128)}, f32[128,128]{1,0:T(8,128)S(1)}, u32[]{:S(2)}, u32[]{:S(2)}) collective-permute-start(f32[128,128]{1,0:T(8,128)} %get-tuple-element.21), channel_id=1, source_target_pairs={{0,16},{16,0},{1,17},{17,1},{2,18},{18,2},{3,19},{19,3},{4,20},{20... | collective-permute-start | bytes 196616 | tf_op jit(solution)/shard_map/ppermute | solution.py:258
  12.8 7.3 %collective-permute-start = (f32[256,128]{1,0:T(8,128)}, f32[256,128]{1,0:T(8,128)S(1)}, u32[]{:S(2)}, u32[]{:S(2)}) collective-permute-start(f32[256,128]{1,0:T(8,128)} %get-tuple-element.19.own_ref), channel_id=1, source_target_pairs={{0,17},{1,16},{16,1},{17,0},{2,19},{3,18},{18,3},{19,2},{4,21},{5,... | collective-permute-start | bytes 393224 | tf_op jit(solution)/shard_map/ppermute | solution.py:257
  17.4 2.7 %collective-permute-start.3 = (f32[256,128]{1,0:T(8,128)S(1)}, f32[256,128]{1,0:T(8,128)S(1)}, u32[]{:S(2)}, u32[]{:S(2)}) collective-permute-start(f32[256,128]{1,0:T(8,128)S(1)} %collective-permute-done.1.panel_ref), channel_id=1, source_target_pairs={{0,8},{8,0},{1,9},{9,1},{2,10},{10,2},{3,11},{11,3},{4,12},{12,4},... | collective-permute-start | bytes 393224 | tf_op jit(solution)/shard_map/ppermute | solution.py:261
  17.6 2.6 %copy-start = (f32[8,32,128]{2,1,0:T(8,128)S(1)}, f32[8,32,128]{2,1,0:T(8,128)}, u32[]{:S(2)}) copy-start(f32[8,32,128]{2,1,0:T(8,128)} %param.9) | copy-start | bytes 393220
  17.6 2.5 %copy-start.2 = (f32[256,128]{1,0:T(8,128)S(1)}, f32[256,128]{1,0:T(8,128)}, u32[]{:S(2)}) copy-start(f32[256,128]{1,0:T(8,128)} %get-tuple-element.19.own_ref) | copy-start | bytes 393220
  41.8 2.4 %collective-permute-start.4 = (f32[64,4,128]{2,1,0:T(4,128)S(1)}, f32[64,4,128]{2,1,0:T(4,128)S(1)}, u32[]{:S(2)}, u32[]{:S(2)}) collective-permute-start(f32[64,4,128]{2,1,0:T(4,128)S(1)} %slice.3), channel_id=1, source_target_pairs={{0,8},{8,0},{1,9},{9,1},{2,10},{10,2},{3,11},{11,3},{4,12},{12,4},... | collective-permute-start | bytes 393224 | tf_op jit(solution)/shard_map/ppermute | solution.py:267
  41.9 6.0 %collective-permute-start.5 = (f32[128,128]{1,0:T(8,128)S(1)}, f32[128,128]{1,0:T(8,128)S(1)}, u32[]{:S(2)}, u32[]{:S(2)}) collective-permute-start(f32[128,128]{1,0:T(8,128)S(1)} %get-tuple-element.29), channel_id=1, source_target_pairs={{0,16},{16,0},{1,17},{17,1},{2,18},{18,2},{3,19},{19,3},{4,20},{20... | collective-permute-start | bytes 196616 | tf_op jit(solution)/shard_map/ppermute | solution.py:268
  47.9 22.3 %copy-start.3 = (f32[128,128]{1,0:T(8,128)S(1)}, f32[128,128]{1,0:T(8,128)}, u32[]{:S(2)}) copy-start(f32[128,128]{1,0:T(8,128)} %w_gate_ref.1) | copy-start | bytes 196612
  47.9 22.3 %copy-start.4 = (f32[128,128]{1,0:T(8,128)S(1)}, f32[128,128]{1,0:T(8,128)}, u32[]{:S(2)}) copy-start(f32[128,128]{1,0:T(8,128)} %w_ref.1) | copy-start | bytes 196612

commit v14 on v11

--- a/solution.py
+++ b/solution.py
@@ -16,8 +16,14 @@
 
 
 PANEL_COLUMNS = (
-    (72361054, 54671032, 53160427, 1764253, 74562031, 25647103, 76045231, 5476312),
-    (61053247, 45671032, 30176425, 62347501, 34205176, 50761342, 42635701, 4276513),
+    (
+        (47531062, 7463125, 12675430, 67140253, 74126350, 60453721, 3265714, 23074165),
+        (13652047, 14520376, 43051627, 42673015, 30546172, 25017436, 47162053, 14732506),
+    ),
+    (
+        (74520136, 54763120, 71653042, 76402153, 74210356, 20456137, 3574216, 12067543),
+        (61732045, 13256074, 36025714, 7241635, 34765012, 21350467, 24137605, 73150246),
+    ),
 )
 
 
@@ -27,7 +33,7 @@
         for yh in range(2):
             for core in range(2):
                 for c in range(8):
-                    column = PANEL_COLUMNS[yh][c] // 10 ** (7 - z) % 10
+                    column = PANEL_COLUMNS[yh][core][c] // 10 ** (7 - z) % 10
                     source = ((c * 2 + yh) * 2 + core) * 8 + column
                     pairs.append((source, ((z * 2 + yh) * 2 + core) * 8 + c))
     return pairs

time: 68.9 us -> 68.8 us (level)
  waiting for transfers between devices: 18.7 us -> 17.1 us
  blocking collectives: 20 us -> 21.4 us
    ppermute x1, starting transfers between devices: 8.02 us -> 1.96 us  [per_device(): met_pair = lax.ppermute(half, 'yh', swap)]
    ppermute x1, starting transfers between devices: 1.89 us -> 5.83 us  [per_device(): panel = lax.ppermute(right, ALL, panel_permutation())]
    all_to_all x1, blocking collectives: 20 us -> 21.4 us  [per_device(): swapped = lax.all_to_all(edges.reshape(64, 8, 128), LAYER, 0, 0, tiled=True)]
    ppermute x1, starting transfers between devices: 0.45 us -> 1.68 us  [per_device(): met = lax.ppermute(left, ('yh', 'yl'), [(0, 3), (1, 2), (2, 1), (3, 0)])]
    ppermute x1, waiting for transfers between devices: 4.15 us -> 2.96 us  [per_device(): met_pair = lax.ppermute(half, 'yh', swap)]
    all_to_all x1, starting transfers between devices: 8.49 us -> 9.44 us  [per_device(): mixed = lax.all_to_all(back.reshape(128, 4, 128), CHIPS, 0, 0, tiled=True)]
where the time goes in v14:
time: 68.8 us; the launch traced here: 68.5 us
  starting transfers between devices  22.1 us (32%)
  blocking collectives  21.4 us (31%)
  waiting for transfers between devices  17.1 us (25%)
  Pallas kernels  7.68 us (11%)
    all_to_all x1, blocking collectives, per_device(): swapped = lax.all_to_all(edges.reshape(64, 8, 128), LAYER, 0, 0, tiled=True)  21.4 us
    all_to_all x1, starting transfers between devices, per_device(): mixed = lax.all_to_all(back.reshape(128, 4, 128), CHIPS, 0, 0, tiled=True)  9.44 us
    pallas_call x6, Pallas kernels, call(): pl.pallas_call(kernel, out_shape=shapes if len(shapes) > 1 else shapes[0]...  7.68 us
    all_to_all x1, waiting for transfers between devices, per_device(): mixed = lax.all_to_all(back.reshape(128, 4, 128), CHIPS, 0, 0, tiled=True)  7.67 us
    ppermute x1, starting transfers between devices, per_device(): panel = lax.ppermute(right, ALL, panel_permutation())  5.83 us
    ppermute x1, waiting for transfers between devices, per_device(): returned = lax.ppermute(sent, 'yh', swap)  3.34 us
    ppermute x1, starting transfers between devices, per_device(): returned = lax.ppermute(sent, 'yh', swap)  3.06 us
    ppermute x1, waiting for transfers between devices, per_device(): met_pair = lax.ppermute(half, 'yh', swap)  2.96 us
  transfers between devices with their start and end apart: 7, of which 5 were waited for; matrix products, arithmetic and copies ran while one was open for 0% of the time, Pallas kernels for 1%

profile of v14, /device:TPU:2, one launch (start us, length us, event | category | flops | bytes accessed | tf_op | source)
XLA Modules:
  0.0 68.5 jit_solution(17624858667963781903)
XLA Ops:
  0.0 0.0 copy-start.5
  0.0 2.9 %shard_map.82 = (f32[256,128]{1,0:T(8,128)}, f32[256,128]{1,0:T(8,128)}, f32[128,128]{1,0:T(8,128)}) custom-call(f32[128,8,256]{2,1,0:T(8,128)} %msa_ref.1, f32[32,256]{1,0:T(8,128)} %bitcast.17, f32[32,256]{1,0:T(8,128)} %bitcast.18, f32[8,2,16,128]{3,2,1,0:T(8,128)} %bitcast.13), custom_call_target="tpu_custom_call" | custom-call | tf_op jit(solution)/shard_map/pallas_call | solution.py:223
  2.9 0.0 copy-start.1
  2.9 5.8 %collective-permute-start.1 = (f32[256,128]{1,0:T(8,128)}, f32[256,128]{1,0:T(8,128)S(1)}, u32[]{:S(2)}, u32[]{:S(2)}) collective-permute-start(f32[256,128]{1,0:T(8,128)} %get-tuple-element.16), channel_id=1, source_target_pairs={{4,0},{32,1},{65,2},{102,3},{135,4},{166,5},{192,6},{226,7},{9,8},... | collective-permute-start | bytes 393224 | tf_op jit(solution)/shard_map/ppermute | solution.py:272
  8.7 2.0 %collective-permute-start.2 = (f32[128,128]{1,0:T(8,128)}, f32[128,128]{1,0:T(8,128)S(1)}, u32[]{:S(2)}, u32[]{:S(2)}) collective-permute-start(f32[128,128]{1,0:T(8,128)} %get-tuple-element.17), channel_id=1, source_target_pairs={{0,16},{16,0},{1,17},{17,1},{2,18},{18,2},{3,19},{19,3},{4,20},{20... | collective-permute-start | bytes 196616 | tf_op jit(solution)/shard_map/ppermute | solution.py:274
  10.7 1.7 %collective-permute-start = (f32[256,128]{1,0:T(8,128)}, f32[256,128]{1,0:T(8,128)S(1)}, u32[]{:S(2)}, u32[]{:S(2)}) collective-permute-start(f32[256,128]{1,0:T(8,128)} %get-tuple-element.15.own_ref), channel_id=1, source_target_pairs={{0,17},{1,16},{16,1},{17,0},{2,19},{3,18},{18,3},{19,2},{4,21},{5,... | collective-permute-start | bytes 393224 | tf_op jit(solution)/shard_map/ppermute | solution.py:273
  12.4 3.0 %collective-permute-done.2.met_pair_ref = f32[128,128]{1,0:T(8,128)S(1)} collective-permute-done((f32[128,128]{1,0:T(8,128)}, f32[128,128]{1,0:T(8,128)S(1)}, u32[]{:S(2)}, u32[]{:S(2)}) %collective-permute-start.2) | collective-permute-done | bytes 65568 | tf_op jit(solution)/shard_map/ppermute | solution.py:274
  15.3 0.0 collective-permute-done.1.panel_ref
  15.3 0.0 collective-permute-start.3
  15.4 0.0 copy-done.5
  15.4 0.1 copy.9
  15.5 0.0 copy-done.1
  15.5 0.0 copy-start
  15.5 0.0 copy-start.2
  15.5 0.3 shard_map.83
  15.9 1.8 %collective-permute-done.met_ref = f32[256,128]{1,0:T(8,128)S(1)} collective-permute-done((f32[256,128]{1,0:T(8,128)}, f32[256,128]{1,0:T(8,128)S(1)}, u32[]{:S(2)}, u32[]{:S(2)}) %collective-permute-start) | collective-permute-done | bytes 131104 | tf_op jit(solution)/shard_map/ppermute | solution.py:273
  17.6 0.0 collective-permute-done.3.sibling_ref
  17.6 0.0 copy-done
  17.6 0.0 copy-done.2
  17.6 1.7 %shard_map.84 = (f32[512,128]{1,0:T(8,128)S(1)}, f32[128,128]{1,0:T(8,128)S(1)}, f32[128,128]{1,0:T(8,128)S(1)}) custom-call(f32[256,128]{1,0:T(8,128)S(1)} %copy-done.2, f32[256,128]{1,0:T(8,128)S(1)} %collective-permute-done.met_ref, f32[128,128]{1,0:T(8,128)S(1)} %collective-permute-done.2.met_pair_ref, f32[256,128]{1,0:T(8,128)S(1)} %collective-permute-done.1.panel_ref, ...), custom_call_target="tpu_custom_call" | custom-call | tf_op jit(solution)/shard_map/pallas_call | solution.py:223
  19.4 21.4 %all_to_all.10 = f32[64,8,128]{2,1,0:T(8,128)S(1)} all-to-all(f32[64,8,128]{2,1,0:T(8,128)S(1)} %bitcast.15), channel_id=1, replica_groups=mesh['z'=8,'yh'=2,'core'=2,'x'=4,'yl'=2] {'z','x','yl'}, dimensions={0} | all-to-all | bytes 524288 | tf_op jit(solution)/shard_map/all_to_all | solution.py:281
  40.8 0.1 collective-permute-start.4
  40.9 1.3 %collective-permute-done.4 = f32[64,4,128]{2,1,0:T(4,128)S(1)} collective-permute-done((f32[64,4,128]{2,1,0:T(4,128)S(1)}, f32[64,4,128]{2,1,0:T(4,128)S(1)}, u32[]{:S(2)}, u32[]{:S(2)}) %collective-permute-start.4) | collective-permute-done | bytes 131104 | tf_op jit(solution)/shard_map/ppermute | solution.py:283
  42.2 1.4 %shard_map.85 = f32[512,128]{1,0:T(8,128)} custom-call(f32[512,128]{1,0:T(8,128)S(1)} %bitcast.10, f32[256,128]{1,0:T(8,128)S(1)} %bitcast.16), custom_call_target="tpu_custom_call" | custom-call | tf_op jit(solution)/shard_map/pallas_call | solution.py:223
  43.6 9.4 %all-to-all-start.1 = ((f32[128,4,128]{2,1,0:T(4,128)}), f32[128,4,128]{2,1,0:T(4,128)S(1)}, u32[]{:S(2)}, u32[]{:S(2)}) async-start(f32[128,4,128]{2,1,0:T(4,128)} %bitcast.7), calls=%async_computation.1 | async-start | bytes 524288 | tf_op jit(solution)/shard_map/all_to_all | solution.py:285
  53.1 3.1 %collective-permute-start.5 = (f32[128,128]{1,0:T(8,128)S(1)}, f32[128,128]{1,0:T(8,128)S(1)}, u32[]{:S(2)}, u32[]{:S(2)}) collective-permute-start(f32[128,128]{1,0:T(8,128)S(1)} %get-tuple-element.24), channel_id=1, source_target_pairs={{0,16},{16,0},{1,17},{17,1},{2,18},{18,2},{3,19},{19,3},{4,20},{20... | collective-permute-start | bytes 196616 | tf_op jit(solution)/shard_map/ppermute | solution.py:282
  56.1 3.3 %collective-permute-done.5.met_ref = f32[128,128]{1,0:T(8,128)S(1)} collective-permute-done((f32[128,128]{1,0:T(8,128)S(1)}, f32[128,128]{1,0:T(8,128)S(1)}, u32[]{:S(2)}, u32[]{:S(2)}) %collective-permute-start.5) | collective-permute-done | bytes 65568 | tf_op jit(solution)/shard_map/ppermute | solution.py:282
  59.5 0.0 copy-done.3
  59.5 0.4 shard_map.86.gates_ref
  59.8 7.7 %all-to-all-done.1 = f32[128,4,128]{2,1,0:T(4,128)S(1)} async-done(((f32[128,4,128]{2,1,0:T(4,128)}), f32[128,4,128]{2,1,0:T(4,128)S(1)}, u32[]{:S(2)}, u32[]{:S(2)}) %all-to-all-start.1) | async-done | bytes 262176 | tf_op jit(solution)/shard_map/all_to_all | solution.py:285
  67.5 0.0 copy-done.4
  67.5 1.0 %shard_map.87 = f32[8,2,16,128]{3,2,1,0:T(8,128)} custom-call(f32[512,128]{1,0:T(8,128)S(1)} %bitcast.12, f32[128,128]{1,0:T(8,128)S(1)} %get-tuple-element.23.kept_ref, f32[128,128]{1,0:T(8,128)S(1)} %collective-permute-done.5.met_ref, f32[2,128,128]{2,1,0:T(8,128)S(1)} %shard_map.86.gates_ref, f32[128,128]{1,0:T(8,128)S(1)} %copy-done.4), custom_call_target="tpu_custom_call" | custom-call | tf_op jit(solution)/shard_map/pallas_call | solution.py:223
  (3 shorter events, 0.0 us)
Async XLA Ops:
  0.0 15.4 %copy-start.5 = (f32[128,512]{1,0:T(8,128)S(1)}, f32[128,512]{1,0:T(8,128)}, u32[]{:S(2)}) copy-start(f32[128,512]{1,0:T(8,128)} %param.13) | copy-start | bytes 786436
  2.9 12.6 %copy-start.1 = (f32[1024,128]{1,0:T(8,128)S(1)}, f32[1024,128]{1,0:T(8,128)}, u32[]{:S(2)}) copy-start(f32[1024,128]{1,0:T(8,128)} %w_outer_ref.1) | copy-start | bytes 1572868
  2.9 12.4 %collective-permute-start.1 = (f32[256,128]{1,0:T(8,128)}, f32[256,128]{1,0:T(8,128)S(1)}, u32[]{:S(2)}, u32[]{:S(2)}) collective-permute-start(f32[256,128]{1,0:T(8,128)} %get-tuple-element.16), channel_id=1, source_target_pairs={{4,0},{32,1},{65,2},{102,3},{135,4},{166,5},{192,6},{226,7},{9,8},... | collective-permute-start | bytes 393224 | tf_op jit(solution)/shard_map/ppermute | solution.py:272
  8.7 6.6 %collective-permute-start.2 = (f32[128,128]{1,0:T(8,128)}, f32[128,128]{1,0:T(8,128)S(1)}, u32[]{:S(2)}, u32[]{:S(2)}) collective-permute-start(f32[128,128]{1,0:T(8,128)} %get-tuple-element.17), channel_id=1, source_target_pairs={{0,16},{16,0},{1,17},{17,1},{2,18},{18,2},{3,19},{19,3},{4,20},{20... | collective-permute-start | bytes 196616 | tf_op jit(solution)/shard_map/ppermute | solution.py:274
  10.7 6.9 %collective-permute-start = (f32[256,128]{1,0:T(8,128)}, f32[256,128]{1,0:T(8,128)S(1)}, u32[]{:S(2)}, u32[]{:S(2)}) collective-permute-start(f32[256,128]{1,0:T(8,128)} %get-tuple-element.15.own_ref), channel_id=1, source_target_pairs={{0,17},{1,16},{16,1},{17,0},{2,19},{3,18},{18,3},{19,2},{4,21},{5,... | collective-permute-start | bytes 393224 | tf_op jit(solution)/shard_map/ppermute | solution.py:273
  15.3 2.3 %collective-permute-start.3 = (f32[256,128]{1,0:T(8,128)S(1)}, f32[256,128]{1,0:T(8,128)S(1)}, u32[]{:S(2)}, u32[]{:S(2)}) collective-permute-start(f32[256,128]{1,0:T(8,128)S(1)} %collective-permute-done.1.panel_ref), channel_id=1, source_target_pairs={{0,8},{8,0},{1,9},{9,1},{2,10},{10,2},{3,11},{11,3},{4,12},{12,4},... | collective-permute-start | bytes 393224 | tf_op jit(solution)/shard_map/ppermute | solution.py:277
  15.5 2.1 %copy-start = (f32[8,32,128]{2,1,0:T(8,128)S(1)}, f32[8,32,128]{2,1,0:T(8,128)}, u32[]{:S(2)}) copy-start(f32[8,32,128]{2,1,0:T(8,128)} %param.9) | copy-start | bytes 393220
  15.5 2.1 %copy-start.2 = (f32[256,128]{1,0:T(8,128)S(1)}, f32[256,128]{1,0:T(8,128)}, u32[]{:S(2)}) copy-start(f32[256,128]{1,0:T(8,128)} %get-tuple-element.15.own_ref) | copy-start | bytes 393220
  40.8 1.4 %collective-permute-start.4 = (f32[64,4,128]{2,1,0:T(4,128)S(1)}, f32[64,4,128]{2,1,0:T(4,128)S(1)}, u32[]{:S(2)}, u32[]{:S(2)}) collective-permute-start(f32[64,4,128]{2,1,0:T(4,128)S(1)} %slice.4), channel_id=1, source_target_pairs={{0,8},{8,0},{1,9},{9,1},{2,10},{10,2},{3,11},{11,3},{4,12},{12,4},... | collective-permute-start | bytes 393224 | tf_op jit(solution)/shard_map/ppermute | solution.py:283
  43.6 15.9 %copy-start.3 = (f32[128,128]{1,0:T(8,128)S(1)}, f32[128,128]{1,0:T(8,128)}, u32[]{:S(2)}) copy-start(f32[128,128]{1,0:T(8,128)} %w_ref.2) | copy-start | bytes 196612
  43.6 23.9 %all-to-all-start.1 = ((f32[128,4,128]{2,1,0:T(4,128)}), f32[128,4,128]{2,1,0:T(4,128)S(1)}, u32[]{:S(2)}, u32[]{:S(2)}) async-start(f32[128,4,128]{2,1,0:T(4,128)} %bitcast.7), calls=%async_computation.1 | async-start | bytes 524288 | tf_op jit(solution)/shard_map/all_to_all | solution.py:285
  53.1 6.4 %collective-permute-start.5 = (f32[128,128]{1,0:T(8,128)S(1)}, f32[128,128]{1,0:T(8,128)S(1)}, u32[]{:S(2)}, u32[]{:S(2)}) collective-permute-start(f32[128,128]{1,0:T(8,128)S(1)} %get-tuple-element.24), channel_id=1, source_target_pairs={{0,16},{16,0},{1,17},{17,1},{2,18},{18,2},{3,19},{19,3},{4,20},{20... | collective-permute-start | bytes 196616 | tf_op jit(solution)/shard_map/ppermute | solution.py:282
  59.5 8.0 %copy-start.4 = (f32[128,128]{1,0:T(8,128)S(1)}, f32[128,128]{1,0:T(8,128)}, u32[]{:S(2)}) copy-start(f32[128,128]{1,0:T(8,128)} %w_ref.3) | copy-start | bytes 196612

commit v15 on v14

--- a/solution.py
+++ b/solution.py
@@ -113,44 +113,50 @@
         out_ref[at] = sigmoid(dot_deep(layer_norm(ref[...], -1), w))
 
 
+def project_block(left, panel, w_outer, outer_ref, flat_ref):
+    outer_ref[...] = dot_t(halves(panel), left)
+    lane = lax.broadcasted_iota(jnp.int32, (8, 128), 1)
+    low_half = lane < 64
+    even = (lane // 32) % 2 == 0
+    for bh in range(8):
+        for ih in range(4):
+            v = [
+                outer_ref[pl.ds((bh * 4 + b) * 8, 8), pl.ds(ih * 128, 128)] for b in range(4)
+            ]
+            for p in range(2):
+                a, c = v[p], v[p + 2]
+                v[p] = jnp.where(low_half, a, pltpu.roll(c, 64, 1))
+                v[p + 2] = jnp.where(low_half, pltpu.roll(a, 64, 1), c)
+            for p in (0, 2):
+                a, c = v[p], v[p + 1]
+                v[p] = jnp.where(even, a, pltpu.roll(c, 32, 1))
+                v[p + 1] = jnp.where(even, pltpu.roll(a, 96, 1), c)
+            for il in range(4):
+                row = ih // 2 * 64 + turned_rows(ih % 2 * 4 + il) * 8
+                flat_ref[pl.ds(row, 8), pl.ds(bh * 128, 128)] = v[il]
+    return dot_deep(flat_ref[...], w_outer)
+
+
+def block_kernel(own_ref, met_ref, panel_ref, w_outer_ref, update_ref, outer_ref, flat_ref):
+    left = jnp.concatenate([own_ref[...], met_ref[...]], 0)
+    update_ref[...] = project_block(left, panel_ref[...], w_outer_ref[...], outer_ref, flat_ref)
+
+
 def pair_kernel(
-    own_ref, met_ref, met_pair_ref, panel_ref, sibling_ref, pair_ref, w_outer_ref, w_tri_ref,
+    own_ref, met_ref, met_pair_ref, sibling_ref, update_ref, pair_ref, w_outer_ref, w_tri_ref,
     edges_ref, kept_ref, sent_ref, outer_ref, flat_ref,
 ):
     yh = lax.axis_index("yh")
+    first = lax.axis_index("core") == 0
     left = jnp.concatenate([own_ref[...], met_ref[...]], 0)
-    first = lax.axis_index("core") == 0
-    panel, sibling = panel_ref[...], sibling_ref[...]
-    panels = jnp.concatenate(
-        [jnp.where(first, panel, sibling), jnp.where(first, sibling, panel)], 0
-    )
-    outer_ref[...] = dot_t(halves(panels), left)
-    lane = lax.broadcasted_iota(jnp.int32, (8, 128), 1)
-    low_half = lane < 64
-    even = (lane // 32) % 2 == 0
-    for o in range(2):
-        for bh in range(8):
-            for ih in range(4):
-                v = [
-                    outer_ref[pl.ds((o * 32 + bh * 4 + b) * 8, 8), pl.ds(ih * 128, 128)]
-                    for b in range(4)
-                ]
-                for p in range(2):
-                    a, c = v[p], v[p + 2]
-                    v[p] = jnp.where(low_half, a, pltpu.roll(c, 64, 1))
-                    v[p + 2] = jnp.where(low_half, pltpu.roll(a, 64, 1), c)
-                for p in (0, 2):
-                    a, c = v[p], v[p + 1]
-                    v[p] = jnp.where(even, a, pltpu.roll(c, 32, 1))
-                    v[p + 1] = jnp.where(even, pltpu.roll(a, 96, 1), c)
-                for il in range(4):
-                    i = ih % 2 * 4 + il
-                    row = ih // 2 * 128 + turned_rows(i) * 16 + o * 8
-                    flat_ref[pl.ds(row, 8), pl.ds(bh * 128, 128)] = v[il]
+    other = project_block(left, sibling_ref[...], w_outer_ref[...], outer_ref, flat_ref)
+    mine = update_ref[...]
+    blocks = jnp.where(first, mine, other), jnp.where(first, other, mine)
+    update = [block[t * 8 : t * 8 + 8] for t in range(16) for block in blocks]
     pair = jnp.concatenate(
         [pair_ref[turned_rows(p), yh] for p in range(8)] + [met_pair_ref[...]], 0
     )
-    mid = pair + dot_deep(flat_ref[...], w_outer_ref[...])
+    mid = pair + jnp.concatenate(update, 0)
     normed = layer_norm(mid, -1)
     projected = dot_t(w_tri_ref[...], normed)
     for side in range(2):
@@ -172,23 +178,35 @@
     return pltpu.roll(x, 0, 1, stride=16, stride_axis=0)
 
 
-def triangle_kernel(left_ref, right_ref, out_ref, l_ref, r_ref):
-    core = lax.axis_index("core")
+def block_masks():
     lane = lax.broadcasted_iota(jnp.int32, (8, 128), 1)
-    masks = [(lane // 16) & bit != 0 for bit in (1, 2, 4)]
+    return [(lane // 16) & bit != 0 for bit in (1, 2, 4)]
+
+
+def own_kernel(edges_ref, l_ref, r_ref):
+    masks = block_masks()
     for h in range(2):
         for z in range(8):
             for y in range(2):
-                x = left_ref[pl.ds(z * 64 + h * 2 + y, 8, stride=8), :]
-                l_ref[pl.ds(y * 64 + z * 8, 8), :] = turn_blocks(x, masks)
-                x = left_ref[pl.ds(z * 64 + (2 + h) * 2 + y, 8, stride=8), :]
-                own = turn_blocks(x, masks)
+                x = edges_ref[pl.ds(z * 64 + h * 2 + y, 8, stride=8), :]
+                l_ref[h, pl.ds(y * 64 + z * 8, 8), :] = turn_blocks(x, masks)
+                x = edges_ref[pl.ds(z * 64 + (2 + h) * 2 + y, 8, stride=8), :]
+                r_ref[h, pl.ds(y * 64 + turned_rows(z) * 8, 8), :] = turn_blocks(x, masks)
+
+
+def triangle_kernel(l_ref, own_ref, right_ref, out_ref, r_ref):
+    masks = block_masks()
+    first = lax.axis_index("core") == 0
+    for h in range(2):
+        for z in range(8):
+            for y in range(2):
                 x = right_ref[pl.ds(z * 32 + h * 2 + y, 8, stride=4), :]
                 other = turn_blocks(x, masks)
-                row = y * 128 + turned_rows(z) * 16
-                r_ref[pl.ds(row, 8), :] = jnp.where(core == 0, own, other)
-                r_ref[pl.ds(row + 8, 8), :] = jnp.where(core == 0, other, own)
-        mixed = dot_t(halves(l_ref[...]), r_ref[...])
+                at = y * 64 + turned_rows(z) * 8
+                own = own_ref[h, pl.ds(at, 8), :]
+                r_ref[pl.ds(at * 2, 8), :] = jnp.where(first, own, other)
+                r_ref[pl.ds(at * 2 + 8, 8), :] = jnp.where(first, other, own)
+        mixed = dot_t(halves(l_ref[h]), r_ref[...])
         for z in range(8):
             for y in range(2):
                 for half in range(2):
@@ -240,17 +258,25 @@
     )
 
 
+def block_update(*args):
+    return call(block_kernel, [(128, 128)], [vmem(256, 512), vmem(128, 1024)], *args)
+
+
 def pair_stage(*args):
     return call(
         pair_kernel,
         [(512, 128), (128, 128), (128, 128)],
-        [vmem(512, 512), vmem(256, 1024)],
+        [vmem(256, 512), vmem(128, 1024)],
         *args,
     )
 
 
-def triangle(left, right):
-    return call(triangle_kernel, [(512, 128)], [vmem(128, 128), vmem(256, 128)], left, right)
+def own_edges(edges):
+    return call(own_kernel, [(2, 128, 128), (2, 128, 128)], [], edges)
+
+
+def triangle(*args):
+    return call(triangle_kernel, [(512, 128)], [vmem(256, 128)], *args)
 
 
 def output_stage(mixed, kept, met, gates, w_out):
@@ -275,13 +301,12 @@
     weights = prepared(w_outer, w_tri.T)
     panel, met_pair = lax.optimization_barrier((panel, met_pair))
     sibling = lax.ppermute(panel, "core", swap)
-    edges, kept, sent = pair_stage(
-        left, met, met_pair, panel, sibling, pair, *weights
-    )
+    update = block_update(left, met, panel, weights[0])
+    edges, kept, sent = pair_stage(left, met, met_pair, sibling, update, pair, *weights)
     swapped = lax.all_to_all(edges.reshape(64, 8, 128), LAYER, 0, 0, tiled=True)
     returned = lax.ppermute(sent, "yh", swap)
     rights = lax.ppermute(swapped[:, 4:], "core", swap)
-    back = triangle(swapped.reshape(512, 128), rights.reshape(256, 128))
+    back = triangle(*own_edges(swapped.reshape(512, 128)), rights.reshape(256, 128))
     mixed = lax.all_to_all(back.reshape(128, 4, 128), CHIPS, 0, 0, tiled=True)
     gates = gates_of(kept, returned, w_gate)
     return output_stage(mixed.reshape(512, 128), kept, returned, gates, w_out).reshape(8, 32, 128)

time: 68.8 us -> 69 us (level)
    pallas_call x6 -> x8, Pallas kernels: 7.68 us -> 8.14 us  [call(): pl.pallas_call(kernel, out_shape=shapes if len(shapes) > 1 else shapes[0]...]
  transfers between devices with their start and end apart: 7 -> 7, of which waited for: 5 -> 5; matrix products, arithmetic and copies ran while one was open for 0% -> 0% of each run, Pallas kernels for 1% -> 3%
where the time goes in v15:
time: 69 us; the launch traced here: 68.7 us
  starting transfers between devices  22.3 us (32%)
  blocking collectives  21.1 us (31%)
  waiting for transfers between devices  16.8 us (24%)
  Pallas kernels  8.14 us (12%)
    all_to_all x1, blocking collectives, per_device(): swapped = lax.all_to_all(edges.reshape(64, 8, 128), LAYER, 0, 0, tiled=True)  21.1 us
    all_to_all x1, starting transfers between devices, per_device(): mixed = lax.all_to_all(back.reshape(128, 4, 128), CHIPS, 0, 0, tiled=True)  9.67 us
    pallas_call x8, Pallas kernels, call(): pl.pallas_call(kernel, out_shape=shapes if len(shapes) > 1 else shapes[0]...  8.14 us
    all_to_all x1, waiting for transfers between devices, per_device(): mixed = lax.all_to_all(back.reshape(128, 4, 128), CHIPS, 0, 0, tiled=True)  7.67 us
    ppermute x1, starting transfers between devices, per_device(): panel = lax.ppermute(right, ALL, panel_permutation())  5.83 us
    ppermute x1, waiting for transfers between devices, per_device(): returned = lax.ppermute(sent, 'yh', swap)  3.34 us
    ppermute x1, starting transfers between devices, per_device(): returned = lax.ppermute(sent, 'yh', swap)  3.06 us
    ppermute x1, waiting for transfers between devices, per_device(): met_pair = lax.ppermute(half, 'yh', swap)  2.96 us
  transfers between devices with their start and end apart: 7, of which 5 were waited for; matrix products, arithmetic and copies ran while one was open for 0% of the time, Pallas kernels for 3%

profile of v15, /device:TPU:2, one launch (start us, length us, event | category | flops | bytes accessed | tf_op | source)
XLA Modules:
  0.0 68.7 jit_solution(216323331840578432)
XLA Ops:
  0.0 0.0 copy-start.5
  0.0 2.9 %shard_map.82 = (f32[256,128]{1,0:T(8,128)}, f32[256,128]{1,0:T(8,128)}, f32[128,128]{1,0:T(8,128)}) custom-call(f32[128,8,256]{2,1,0:T(8,128)} %msa_ref.1, f32[32,256]{1,0:T(8,128)} %bitcast.17, f32[32,256]{1,0:T(8,128)} %bitcast.18, f32[8,2,16,128]{3,2,1,0:T(8,128)} %bitcast.13), custom_call_target="tpu_custom_call" | custom-call | tf_op jit(solution)/shard_map/pallas_call | solution.py:241
  2.9 5.8 %collective-permute-start.1 = (f32[256,128]{1,0:T(8,128)}, f32[256,128]{1,0:T(8,128)S(1)}, u32[]{:S(2)}, u32[]{:S(2)}) collective-permute-start(f32[256,128]{1,0:T(8,128)} %get-tuple-element.18), channel_id=1, source_target_pairs={{4,0},{32,1},{65,2},{102,3},{135,4},{166,5},{192,6},{226,7},{9,8},... | collective-permute-start | bytes 393224 | tf_op jit(solution)/shard_map/ppermute | solution.py:298
  8.7 2.0 %collective-permute-start.2 = (f32[128,128]{1,0:T(8,128)}, f32[128,128]{1,0:T(8,128)S(1)}, u32[]{:S(2)}, u32[]{:S(2)}) collective-permute-start(f32[128,128]{1,0:T(8,128)} %get-tuple-element.19), channel_id=1, source_target_pairs={{0,16},{16,0},{1,17},{17,1},{2,18},{18,2},{3,19},{19,3},{4,20},{20... | collective-permute-start | bytes 196616 | tf_op jit(solution)/shard_map/ppermute | solution.py:300
  10.7 1.7 %collective-permute-start = (f32[256,128]{1,0:T(8,128)}, f32[256,128]{1,0:T(8,128)S(1)}, u32[]{:S(2)}, u32[]{:S(2)}) collective-permute-start(f32[256,128]{1,0:T(8,128)} %get-tuple-element.17.own_ref), channel_id=1, source_target_pairs={{0,17},{1,16},{16,1},{17,0},{2,19},{3,18},{18,3},{19,2},{4,21},{5,... | collective-permute-start | bytes 393224 | tf_op jit(solution)/shard_map/ppermute | solution.py:299
  12.4 3.0 %collective-permute-done.2.met_pair_ref = f32[128,128]{1,0:T(8,128)S(1)} collective-permute-done((f32[128,128]{1,0:T(8,128)}, f32[128,128]{1,0:T(8,128)S(1)}, u32[]{:S(2)}, u32[]{:S(2)}) %collective-permute-start.2) | collective-permute-done | bytes 65568 | tf_op jit(solution)/shard_map/ppermute | solution.py:300
  15.3 0.0 collective-permute-done.1.panel_ref
  15.3 0.0 collective-permute-start.3
  15.4 0.0 copy-done.5
  15.4 0.1 copy.9
  15.5 0.0 copy-done
  15.5 0.0 copy-start.2
  15.5 0.3 shard_map.83
  15.8 1.8 %collective-permute-done.met_ref = f32[256,128]{1,0:T(8,128)S(1)} collective-permute-done((f32[256,128]{1,0:T(8,128)}, f32[256,128]{1,0:T(8,128)S(1)}, u32[]{:S(2)}, u32[]{:S(2)}) %collective-permute-start) | collective-permute-done | bytes 131104 | tf_op jit(solution)/shard_map/ppermute | solution.py:299
  17.6 0.0 copy-done.2
  17.6 0.7 %shard_map.84.update_ref = f32[128,128]{1,0:T(8,128)S(1)} custom-call(f32[256,128]{1,0:T(8,128)S(1)} %copy-done.2, f32[256,128]{1,0:T(8,128)S(1)} %collective-permute-done.met_ref, f32[256,128]{1,0:T(8,128)S(1)} %collective-permute-done.1.panel_ref, bf16[1024,256]{1,0:T(8,128)(2,1)S(1)} %get-tuple-element.22.w_outer_ref), custom_call_target="tpu_custom_call" | custom-call | tf_op jit(solution)/shard_map/pallas_call | solution.py:241
  18.4 0.0 collective-permute-done.3.sibling_ref
  18.4 0.1 copy-done.1
  18.5 1.2 %shard_map.85 = (f32[512,128]{1,0:T(8,128)S(1)}, f32[128,128]{1,0:T(8,128)S(1)}, f32[128,128]{1,0:T(8,128)S(1)}) custom-call(f32[256,128]{1,0:T(8,128)S(1)} %copy-done.2, f32[256,128]{1,0:T(8,128)S(1)} %collective-permute-done.met_ref, f32[128,128]{1,0:T(8,128)S(1)} %collective-permute-done.2.met_pair_ref, ...), custom_call_target="tpu_custom_call" | custom-call | tf_op jit(solution)/shard_map/pallas_call | solution.py:241
  19.8 21.1 %all_to_all.10 = f32[64,8,128]{2,1,0:T(8,128)S(1)} all-to-all(f32[64,8,128]{2,1,0:T(8,128)S(1)} %bitcast.15), channel_id=1, replica_groups=mesh['z'=8,'yh'=2,'core'=2,'x'=4,'yl'=2] {'z','x','yl'}, dimensions={0} | all-to-all | bytes 524288 | tf_op jit(solution)/shard_map/all_to_all | solution.py:306
  40.9 0.1 collective-permute-start.4
  41.0 0.3 shard_map.86
  41.3 1.0 %collective-permute-done.4 = f32[64,4,128]{2,1,0:T(4,128)S(1)} collective-permute-done((f32[64,4,128]{2,1,0:T(4,128)S(1)}, f32[64,4,128]{2,1,0:T(4,128)S(1)}, u32[]{:S(2)}, u32[]{:S(2)}) %collective-permute-start.4) | collective-permute-done | bytes 131104 | tf_op jit(solution)/shard_map/ppermute | solution.py:308
  42.3 1.3 %shard_map.87 = f32[512,128]{1,0:T(8,128)} custom-call(f32[2,128,128]{2,1,0:T(8,128)S(1)} %get-tuple-element.25.l_ref, f32[2,128,128]{2,1,0:T(8,128)S(1)} %get-tuple-element.26.own_ref, f32[256,128]{1,0:T(8,128)S(1)} %bitcast.16), custom_call_target="tpu_custom_call" | custom-call | tf_op jit(solution)/shard_map/pallas_call | solution.py:241
  43.6 9.7 %all-to-all-start.1 = ((f32[128,4,128]{2,1,0:T(4,128)}), f32[128,4,128]{2,1,0:T(4,128)S(1)}, u32[]{:S(2)}, u32[]{:S(2)}) async-start(f32[128,4,128]{2,1,0:T(4,128)} %bitcast.7), calls=%async_computation.1 | async-start | bytes 524288 | tf_op jit(solution)/shard_map/all_to_all | solution.py:310
  53.3 3.1 %collective-permute-start.5 = (f32[128,128]{1,0:T(8,128)S(1)}, f32[128,128]{1,0:T(8,128)S(1)}, u32[]{:S(2)}, u32[]{:S(2)}) collective-permute-start(f32[128,128]{1,0:T(8,128)S(1)} %get-tuple-element.28), channel_id=1, source_target_pairs={{0,16},{16,0},{1,17},{17,1},{2,18},{18,2},{3,19},{19,3},{4,20},{20... | collective-permute-start | bytes 196616 | tf_op jit(solution)/shard_map/ppermute | solution.py:307
  56.4 3.3 %collective-permute-done.5.met_ref = f32[128,128]{1,0:T(8,128)S(1)} collective-permute-done((f32[128,128]{1,0:T(8,128)S(1)}, f32[128,128]{1,0:T(8,128)S(1)}, u32[]{:S(2)}, u32[]{:S(2)}) %collective-permute-start.5) | collective-permute-done | bytes 65568 | tf_op jit(solution)/shard_map/ppermute | solution.py:307
  59.7 0.0 copy-done.3
  59.7 0.4 shard_map.88.gates_ref
  60.1 7.7 %all-to-all-done.1 = f32[128,4,128]{2,1,0:T(4,128)S(1)} async-done(((f32[128,4,128]{2,1,0:T(4,128)}), f32[128,4,128]{2,1,0:T(4,128)S(1)}, u32[]{:S(2)}, u32[]{:S(2)}) %all-to-all-start.1) | async-done | bytes 262176 | tf_op jit(solution)/shard_map/all_to_all | solution.py:310
  67.8 0.0 copy-done.4
  67.8 1.0 %shard_map.89 = f32[8,2,16,128]{3,2,1,0:T(8,128)} custom-call(f32[512,128]{1,0:T(8,128)S(1)} %bitcast.12, f32[128,128]{1,0:T(8,128)S(1)} %get-tuple-element.27.kept_ref, f32[128,128]{1,0:T(8,128)S(1)} %collective-permute-done.5.met_ref, f32[2,128,128]{2,1,0:T(8,128)S(1)} %shard_map.88.gates_ref, f32[128,128]{1,0:T(8,128)S(1)} %copy-done.4), custom_call_target="tpu_custom_call" | custom-call | tf_op jit(solution)/shard_map/pallas_call | solution.py:241
  (5 shorter events, 0.0 us)
Async XLA Ops:
  0.0 15.4 %copy-start.5 = (f32[128,512]{1,0:T(8,128)S(1)}, f32[128,512]{1,0:T(8,128)}, u32[]{:S(2)}) copy-start(f32[128,512]{1,0:T(8,128)} %param.13) | copy-start | bytes 786436
  2.9 12.6 %copy-start = (f32[1024,128]{1,0:T(8,128)S(1)}, f32[1024,128]{1,0:T(8,128)}, u32[]{:S(2)}) copy-start(f32[1024,128]{1,0:T(8,128)} %w_outer_ref.1) | copy-start | bytes 1572868
  2.9 12.4 %collective-permute-start.1 = (f32[256,128]{1,0:T(8,128)}, f32[256,128]{1,0:T(8,128)S(1)}, u32[]{:S(2)}, u32[]{:S(2)}) collective-permute-start(f32[256,128]{1,0:T(8,128)} %get-tuple-element.18), channel_id=1, source_target_pairs={{4,0},{32,1},{65,2},{102,3},{135,4},{166,5},{192,6},{226,7},{9,8},... | collective-permute-start | bytes 393224 | tf_op jit(solution)/shard_map/ppermute | solution.py:298
  8.7 6.6 %collective-permute-start.2 = (f32[128,128]{1,0:T(8,128)}, f32[128,128]{1,0:T(8,128)S(1)}, u32[]{:S(2)}, u32[]{:S(2)}) collective-permute-start(f32[128,128]{1,0:T(8,128)} %get-tuple-element.19), channel_id=1, source_target_pairs={{0,16},{16,0},{1,17},{17,1},{2,18},{18,2},{3,19},{19,3},{4,20},{20... | collective-permute-start | bytes 196616 | tf_op jit(solution)/shard_map/ppermute | solution.py:300
  10.7 6.9 %collective-permute-start = (f32[256,128]{1,0:T(8,128)}, f32[256,128]{1,0:T(8,128)S(1)}, u32[]{:S(2)}, u32[]{:S(2)}) collective-permute-start(f32[256,128]{1,0:T(8,128)} %get-tuple-element.17.own_ref), channel_id=1, source_target_pairs={{0,17},{1,16},{16,1},{17,0},{2,19},{3,18},{18,3},{19,2},{4,21},{5,... | collective-permute-start | bytes 393224 | tf_op jit(solution)/shard_map/ppermute | solution.py:299
  15.3 3.1 %collective-permute-start.3 = (f32[256,128]{1,0:T(8,128)S(1)}, f32[256,128]{1,0:T(8,128)S(1)}, u32[]{:S(2)}, u32[]{:S(2)}) collective-permute-start(f32[256,128]{1,0:T(8,128)S(1)} %collective-permute-done.1.panel_ref), channel_id=1, source_target_pairs={{0,8},{8,0},{1,9},{9,1},{2,10},{10,2},{3,11},{11,3},{4,12},{12,4},... | collective-permute-start | bytes 393224 | tf_op jit(solution)/shard_map/ppermute | solution.py:303
  15.5 2.1 %copy-start.2 = (f32[256,128]{1,0:T(8,128)S(1)}, f32[256,128]{1,0:T(8,128)}, u32[]{:S(2)}) copy-start(f32[256,128]{1,0:T(8,128)} %get-tuple-element.17.own_ref) | copy-start | bytes 393220
  17.6 0.9 %copy-start.1 = (f32[8,32,128]{2,1,0:T(8,128)S(1)}, f32[8,32,128]{2,1,0:T(8,128)}, u32[]{:S(2)}) copy-start(f32[8,32,128]{2,1,0:T(8,128)} %param.9) | copy-start | bytes 393220
  40.9 1.4 %collective-permute-start.4 = (f32[64,4,128]{2,1,0:T(4,128)S(1)}, f32[64,4,128]{2,1,0:T(4,128)S(1)}, u32[]{:S(2)}, u32[]{:S(2)}) collective-permute-start(f32[64,4,128]{2,1,0:T(4,128)S(1)} %slice.4), channel_id=1, source_target_pairs={{0,8},{8,0},{1,9},{9,1},{2,10},{10,2},{3,11},{11,3},{4,12},{12,4},... | collective-permute-start | bytes 393224 | tf_op jit(solution)/shard_map/ppermute | solution.py:308
  43.6 16.1 %copy-start.3 = (f32[128,128]{1,0:T(8,128)S(1)}, f32[128,128]{1,0:T(8,128)}, u32[]{:S(2)}) copy-start(f32[128,128]{1,0:T(8,128)} %w_ref.2) | copy-start | bytes 196612
  43.6 24.1 %all-to-all-start.1 = ((f32[128,4,128]{2,1,0:T(4,128)}), f32[128,4,128]{2,1,0:T(4,128)S(1)}, u32[]{:S(2)}, u32[]{:S(2)}) async-start(f32[128,4,128]{2,1,0:T(4,128)} %bitcast.7), calls=%async_computation.1 | async-start | bytes 524288 | tf_op jit(solution)/shard_map/all_to_all | solution.py:310
  53.3 6.4 %collective-permute-start.5 = (f32[128,128]{1,0:T(8,128)S(1)}, f32[128,128]{1,0:T(8,128)S(1)}, u32[]{:S(2)}, u32[]{:S(2)}) collective-permute-start(f32[128,128]{1,0:T(8,128)S(1)} %get-tuple-element.28), channel_id=1, source_target_pairs={{0,16},{16,0},{1,17},{17,1},{2,18},{18,2},{3,19},{19,3},{4,20},{20... | collective-permute-start | bytes 196616 | tf_op jit(solution)/shard_map/ppermute | solution.py:307
  59.7 8.0 %copy-start.4 = (f32[128,128]{1,0:T(8,128)S(1)}, f32[128,128]{1,0:T(8,128)}, u32[]{:S(2)}) copy-start(f32[128,128]{1,0:T(8,128)} %w_ref.3) | copy-start | bytes 196612

commit v16 on v15

--- a/solution.py
+++ b/solution.py
@@ -101,7 +101,8 @@
         half_ref[pl.ds(p * 16, 16), :] = pair_ref[turned_rows(p), other]
 
 
-def weight_kernel(w_outer_ref, w_tri_ref, outer_ref, tri_ref):
+def weight_kernel(w_outer_ref, w_tri_ref, left_ref, outer_ref, tri_ref, kept_ref):
+    kept_ref[...] = left_ref[...]
     for b in range(32):
         outer_ref[pl.ds(b * 32, 32), :] = halves(w_outer_ref[pl.ds(b, 32, stride=32), :])
     tri_ref[...] = halves(w_tri_ref[...])
@@ -236,8 +237,9 @@
             out_ref[i, half] = mid[p : p + 16] + gate[p : p + 16] * update[i * 16 : i * 16 + 16]
 
 
-def call(kernel, out_shapes, scratch, *args, limit=VMEM_LIMIT, kind=jnp.float32):
-    shapes = [jax.ShapeDtypeStruct(s, kind) for s in out_shapes]
+def call(kernel, out_shapes, scratch, *args, limit=VMEM_LIMIT, short=0):
+    kinds = [jnp.bfloat16] * short + [jnp.float32] * (len(out_shapes) - short)
+    shapes = [jax.ShapeDtypeStruct(s, kind) for s, kind in zip(out_shapes, kinds)]
     return pl.pallas_call(
         kernel,
         out_shape=shapes if len(shapes) > 1 else shapes[0],
@@ -287,8 +289,8 @@
     return call(gate_kernel, [(2, 128, 128)], [], kept, met, w_gate)
 
 
-def prepared(w_outer, w_tri):
-    return call(weight_kernel, [(1024, 256), (512, 256)], [], w_outer, w_tri, kind=jnp.bfloat16)
+def prepared(*args):
+    return call(weight_kernel, [(1024, 256), (512, 256), (256, 128)], [], *args, short=2)
 
 
 def per_device(homolog, pair, w_first, w_second, w_outer, w_tri, w_gate, w_out):
@@ -298,8 +300,8 @@
     panel = lax.ppermute(right, ALL, panel_permutation())
     met = lax.ppermute(left, ("yh", "yl"), [(0, 3), (1, 2), (2, 1), (3, 0)])
     met_pair = lax.ppermute(half, "yh", swap)
-    weights = prepared(w_outer, w_tri.T)
-    panel, met_pair = lax.optimization_barrier((panel, met_pair))
+    ready = prepared(w_outer, w_tri.T, left)
+    panel, met_pair, (*weights, left) = lax.optimization_barrier((panel, met_pair, ready))
     sibling = lax.ppermute(panel, "core", swap)
     update = block_update(left, met, panel, weights[0])
     edges, kept, sent = pair_stage(left, met, met_pair, sibling, update, pair, *weights)

time: 69 us -> 68.1 us (0.987)
  waiting for transfers between devices: 16.8 us -> 15.9 us
  local copies, waits for them, and re-layouts: 0.31 us -> 1.07 us
    ppermute x1, waiting for transfers between devices: 2.96 us -> 1.58 us  [per_device(): met_pair = lax.ppermute(half, 'yh', swap)]
    unnamed x13, local copies, waits for them, and re-layouts: 0.28 us -> 1.04 us
where the time goes in v16:
time: 68.1 us; the launch traced here: 67.8 us
  starting transfers between devices  22 us (32%)
  blocking collectives  20.6 us (30%)
  waiting for transfers between devices  15.9 us (23%)
  Pallas kernels  8.16 us (12%)
  local copies, waits for them, and re-layouts  1.07 us (2%)
    all_to_all x1, blocking collectives, per_device(): swapped = lax.all_to_all(edges.reshape(64, 8, 128), LAYER, 0, 0, tiled=True)  20.6 us
    all_to_all x1, starting transfers between devices, per_device(): mixed = lax.all_to_all(back.reshape(128, 4, 128), CHIPS, 0, 0, tiled=True)  9.33 us
    pallas_call x8, Pallas kernels, call(): pl.pallas_call(kernel, out_shape=shapes if len(shapes) > 1 else shapes[0]...  8.16 us
    all_to_all x1, waiting for transfers between devices, per_device(): mixed = lax.all_to_all(back.reshape(128, 4, 128), CHIPS, 0, 0, tiled=True)  7.67 us
    ppermute x1, starting transfers between devices, per_device(): panel = lax.ppermute(right, ALL, panel_permutation())  5.83 us
    ppermute x1, waiting for transfers between devices, per_device(): returned = lax.ppermute(sent, 'yh', swap)  3.34 us
    ppermute x1, starting transfers between devices, per_device(): returned = lax.ppermute(sent, 'yh', swap)  3.06 us
    ppermute x1, waiting for transfers between devices, per_device(): met = lax.ppermute(left, ('yh', 'yl'), [(0, 3), (1, 2), (2, 1), (3, 0)])  2.27 us
  transfers between devices with their start and end apart: 7, of which 5 were waited for; matrix products, arithmetic and copies ran while one was open for 0% of the time, Pallas kernels for 3%

profile of v16, /device:TPU:2, one launch (start us, length us, event | category | flops | bytes accessed | tf_op | source)
XLA Modules:
  0.0 67.8 jit_solution(16451391895085648842)
XLA Ops:
  0.0 0.0 copy-start.5
  0.0 2.9 %shard_map.82 = (f32[256,128]{1,0:T(8,128)}, f32[256,128]{1,0:T(8,128)}, f32[128,128]{1,0:T(8,128)}) custom-call(f32[128,8,256]{2,1,0:T(8,128)} %msa_ref.1, f32[32,256]{1,0:T(8,128)} %bitcast.17, f32[32,256]{1,0:T(8,128)} %bitcast.18, f32[8,2,16,128]{3,2,1,0:T(8,128)} %bitcast.13), custom_call_target="tpu_custom_call" | custom-call | tf_op jit(solution)/shard_map/pallas_call | solution.py:243
  2.9 5.8 %collective-permute-start = (f32[256,128]{1,0:T(8,128)}, f32[256,128]{1,0:T(8,128)S(1)}, u32[]{:S(2)}, u32[]{:S(2)}) collective-permute-start(f32[256,128]{1,0:T(8,128)} %get-tuple-element.21), channel_id=1, source_target_pairs={{4,0},{32,1},{65,2},{102,3},{135,4},{166,5},{192,6},{226,7},{9,8},... | collective-permute-start | bytes 393224 | tf_op jit(solution)/shard_map/ppermute | solution.py:300
  8.7 2.0 %collective-permute-start.1 = (f32[128,128]{1,0:T(8,128)}, f32[128,128]{1,0:T(8,128)S(1)}, u32[]{:S(2)}, u32[]{:S(2)}) collective-permute-start(f32[128,128]{1,0:T(8,128)} %get-tuple-element.22), channel_id=1, source_target_pairs={{0,16},{16,0},{1,17},{17,1},{2,18},{18,2},{3,19},{19,3},{4,20},{20... | collective-permute-start | bytes 196616 | tf_op jit(solution)/shard_map/ppermute | solution.py:302
  10.7 1.7 %collective-permute-start.2 = (f32[256,128]{1,0:T(8,128)}, f32[256,128]{1,0:T(8,128)S(1)}, u32[]{:S(2)}, u32[]{:S(2)}) collective-permute-start(f32[256,128]{1,0:T(8,128)} %get-tuple-element.23.left_ref), channel_id=1, source_target_pairs={{0,17},{1,16},{16,1},{17,0},{2,19},{3,18},{18,3},{19,2},{4,21},{5,... | collective-permute-start | bytes 393224 | tf_op jit(solution)/shard_map/ppermute | solution.py:301
  12.4 0.0 copy-done.5
  12.4 0.1 copy.9
  12.5 0.0 copy-done
  12.5 0.0 copy-start.2
  12.5 0.9 %copy-done.2 = f32[256,128]{1,0:T(8,128)S(1)} copy-done((f32[256,128]{1,0:T(8,128)S(1)}, f32[256,128]{1,0:T(8,128)}, u32[]{:S(2)}) %copy-start.2) | copy-done | bytes 131096
  13.4 0.3 shard_map.83
  13.7 1.6 %collective-permute-done.1.met_pair_ref = f32[128,128]{1,0:T(8,128)S(1)} collective-permute-done((f32[128,128]{1,0:T(8,128)}, f32[128,128]{1,0:T(8,128)S(1)}, u32[]{:S(2)}, u32[]{:S(2)}) %collective-permute-start.1) | collective-permute-done | bytes 65568 | tf_op jit(solution)/shard_map/ppermute | solution.py:302
  15.3 0.0 collective-permute-done.panel_ref
  15.3 0.0 collective-permute-start.3
  15.4 2.3 %collective-permute-done.2.met_ref = f32[256,128]{1,0:T(8,128)S(1)} collective-permute-done((f32[256,128]{1,0:T(8,128)}, f32[256,128]{1,0:T(8,128)S(1)}, u32[]{:S(2)}, u32[]{:S(2)}) %collective-permute-start.2) | collective-permute-done | bytes 131104 | tf_op jit(solution)/shard_map/ppermute | solution.py:301
  17.6 0.8 %shard_map.84.update_ref = f32[128,128]{1,0:T(8,128)S(1)} custom-call(f32[256,128]{1,0:T(8,128)S(1)} %get-tuple-element.27.own_ref, f32[256,128]{1,0:T(8,128)S(1)} %collective-permute-done.2.met_ref, f32[256,128]{1,0:T(8,128)S(1)} %collective-permute-done.panel_ref, bf16[1024,256]{1,0:T(8,128)(2,1)S(1)} %get-tuple-element.30.w_outer_ref), custom_call_target="tpu_custom_call" | custom-call | tf_op jit(solution)/shard_map/pallas_call | solution.py:243
  18.4 0.0 collective-permute-done.3.sibling_ref
  18.4 0.0 copy-done.1
  18.4 1.2 %shard_map.85 = (f32[512,128]{1,0:T(8,128)S(1)}, f32[128,128]{1,0:T(8,128)S(1)}, f32[128,128]{1,0:T(8,128)S(1)}) custom-call(f32[256,128]{1,0:T(8,128)S(1)} %get-tuple-element.27.own_ref, f32[256,128]{1,0:T(8,128)S(1)} %collective-permute-done.2.met_ref, f32[128,128]{1,0:T(8,128)S(1)} %collective-permute-done.1.met_pair_ref, ...), custom_call_target="tpu_custom_call" | custom-call | tf_op jit(solution)/shard_map/pallas_call | solution.py:243
  19.7 20.6 %all_to_all.10 = f32[64,8,128]{2,1,0:T(8,128)S(1)} all-to-all(f32[64,8,128]{2,1,0:T(8,128)S(1)} %bitcast.15), channel_id=1, replica_groups=mesh['z'=8,'yh'=2,'core'=2,'x'=4,'yl'=2] {'z','x','yl'}, dimensions={0} | all-to-all | bytes 524288 | tf_op jit(solution)/shard_map/all_to_all | solution.py:308
  40.3 0.1 collective-permute-start.4
  40.4 0.3 shard_map.86
  40.7 1.0 %collective-permute-done.4 = f32[64,4,128]{2,1,0:T(4,128)S(1)} collective-permute-done((f32[64,4,128]{2,1,0:T(4,128)S(1)}, f32[64,4,128]{2,1,0:T(4,128)S(1)}, u32[]{:S(2)}, u32[]{:S(2)}) %collective-permute-start.4) | collective-permute-done | bytes 131104 | tf_op jit(solution)/shard_map/ppermute | solution.py:310
  41.7 1.3 %shard_map.87 = f32[512,128]{1,0:T(8,128)} custom-call(f32[2,128,128]{2,1,0:T(8,128)S(1)} %get-tuple-element.33.l_ref, f32[2,128,128]{2,1,0:T(8,128)S(1)} %get-tuple-element.34.own_ref, f32[256,128]{1,0:T(8,128)S(1)} %bitcast.16), custom_call_target="tpu_custom_call" | custom-call | tf_op jit(solution)/shard_map/pallas_call | solution.py:243
  43.1 9.3 %all-to-all-start.1 = ((f32[128,4,128]{2,1,0:T(4,128)}), f32[128,4,128]{2,1,0:T(4,128)S(1)}, u32[]{:S(2)}, u32[]{:S(2)}) async-start(f32[128,4,128]{2,1,0:T(4,128)} %bitcast.7), calls=%async_computation.1 | async-start | bytes 524288 | tf_op jit(solution)/shard_map/all_to_all | solution.py:312
  52.4 3.1 %collective-permute-start.5 = (f32[128,128]{1,0:T(8,128)S(1)}, f32[128,128]{1,0:T(8,128)S(1)}, u32[]{:S(2)}, u32[]{:S(2)}) collective-permute-start(f32[128,128]{1,0:T(8,128)S(1)} %get-tuple-element.36), channel_id=1, source_target_pairs={{0,16},{16,0},{1,17},{17,1},{2,18},{18,2},{3,19},{19,3},{4,20},{20... | collective-permute-start | bytes 196616 | tf_op jit(solution)/shard_map/ppermute | solution.py:309
  55.4 3.3 %collective-permute-done.5.met_ref = f32[128,128]{1,0:T(8,128)S(1)} collective-permute-done((f32[128,128]{1,0:T(8,128)S(1)}, f32[128,128]{1,0:T(8,128)S(1)}, u32[]{:S(2)}, u32[]{:S(2)}) %collective-permute-start.5) | collective-permute-done | bytes 65568 | tf_op jit(solution)/shard_map/ppermute | solution.py:309
  58.8 0.0 copy-done.3
  58.8 0.4 shard_map.88.gates_ref
  59.2 7.7 %all-to-all-done.1 = f32[128,4,128]{2,1,0:T(4,128)S(1)} async-done(((f32[128,4,128]{2,1,0:T(4,128)}), f32[128,4,128]{2,1,0:T(4,128)S(1)}, u32[]{:S(2)}, u32[]{:S(2)}) %all-to-all-start.1) | async-done | bytes 262176 | tf_op jit(solution)/shard_map/all_to_all | solution.py:312
  66.8 0.0 copy-done.4
  66.8 1.0 %shard_map.89 = f32[8,2,16,128]{3,2,1,0:T(8,128)} custom-call(f32[512,128]{1,0:T(8,128)S(1)} %bitcast.12, f32[128,128]{1,0:T(8,128)S(1)} %get-tuple-element.35.kept_ref, f32[128,128]{1,0:T(8,128)S(1)} %collective-permute-done.5.met_ref, f32[2,128,128]{2,1,0:T(8,128)S(1)} %shard_map.88.gates_ref, f32[128,128]{1,0:T(8,128)S(1)} %copy-done.4), custom_call_target="tpu_custom_call" | custom-call | tf_op jit(solution)/shard_map/pallas_call | solution.py:243
  (5 shorter events, 0.0 us)
Async XLA Ops:
  0.0 12.4 %copy-start.5 = (f32[128,512]{1,0:T(8,128)S(1)}, f32[128,512]{1,0:T(8,128)}, u32[]{:S(2)}) copy-start(f32[128,512]{1,0:T(8,128)} %param.13) | copy-start | bytes 786436
  2.9 9.6 %copy-start = (f32[1024,128]{1,0:T(8,128)S(1)}, f32[1024,128]{1,0:T(8,128)}, u32[]{:S(2)}) copy-start(f32[1024,128]{1,0:T(8,128)} %w_outer_ref.1) | copy-start | bytes 1572868
  2.9 12.4 %collective-permute-start = (f32[256,128]{1,0:T(8,128)}, f32[256,128]{1,0:T(8,128)S(1)}, u32[]{:S(2)}, u32[]{:S(2)}) collective-permute-start(f32[256,128]{1,0:T(8,128)} %get-tuple-element.21), channel_id=1, source_target_pairs={{4,0},{32,1},{65,2},{102,3},{135,4},{166,5},{192,6},{226,7},{9,8},... | collective-permute-start | bytes 393224 | tf_op jit(solution)/shard_map/ppermute | solution.py:300
  8.7 6.6 %collective-permute-start.1 = (f32[128,128]{1,0:T(8,128)}, f32[128,128]{1,0:T(8,128)S(1)}, u32[]{:S(2)}, u32[]{:S(2)}) collective-permute-start(f32[128,128]{1,0:T(8,128)} %get-tuple-element.22), channel_id=1, source_target_pairs={{0,16},{16,0},{1,17},{17,1},{2,18},{18,2},{3,19},{19,3},{4,20},{20... | collective-permute-start | bytes 196616 | tf_op jit(solution)/shard_map/ppermute | solution.py:302
  10.7 6.9 %collective-permute-start.2 = (f32[256,128]{1,0:T(8,128)}, f32[256,128]{1,0:T(8,128)S(1)}, u32[]{:S(2)}, u32[]{:S(2)}) collective-permute-start(f32[256,128]{1,0:T(8,128)} %get-tuple-element.23.left_ref), channel_id=1, source_target_pairs={{0,17},{1,16},{16,1},{17,0},{2,19},{3,18},{18,3},{19,2},{4,21},{5,... | collective-permute-start | bytes 393224 | tf_op jit(solution)/shard_map/ppermute | solution.py:301
  12.5 0.9 %copy-start.2 = (f32[256,128]{1,0:T(8,128)S(1)}, f32[256,128]{1,0:T(8,128)}, u32[]{:S(2)}) copy-start(f32[256,128]{1,0:T(8,128)} %get-tuple-element.23.left_ref) | copy-start | bytes 393220
  15.3 3.1 %copy-start.1 = (f32[8,32,128]{2,1,0:T(8,128)S(1)}, f32[8,32,128]{2,1,0:T(8,128)}, u32[]{:S(2)}) copy-start(f32[8,32,128]{2,1,0:T(8,128)} %param.9) | copy-start | bytes 393220
  15.3 3.1 %collective-permute-start.3 = (f32[256,128]{1,0:T(8,128)S(1)}, f32[256,128]{1,0:T(8,128)S(1)}, u32[]{:S(2)}, u32[]{:S(2)}) collective-permute-start(f32[256,128]{1,0:T(8,128)S(1)} %collective-permute-done.panel_ref), channel_id=1, source_target_pairs={{0,8},{8,0},{1,9},{9,1},{2,10},{10,2},{3,11},{11,3},{4,12},{12,4},... | collective-permute-start | bytes 393224 | tf_op jit(solution)/shard_map/ppermute | solution.py:305
  40.3 1.4 %collective-permute-start.4 = (f32[64,4,128]{2,1,0:T(4,128)S(1)}, f32[64,4,128]{2,1,0:T(4,128)S(1)}, u32[]{:S(2)}, u32[]{:S(2)}) collective-permute-start(f32[64,4,128]{2,1,0:T(4,128)S(1)} %slice.4), channel_id=1, source_target_pairs={{0,8},{8,0},{1,9},{9,1},{2,10},{10,2},{3,11},{11,3},{4,12},{12,4},... | collective-permute-start | bytes 393224 | tf_op jit(solution)/shard_map/ppermute | solution.py:310
  43.1 15.7 %copy-start.3 = (f32[128,128]{1,0:T(8,128)S(1)}, f32[128,128]{1,0:T(8,128)}, u32[]{:S(2)}) copy-start(f32[128,128]{1,0:T(8,128)} %w_ref.2) | copy-start | bytes 196612
  43.1 23.8 %all-to-all-start.1 = ((f32[128,4,128]{2,1,0:T(4,128)}), f32[128,4,128]{2,1,0:T(4,128)S(1)}, u32[]{:S(2)}, u32[]{:S(2)}) async-start(f32[128,4,128]{2,1,0:T(4,128)} %bitcast.7), calls=%async_computation.1 | async-start | bytes 524288 | tf_op jit(solution)/shard_map/all_to_all | solution.py:312
  52.4 6.4 %collective-permute-start.5 = (f32[128,128]{1,0:T(8,128)S(1)}, f32[128,128]{1,0:T(8,128)S(1)}, u32[]{:S(2)}, u32[]{:S(2)}) collective-permute-start(f32[128,128]{1,0:T(8,128)S(1)} %get-tuple-element.36), channel_id=1, source_target_pairs={{0,16},{16,0},{1,17},{17,1},{2,18},{18,2},{3,19},{19,3},{4,20},{20... | collective-permute-start | bytes 196616 | tf_op jit(solution)/shard_map/ppermute | solution.py:309
  58.8 8.0 %copy-start.4 = (f32[128,128]{1,0:T(8,128)S(1)}, f32[128,128]{1,0:T(8,128)}, u32[]{:S(2)}) copy-start(f32[128,128]{1,0:T(8,128)} %w_ref.3) | copy-start | bytes 196612

commit v17 on v16

--- a/solution.py
+++ b/solution.py
@@ -217,9 +217,10 @@
                     )
 
 
-def output_kernel(mixed_ref, kept_ref, met_ref, gates_ref, w_ref, out_ref):
+def output_kernel(mixed_ref, kept_ref, met_ref, gates_ref, w_ref, out_ref, held, sems):
     yh = lax.axis_index("yh")
     w = halves(w_ref[...])
+    copies = []
     for half in range(2):
         tiles = []
         for h in range(2):
@@ -234,10 +235,14 @@
         gate = jnp.where(yh == half, gates_ref[0], gates_ref[1])
         for i in range(8):
             p = turned_rows(i) * 16
-            out_ref[i, half] = mid[p : p + 16] + gate[p : p + 16] * update[i * 16 : i * 16 + 16]
-
-
-def call(kernel, out_shapes, scratch, *args, limit=VMEM_LIMIT, short=0):
+            held[half, i] = mid[p : p + 16] + gate[p : p + 16] * update[i * 16 : i * 16 + 16]
+        copies.append(pltpu.make_async_copy(held.at[half], out_ref.at[:, half], sems.at[half]))
+        copies[half].start()
+    for copy in copies:
+        copy.wait()
+
+
+def call(kernel, out_shapes, scratch, *args, limit=VMEM_LIMIT, short=0, **more):
     kinds = [jnp.bfloat16] * short + [jnp.float32] * (len(out_shapes) - short)
     shapes = [jax.ShapeDtypeStruct(s, kind) for s, kind in zip(out_shapes, kinds)]
     return pl.pallas_call(
@@ -245,6 +250,7 @@
         out_shape=shapes if len(shapes) > 1 else shapes[0],
         scratch_shapes=scratch,
         compiler_params=pltpu.CompilerParams(vmem_limit_bytes=limit),
+        **more,
     )(*args)
 
 
@@ -281,8 +287,14 @@
     return call(triangle_kernel, [(512, 128)], [vmem(256, 128)], *args)
 
 
-def output_stage(mixed, kept, met, gates, w_out):
-    return call(output_kernel, [(8, 2, 16, 128)], [], mixed, kept, met, gates, w_out)
+def output_stage(*args):
+    return call(
+        output_kernel,
+        [(8, 2, 16, 128)],
+        [vmem(2, 8, 16, 128), pltpu.SemaphoreType.DMA((2,))],
+        *args,
+        out_specs=pl.BlockSpec(memory_space=pl.ANY),
+    )
 
 
 def gates_of(kept, met, w_gate):

time: 68.1 us -> 68.1 us (level)
  no operation moved by 1% of the time
where the time goes in v17:
time: 68.1 us; the launch traced here: 67.8 us
  starting transfers between devices  22 us (32%)
  blocking collectives  20.6 us (30%)
  waiting for transfers between devices  15.9 us (23%)
  Pallas kernels  8.15 us (12%)
  local copies, waits for them, and re-layouts  1.07 us (2%)
    all_to_all x1, blocking collectives, per_device(): swapped = lax.all_to_all(edges.reshape(64, 8, 128), LAYER, 0, 0, tiled=True)  20.6 us
    all_to_all x1, starting transfers between devices, per_device(): mixed = lax.all_to_all(back.reshape(128, 4, 128), CHIPS, 0, 0, tiled=True)  9.33 us
    pallas_call x8, Pallas kernels, call(): pl.pallas_call(kernel, out_shape=shapes if len(shapes) > 1 else shapes[0]...  8.15 us
    all_to_all x1, waiting for transfers between devices, per_device(): mixed = lax.all_to_all(back.reshape(128, 4, 128), CHIPS, 0, 0, tiled=True)  7.67 us
    ppermute x1, starting transfers between devices, per_device(): panel = lax.ppermute(right, ALL, panel_permutation())  5.83 us
    ppermute x1, waiting for transfers between devices, per_device(): returned = lax.ppermute(sent, 'yh', swap)  3.34 us
    ppermute x1, starting transfers between devices, per_device(): returned = lax.ppermute(sent, 'yh', swap)  3.06 us
    ppermute x1, waiting for transfers between devices, per_device(): met = lax.ppermute(left, ('yh', 'yl'), [(0, 3), (1, 2), (2, 1), (3, 0)])  2.27 us
  transfers between devices with their start and end apart: 7, of which 5 were waited for; matrix products, arithmetic and copies ran while one was open for 0% of the time, Pallas kernels for 3%

profile of v17, /device:TPU:2, one launch (start us, length us, event | category | flops | bytes accessed | tf_op | source)
XLA Modules:
  0.0 67.8 jit_solution(14461441017300398948)
XLA Ops:
  0.0 0.0 copy-start.5
  0.0 2.9 %shard_map.82 = (f32[256,128]{1,0:T(8,128)}, f32[256,128]{1,0:T(8,128)}, f32[128,128]{1,0:T(8,128)}) custom-call(f32[128,8,256]{2,1,0:T(8,128)} %msa_ref.1, f32[32,256]{1,0:T(8,128)} %bitcast.17, f32[32,256]{1,0:T(8,128)} %bitcast.18, f32[8,2,16,128]{3,2,1,0:T(8,128)} %bitcast.13), custom_call_target="tpu_custom_call" | custom-call | tf_op jit(solution)/shard_map/pallas_call | solution.py:248
  2.9 5.8 %collective-permute-start = (f32[256,128]{1,0:T(8,128)}, f32[256,128]{1,0:T(8,128)S(1)}, u32[]{:S(2)}, u32[]{:S(2)}) collective-permute-start(f32[256,128]{1,0:T(8,128)} %get-tuple-element.21), channel_id=1, source_target_pairs={{4,0},{32,1},{65,2},{102,3},{135,4},{166,5},{192,6},{226,7},{9,8},... | collective-permute-start | bytes 393224 | tf_op jit(solution)/shard_map/ppermute | solution.py:312
  8.7 2.0 %collective-permute-start.1 = (f32[128,128]{1,0:T(8,128)}, f32[128,128]{1,0:T(8,128)S(1)}, u32[]{:S(2)}, u32[]{:S(2)}) collective-permute-start(f32[128,128]{1,0:T(8,128)} %get-tuple-element.22), channel_id=1, source_target_pairs={{0,16},{16,0},{1,17},{17,1},{2,18},{18,2},{3,19},{19,3},{4,20},{20... | collective-permute-start | bytes 196616 | tf_op jit(solution)/shard_map/ppermute | solution.py:314
  10.7 1.7 %collective-permute-start.2 = (f32[256,128]{1,0:T(8,128)}, f32[256,128]{1,0:T(8,128)S(1)}, u32[]{:S(2)}, u32[]{:S(2)}) collective-permute-start(f32[256,128]{1,0:T(8,128)} %get-tuple-element.23.left_ref), channel_id=1, source_target_pairs={{0,17},{1,16},{16,1},{17,0},{2,19},{3,18},{18,3},{19,2},{4,21},{5,... | collective-permute-start | bytes 393224 | tf_op jit(solution)/shard_map/ppermute | solution.py:313
  12.4 0.0 copy-done.5
  12.4 0.1 copy.9
  12.5 0.0 copy-done
  12.5 0.0 copy-start.2
  12.5 0.9 %copy-done.2 = f32[256,128]{1,0:T(8,128)S(1)} copy-done((f32[256,128]{1,0:T(8,128)S(1)}, f32[256,128]{1,0:T(8,128)}, u32[]{:S(2)}) %copy-start.2) | copy-done | bytes 131096
  13.4 0.3 shard_map.83
  13.7 1.6 %collective-permute-done.1.met_pair_ref = f32[128,128]{1,0:T(8,128)S(1)} collective-permute-done((f32[128,128]{1,0:T(8,128)}, f32[128,128]{1,0:T(8,128)S(1)}, u32[]{:S(2)}, u32[]{:S(2)}) %collective-permute-start.1) | collective-permute-done | bytes 65568 | tf_op jit(solution)/shard_map/ppermute | solution.py:314
  15.3 0.0 collective-permute-done.panel_ref
  15.3 0.0 collective-permute-start.3
  15.4 2.3 %collective-permute-done.2.met_ref = f32[256,128]{1,0:T(8,128)S(1)} collective-permute-done((f32[256,128]{1,0:T(8,128)}, f32[256,128]{1,0:T(8,128)S(1)}, u32[]{:S(2)}, u32[]{:S(2)}) %collective-permute-start.2) | collective-permute-done | bytes 131104 | tf_op jit(solution)/shard_map/ppermute | solution.py:313
  17.6 0.8 %shard_map.84.update_ref = f32[128,128]{1,0:T(8,128)S(1)} custom-call(f32[256,128]{1,0:T(8,128)S(1)} %get-tuple-element.27.own_ref, f32[256,128]{1,0:T(8,128)S(1)} %collective-permute-done.2.met_ref, f32[256,128]{1,0:T(8,128)S(1)} %collective-permute-done.panel_ref, bf16[1024,256]{1,0:T(8,128)(2,1)S(1)} %get-tuple-element.30.w_outer_ref), custom_call_target="tpu_custom_call" | custom-call | tf_op jit(solution)/shard_map/pallas_call | solution.py:248
  18.4 0.0 collective-permute-done.3.sibling_ref
  18.4 0.0 copy-done.1
  18.4 1.2 %shard_map.85 = (f32[512,128]{1,0:T(8,128)S(1)}, f32[128,128]{1,0:T(8,128)S(1)}, f32[128,128]{1,0:T(8,128)S(1)}) custom-call(f32[256,128]{1,0:T(8,128)S(1)} %get-tuple-element.27.own_ref, f32[256,128]{1,0:T(8,128)S(1)} %collective-permute-done.2.met_ref, f32[128,128]{1,0:T(8,128)S(1)} %collective-permute-done.1.met_pair_ref, ...), custom_call_target="tpu_custom_call" | custom-call | tf_op jit(solution)/shard_map/pallas_call | solution.py:248
  19.7 20.6 %all_to_all.10 = f32[64,8,128]{2,1,0:T(8,128)S(1)} all-to-all(f32[64,8,128]{2,1,0:T(8,128)S(1)} %bitcast.15), channel_id=1, replica_groups=mesh['z'=8,'yh'=2,'core'=2,'x'=4,'yl'=2] {'z','x','yl'}, dimensions={0} | all-to-all | bytes 524288 | tf_op jit(solution)/shard_map/all_to_all | solution.py:320
  40.3 0.1 collective-permute-start.4
  40.4 0.3 shard_map.86
  40.7 1.0 %collective-permute-done.4 = f32[64,4,128]{2,1,0:T(4,128)S(1)} collective-permute-done((f32[64,4,128]{2,1,0:T(4,128)S(1)}, f32[64,4,128]{2,1,0:T(4,128)S(1)}, u32[]{:S(2)}, u32[]{:S(2)}) %collective-permute-start.4) | collective-permute-done | bytes 131104 | tf_op jit(solution)/shard_map/ppermute | solution.py:322
  41.7 1.3 %shard_map.87 = f32[512,128]{1,0:T(8,128)} custom-call(f32[2,128,128]{2,1,0:T(8,128)S(1)} %get-tuple-element.33.l_ref, f32[2,128,128]{2,1,0:T(8,128)S(1)} %get-tuple-element.34.own_ref, f32[256,128]{1,0:T(8,128)S(1)} %bitcast.16), custom_call_target="tpu_custom_call" | custom-call | tf_op jit(solution)/shard_map/pallas_call | solution.py:248
  43.1 9.3 %all-to-all-start.1 = ((f32[128,4,128]{2,1,0:T(4,128)}), f32[128,4,128]{2,1,0:T(4,128)S(1)}, u32[]{:S(2)}, u32[]{:S(2)}) async-start(f32[128,4,128]{2,1,0:T(4,128)} %bitcast.7), calls=%async_computation.1 | async-start | bytes 524288 | tf_op jit(solution)/shard_map/all_to_all | solution.py:324
  52.4 3.1 %collective-permute-start.5 = (f32[128,128]{1,0:T(8,128)S(1)}, f32[128,128]{1,0:T(8,128)S(1)}, u32[]{:S(2)}, u32[]{:S(2)}) collective-permute-start(f32[128,128]{1,0:T(8,128)S(1)} %get-tuple-element.36), channel_id=1, source_target_pairs={{0,16},{16,0},{1,17},{17,1},{2,18},{18,2},{3,19},{19,3},{4,20},{20... | collective-permute-start | bytes 196616 | tf_op jit(solution)/shard_map/ppermute | solution.py:321
  55.4 3.3 %collective-permute-done.5.met_ref = f32[128,128]{1,0:T(8,128)S(1)} collective-permute-done((f32[128,128]{1,0:T(8,128)S(1)}, f32[128,128]{1,0:T(8,128)S(1)}, u32[]{:S(2)}, u32[]{:S(2)}) %collective-permute-start.5) | collective-permute-done | bytes 65568 | tf_op jit(solution)/shard_map/ppermute | solution.py:321
  58.8 0.0 copy-done.3
  58.8 0.4 shard_map.88.gates_ref
  59.2 7.7 %all-to-all-done.1 = f32[128,4,128]{2,1,0:T(4,128)S(1)} async-done(((f32[128,4,128]{2,1,0:T(4,128)}), f32[128,4,128]{2,1,0:T(4,128)S(1)}, u32[]{:S(2)}, u32[]{:S(2)}) %all-to-all-start.1) | async-done | bytes 262176 | tf_op jit(solution)/shard_map/all_to_all | solution.py:324
  66.8 0.0 copy-done.4
  66.8 1.0 %shard_map.89 = f32[8,2,16,128]{3,2,1,0:T(8,128)} custom-call(f32[512,128]{1,0:T(8,128)S(1)} %bitcast.12, f32[128,128]{1,0:T(8,128)S(1)} %get-tuple-element.35.kept_ref, f32[128,128]{1,0:T(8,128)S(1)} %collective-permute-done.5.met_ref, f32[2,128,128]{2,1,0:T(8,128)S(1)} %shard_map.88.gates_ref, f32[128,128]{1,0:T(8,128)S(1)} %copy-done.4), custom_call_target="tpu_custom_call" | custom-call | tf_op jit(solution)/shard_map/pallas_call | solution.py:248
  (5 shorter events, 0.0 us)
Async XLA Ops:
  0.0 12.4 %copy-start.5 = (f32[128,512]{1,0:T(8,128)S(1)}, f32[128,512]{1,0:T(8,128)}, u32[]{:S(2)}) copy-start(f32[128,512]{1,0:T(8,128)} %param.13) | copy-start | bytes 786436
  2.9 9.6 %copy-start = (f32[1024,128]{1,0:T(8,128)S(1)}, f32[1024,128]{1,0:T(8,128)}, u32[]{:S(2)}) copy-start(f32[1024,128]{1,0:T(8,128)} %w_outer_ref.1) | copy-start | bytes 1572868
  2.9 12.4 %collective-permute-start = (f32[256,128]{1,0:T(8,128)}, f32[256,128]{1,0:T(8,128)S(1)}, u32[]{:S(2)}, u32[]{:S(2)}) collective-permute-start(f32[256,128]{1,0:T(8,128)} %get-tuple-element.21), channel_id=1, source_target_pairs={{4,0},{32,1},{65,2},{102,3},{135,4},{166,5},{192,6},{226,7},{9,8},... | collective-permute-start | bytes 393224 | tf_op jit(solution)/shard_map/ppermute | solution.py:312
  8.7 6.6 %collective-permute-start.1 = (f32[128,128]{1,0:T(8,128)}, f32[128,128]{1,0:T(8,128)S(1)}, u32[]{:S(2)}, u32[]{:S(2)}) collective-permute-start(f32[128,128]{1,0:T(8,128)} %get-tuple-element.22), channel_id=1, source_target_pairs={{0,16},{16,0},{1,17},{17,1},{2,18},{18,2},{3,19},{19,3},{4,20},{20... | collective-permute-start | bytes 196616 | tf_op jit(solution)/shard_map/ppermute | solution.py:314
  10.7 6.9 %collective-permute-start.2 = (f32[256,128]{1,0:T(8,128)}, f32[256,128]{1,0:T(8,128)S(1)}, u32[]{:S(2)}, u32[]{:S(2)}) collective-permute-start(f32[256,128]{1,0:T(8,128)} %get-tuple-element.23.left_ref), channel_id=1, source_target_pairs={{0,17},{1,16},{16,1},{17,0},{2,19},{3,18},{18,3},{19,2},{4,21},{5,... | collective-permute-start | bytes 393224 | tf_op jit(solution)/shard_map/ppermute | solution.py:313
  12.5 0.9 %copy-start.2 = (f32[256,128]{1,0:T(8,128)S(1)}, f32[256,128]{1,0:T(8,128)}, u32[]{:S(2)}) copy-start(f32[256,128]{1,0:T(8,128)} %get-tuple-element.23.left_ref) | copy-start | bytes 393220
  15.3 3.1 %copy-start.1 = (f32[8,32,128]{2,1,0:T(8,128)S(1)}, f32[8,32,128]{2,1,0:T(8,128)}, u32[]{:S(2)}) copy-start(f32[8,32,128]{2,1,0:T(8,128)} %param.9) | copy-start | bytes 393220
  15.3 3.1 %collective-permute-start.3 = (f32[256,128]{1,0:T(8,128)S(1)}, f32[256,128]{1,0:T(8,128)S(1)}, u32[]{:S(2)}, u32[]{:S(2)}) collective-permute-start(f32[256,128]{1,0:T(8,128)S(1)} %collective-permute-done.panel_ref), channel_id=1, source_target_pairs={{0,8},{8,0},{1,9},{9,1},{2,10},{10,2},{3,11},{11,3},{4,12},{12,4},... | collective-permute-start | bytes 393224 | tf_op jit(solution)/shard_map/ppermute | solution.py:317
  40.3 1.4 %collective-permute-start.4 = (f32[64,4,128]{2,1,0:T(4,128)S(1)}, f32[64,4,128]{2,1,0:T(4,128)S(1)}, u32[]{:S(2)}, u32[]{:S(2)}) collective-permute-start(f32[64,4,128]{2,1,0:T(4,128)S(1)} %slice.4), channel_id=1, source_target_pairs={{0,8},{8,0},{1,9},{9,1},{2,10},{10,2},{3,11},{11,3},{4,12},{12,4},... | collective-permute-start | bytes 393224 | tf_op jit(solution)/shard_map/ppermute | solution.py:322
  43.1 15.7 %copy-start.3 = (f32[128,128]{1,0:T(8,128)S(1)}, f32[128,128]{1,0:T(8,128)}, u32[]{:S(2)}) copy-start(f32[128,128]{1,0:T(8,128)} %w_ref.2) | copy-start | bytes 196612
  43.1 23.8 %all-to-all-start.1 = ((f32[128,4,128]{2,1,0:T(4,128)}), f32[128,4,128]{2,1,0:T(4,128)S(1)}, u32[]{:S(2)}, u32[]{:S(2)}) async-start(f32[128,4,128]{2,1,0:T(4,128)} %bitcast.7), calls=%async_computation.1 | async-start | bytes 524288 | tf_op jit(solution)/shard_map/all_to_all | solution.py:324
  52.4 6.4 %collective-permute-start.5 = (f32[128,128]{1,0:T(8,128)S(1)}, f32[128,128]{1,0:T(8,128)S(1)}, u32[]{:S(2)}, u32[]{:S(2)}) collective-permute-start(f32[128,128]{1,0:T(8,128)S(1)} %get-tuple-element.36), channel_id=1, source_target_pairs={{0,16},{16,0},{1,17},{17,1},{2,18},{18,2},{3,19},{19,3},{4,20},{20... | collective-permute-start | bytes 196616 | tf_op jit(solution)/shard_map/ppermute | solution.py:321
  58.8 8.0 %copy-start.4 = (f32[128,128]{1,0:T(8,128)S(1)}, f32[128,128]{1,0:T(8,128)}, u32[]{:S(2)}) copy-start(f32[128,128]{1,0:T(8,128)} %w_ref.3) | copy-start | bytes 196612

commit v18 on v16

--- a/solution.py
+++ b/solution.py
@@ -101,8 +101,11 @@
         half_ref[pl.ds(p * 16, 16), :] = pair_ref[turned_rows(p), other]
 
 
-def weight_kernel(w_outer_ref, w_tri_ref, left_ref, outer_ref, tri_ref, kept_ref):
+def weight_kernel(
+    w_outer_ref, w_tri_ref, left_ref, pair_ref, outer_ref, tri_ref, kept_ref, kept_pair_ref
+):
     kept_ref[...] = left_ref[...]
+    kept_pair_ref[...] = pair_ref[...]
     for b in range(32):
         outer_ref[pl.ds(b * 32, 32), :] = halves(w_outer_ref[pl.ds(b, 32, stride=32), :])
     tri_ref[...] = halves(w_tri_ref[...])
@@ -290,7 +293,8 @@
 
 
 def prepared(*args):
-    return call(weight_kernel, [(1024, 256), (512, 256), (256, 128)], [], *args, short=2)
+    shapes = [(1024, 256), (512, 256), (256, 128), (8, 2, 16, 128)]
+    return call(weight_kernel, shapes, [], *args, short=2)
 
 
 def per_device(homolog, pair, w_first, w_second, w_outer, w_tri, w_gate, w_out):
@@ -300,8 +304,9 @@
     panel = lax.ppermute(right, ALL, panel_permutation())
     met = lax.ppermute(left, ("yh", "yl"), [(0, 3), (1, 2), (2, 1), (3, 0)])
     met_pair = lax.ppermute(half, "yh", swap)
-    ready = prepared(w_outer, w_tri.T, left)
-    panel, met_pair, (*weights, left) = lax.optimization_barrier((panel, met_pair, ready))
+    ready = prepared(w_outer, w_tri.T, left, pair)
+    panel, met_pair, ready = lax.optimization_barrier((panel, met_pair, ready))
+    *weights, left, pair = ready
     sibling = lax.ppermute(panel, "core", swap)
     update = block_update(left, met, panel, weights[0])
     edges, kept, sent = pair_stage(left, met, met_pair, sibling, update, pair, *weights)

time: 68.1 us -> 68.1 us (level)
  no operation moved by 1% of the time
where the time goes in v18:
time: 68.1 us; the launch traced here: 67.8 us
  starting transfers between devices  22 us (32%)
  blocking collectives  20.6 us (30%)
  waiting for transfers between devices  15.9 us (23%)
  Pallas kernels  8.18 us (12%)
  local copies, waits for them, and re-layouts  1.07 us (2%)
    all_to_all x1, blocking collectives, per_device(): swapped = lax.all_to_all(edges.reshape(64, 8, 128), LAYER, 0, 0, tiled=True)  20.6 us
    all_to_all x1, starting transfers between devices, per_device(): mixed = lax.all_to_all(back.reshape(128, 4, 128), CHIPS, 0, 0, tiled=True)  9.33 us
    pallas_call x8, Pallas kernels, call(): pl.pallas_call(kernel, out_shape=shapes if len(shapes) > 1 else shapes[0]...  8.18 us
    all_to_all x1, waiting for transfers between devices, per_device(): mixed = lax.all_to_all(back.reshape(128, 4, 128), CHIPS, 0, 0, tiled=True)  7.67 us
    ppermute x1, starting transfers between devices, per_device(): panel = lax.ppermute(right, ALL, panel_permutation())  5.83 us
    ppermute x1, waiting for transfers between devices, per_device(): returned = lax.ppermute(sent, 'yh', swap)  3.34 us
    ppermute x1, starting transfers between devices, per_device(): returned = lax.ppermute(sent, 'yh', swap)  3.06 us
    ppermute x1, waiting for transfers between devices, per_device(): met = lax.ppermute(left, ('yh', 'yl'), [(0, 3), (1, 2), (2, 1), (3, 0)])  2.28 us
  transfers between devices with their start and end apart: 7, of which 5 were waited for; matrix products, arithmetic and copies ran while one was open for 0% of the time, Pallas kernels for 3%

profile of v18, /device:TPU:2, one launch (start us, length us, event | category | flops | bytes accessed | tf_op | source)
XLA Modules:
  0.0 67.8 jit_solution(8641459582335882085)
XLA Ops:
  0.0 0.0 copy-start.5
  0.0 2.9 %shard_map.82 = (f32[256,128]{1,0:T(8,128)}, f32[256,128]{1,0:T(8,128)}, f32[128,128]{1,0:T(8,128)}) custom-call(f32[128,8,256]{2,1,0:T(8,128)} %msa_ref.1, f32[32,256]{1,0:T(8,128)} %bitcast.17, f32[32,256]{1,0:T(8,128)} %bitcast.18, f32[8,2,16,128]{3,2,1,0:T(8,128)} %bitcast.13), custom_call_target="tpu_custom_call" | custom-call | tf_op jit(solution)/shard_map/pallas_call | solution.py:246
  2.9 5.8 %collective-permute-start = (f32[256,128]{1,0:T(8,128)}, f32[256,128]{1,0:T(8,128)S(1)}, u32[]{:S(2)}, u32[]{:S(2)}) collective-permute-start(f32[256,128]{1,0:T(8,128)} %get-tuple-element.23), channel_id=1, source_target_pairs={{4,0},{32,1},{65,2},{102,3},{135,4},{166,5},{192,6},{226,7},{9,8},... | collective-permute-start | bytes 393224 | tf_op jit(solution)/shard_map/ppermute | solution.py:304
  8.7 2.0 %collective-permute-start.1 = (f32[128,128]{1,0:T(8,128)}, f32[128,128]{1,0:T(8,128)S(1)}, u32[]{:S(2)}, u32[]{:S(2)}) collective-permute-start(f32[128,128]{1,0:T(8,128)} %get-tuple-element.24), channel_id=1, source_target_pairs={{0,16},{16,0},{1,17},{17,1},{2,18},{18,2},{3,19},{19,3},{4,20},{20... | collective-permute-start | bytes 196616 | tf_op jit(solution)/shard_map/ppermute | solution.py:306
  10.7 1.7 %collective-permute-start.2 = (f32[256,128]{1,0:T(8,128)}, f32[256,128]{1,0:T(8,128)S(1)}, u32[]{:S(2)}, u32[]{:S(2)}) collective-permute-start(f32[256,128]{1,0:T(8,128)} %get-tuple-element.25.left_ref), channel_id=1, source_target_pairs={{0,17},{1,16},{16,1},{17,0},{2,19},{3,18},{18,3},{19,2},{4,21},{5,... | collective-permute-start | bytes 393224 | tf_op jit(solution)/shard_map/ppermute | solution.py:305
  12.4 0.0 copy-done.5
  12.4 0.1 copy.9
  12.5 0.0 copy-done.1
  12.5 0.0 copy-done
  12.5 0.0 copy-start.2
  12.5 0.9 %copy-done.2 = f32[256,128]{1,0:T(8,128)S(1)} copy-done((f32[256,128]{1,0:T(8,128)S(1)}, f32[256,128]{1,0:T(8,128)}, u32[]{:S(2)}) %copy-start.2) | copy-done | bytes 131096
  13.4 0.3 shard_map.83
  13.8 1.6 %collective-permute-done.1.met_pair_ref = f32[128,128]{1,0:T(8,128)S(1)} collective-permute-done((f32[128,128]{1,0:T(8,128)}, f32[128,128]{1,0:T(8,128)S(1)}, u32[]{:S(2)}, u32[]{:S(2)}) %collective-permute-start.1) | collective-permute-done | bytes 65568 | tf_op jit(solution)/shard_map/ppermute | solution.py:306
  15.3 0.0 collective-permute-done.panel_ref
  15.3 0.0 collective-permute-start.3
  15.4 2.3 %collective-permute-done.2.met_ref = f32[256,128]{1,0:T(8,128)S(1)} collective-permute-done((f32[256,128]{1,0:T(8,128)}, f32[256,128]{1,0:T(8,128)S(1)}, u32[]{:S(2)}, u32[]{:S(2)}) %collective-permute-start.2) | collective-permute-done | bytes 131104 | tf_op jit(solution)/shard_map/ppermute | solution.py:305
  17.6 0.8 %shard_map.84.update_ref = f32[128,128]{1,0:T(8,128)S(1)} custom-call(f32[256,128]{1,0:T(8,128)S(1)} %get-tuple-element.30.own_ref, f32[256,128]{1,0:T(8,128)S(1)} %collective-permute-done.2.met_ref, f32[256,128]{1,0:T(8,128)S(1)} %collective-permute-done.panel_ref, bf16[1024,256]{1,0:T(8,128)(2,1)S(1)} %get-tuple-element.33.w_outer_ref), custom_call_target="tpu_custom_call" | custom-call | tf_op jit(solution)/shard_map/pallas_call | solution.py:246
  18.4 0.0 collective-permute-done.3.sibling_ref
  18.4 1.2 %shard_map.85 = (f32[512,128]{1,0:T(8,128)S(1)}, f32[128,128]{1,0:T(8,128)S(1)}, f32[128,128]{1,0:T(8,128)S(1)}) custom-call(f32[256,128]{1,0:T(8,128)S(1)} %get-tuple-element.30.own_ref, f32[256,128]{1,0:T(8,128)S(1)} %collective-permute-done.2.met_ref, f32[128,128]{1,0:T(8,128)S(1)} %collective-permute-done.1.met_pair_ref, ...), custom_call_target="tpu_custom_call" | custom-call | tf_op jit(solution)/shard_map/pallas_call | solution.py:246
  19.7 20.6 %all_to_all.10 = f32[64,8,128]{2,1,0:T(8,128)S(1)} all-to-all(f32[64,8,128]{2,1,0:T(8,128)S(1)} %bitcast.15), channel_id=1, replica_groups=mesh['z'=8,'yh'=2,'core'=2,'x'=4,'yl'=2] {'z','x','yl'}, dimensions={0} | all-to-all | bytes 524288 | tf_op jit(solution)/shard_map/all_to_all | solution.py:313
  40.3 0.1 collective-permute-start.4
  40.4 0.3 shard_map.86
  40.7 1.0 %collective-permute-done.4 = f32[64,4,128]{2,1,0:T(4,128)S(1)} collective-permute-done((f32[64,4,128]{2,1,0:T(4,128)S(1)}, f32[64,4,128]{2,1,0:T(4,128)S(1)}, u32[]{:S(2)}, u32[]{:S(2)}) %collective-permute-start.4) | collective-permute-done | bytes 131104 | tf_op jit(solution)/shard_map/ppermute | solution.py:315
  41.7 1.3 %shard_map.87 = f32[512,128]{1,0:T(8,128)} custom-call(f32[2,128,128]{2,1,0:T(8,128)S(1)} %get-tuple-element.37.l_ref, f32[2,128,128]{2,1,0:T(8,128)S(1)} %get-tuple-element.38.own_ref, f32[256,128]{1,0:T(8,128)S(1)} %bitcast.16), custom_call_target="tpu_custom_call" | custom-call | tf_op jit(solution)/shard_map/pallas_call | solution.py:246
  43.1 9.3 %all-to-all-start.1 = ((f32[128,4,128]{2,1,0:T(4,128)}), f32[128,4,128]{2,1,0:T(4,128)S(1)}, u32[]{:S(2)}, u32[]{:S(2)}) async-start(f32[128,4,128]{2,1,0:T(4,128)} %bitcast.7), calls=%async_computation.1 | async-start | bytes 524288 | tf_op jit(solution)/shard_map/all_to_all | solution.py:317
  52.4 3.1 %collective-permute-start.5 = (f32[128,128]{1,0:T(8,128)S(1)}, f32[128,128]{1,0:T(8,128)S(1)}, u32[]{:S(2)}, u32[]{:S(2)}) collective-permute-start(f32[128,128]{1,0:T(8,128)S(1)} %get-tuple-element.40), channel_id=1, source_target_pairs={{0,16},{16,0},{1,17},{17,1},{2,18},{18,2},{3,19},{19,3},{4,20},{20... | collective-permute-start | bytes 196616 | tf_op jit(solution)/shard_map/ppermute | solution.py:314
  55.5 3.3 %collective-permute-done.5.met_ref = f32[128,128]{1,0:T(8,128)S(1)} collective-permute-done((f32[128,128]{1,0:T(8,128)S(1)}, f32[128,128]{1,0:T(8,128)S(1)}, u32[]{:S(2)}, u32[]{:S(2)}) %collective-permute-start.5) | collective-permute-done | bytes 65568 | tf_op jit(solution)/shard_map/ppermute | solution.py:314
  58.8 0.0 copy-done.3
  58.8 0.4 shard_map.88.gates_ref
  59.2 7.7 %all-to-all-done.1 = f32[128,4,128]{2,1,0:T(4,128)S(1)} async-done(((f32[128,4,128]{2,1,0:T(4,128)}), f32[128,4,128]{2,1,0:T(4,128)S(1)}, u32[]{:S(2)}, u32[]{:S(2)}) %all-to-all-start.1) | async-done | bytes 262176 | tf_op jit(solution)/shard_map/all_to_all | solution.py:317
  66.8 0.0 copy-done.4
  66.8 1.0 %shard_map.89 = f32[8,2,16,128]{3,2,1,0:T(8,128)} custom-call(f32[512,128]{1,0:T(8,128)S(1)} %bitcast.11, f32[128,128]{1,0:T(8,128)S(1)} %get-tuple-element.39.kept_ref, f32[128,128]{1,0:T(8,128)S(1)} %collective-permute-done.5.met_ref, f32[2,128,128]{2,1,0:T(8,128)S(1)} %shard_map.88.gates_ref, f32[128,128]{1,0:T(8,128)S(1)} %copy-done.4), custom_call_target="tpu_custom_call" | custom-call | tf_op jit(solution)/shard_map/pallas_call | solution.py:246
  (5 shorter events, 0.0 us)
Async XLA Ops:
  0.0 12.4 %copy-start.5 = (f32[128,512]{1,0:T(8,128)S(1)}, f32[128,512]{1,0:T(8,128)}, u32[]{:S(2)}) copy-start(f32[128,512]{1,0:T(8,128)} %param.13) | copy-start | bytes 786436
  0.0 12.5 %copy-start.1 = (f32[8,32,128]{2,1,0:T(8,128)S(1)}, f32[8,32,128]{2,1,0:T(8,128)}, u32[]{:S(2)}) copy-start(f32[8,32,128]{2,1,0:T(8,128)} %param.9) | copy-start | bytes 393220
  2.9 9.6 %copy-start = (f32[1024,128]{1,0:T(8,128)S(1)}, f32[1024,128]{1,0:T(8,128)}, u32[]{:S(2)}) copy-start(f32[1024,128]{1,0:T(8,128)} %w_outer_ref.1) | copy-start | bytes 1572868
  2.9 12.4 %collective-permute-start = (f32[256,128]{1,0:T(8,128)}, f32[256,128]{1,0:T(8,128)S(1)}, u32[]{:S(2)}, u32[]{:S(2)}) collective-permute-start(f32[256,128]{1,0:T(8,128)} %get-tuple-element.23), channel_id=1, source_target_pairs={{4,0},{32,1},{65,2},{102,3},{135,4},{166,5},{192,6},{226,7},{9,8},... | collective-permute-start | bytes 393224 | tf_op jit(solution)/shard_map/ppermute | solution.py:304
  8.7 6.6 %collective-permute-start.1 = (f32[128,128]{1,0:T(8,128)}, f32[128,128]{1,0:T(8,128)S(1)}, u32[]{:S(2)}, u32[]{:S(2)}) collective-permute-start(f32[128,128]{1,0:T(8,128)} %get-tuple-element.24), channel_id=1, source_target_pairs={{0,16},{16,0},{1,17},{17,1},{2,18},{18,2},{3,19},{19,3},{4,20},{20... | collective-permute-start | bytes 196616 | tf_op jit(solution)/shard_map/ppermute | solution.py:306
  10.7 6.9 %collective-permute-start.2 = (f32[256,128]{1,0:T(8,128)}, f32[256,128]{1,0:T(8,128)S(1)}, u32[]{:S(2)}, u32[]{:S(2)}) collective-permute-start(f32[256,128]{1,0:T(8,128)} %get-tuple-element.25.left_ref), channel_id=1, source_target_pairs={{0,17},{1,16},{16,1},{17,0},{2,19},{3,18},{18,3},{19,2},{4,21},{5,... | collective-permute-start | bytes 393224 | tf_op jit(solution)/shard_map/ppermute | solution.py:305
  12.5 0.9 %copy-start.2 = (f32[256,128]{1,0:T(8,128)S(1)}, f32[256,128]{1,0:T(8,128)}, u32[]{:S(2)}) copy-start(f32[256,128]{1,0:T(8,128)} %get-tuple-element.25.left_ref) | copy-start | bytes 393220
  15.3 3.1 %collective-permute-start.3 = (f32[256,128]{1,0:T(8,128)S(1)}, f32[256,128]{1,0:T(8,128)S(1)}, u32[]{:S(2)}, u32[]{:S(2)}) collective-permute-start(f32[256,128]{1,0:T(8,128)S(1)} %collective-permute-done.panel_ref), channel_id=1, source_target_pairs={{0,8},{8,0},{1,9},{9,1},{2,10},{10,2},{3,11},{11,3},{4,12},{12,4},... | collective-permute-start | bytes 393224 | tf_op jit(solution)/shard_map/ppermute | solution.py:310
  40.3 1.4 %collective-permute-start.4 = (f32[64,4,128]{2,1,0:T(4,128)S(1)}, f32[64,4,128]{2,1,0:T(4,128)S(1)}, u32[]{:S(2)}, u32[]{:S(2)}) collective-permute-start(f32[64,4,128]{2,1,0:T(4,128)S(1)} %slice.4), channel_id=1, source_target_pairs={{0,8},{8,0},{1,9},{9,1},{2,10},{10,2},{3,11},{11,3},{4,12},{12,4},... | collective-permute-start | bytes 393224 | tf_op jit(solution)/shard_map/ppermute | solution.py:315
  43.1 15.7 %copy-start.3 = (f32[128,128]{1,0:T(8,128)S(1)}, f32[128,128]{1,0:T(8,128)}, u32[]{:S(2)}) copy-start(f32[128,128]{1,0:T(8,128)} %w_ref.2) | copy-start | bytes 196612
  43.1 23.8 %all-to-all-start.1 = ((f32[128,4,128]{2,1,0:T(4,128)}), f32[128,4,128]{2,1,0:T(4,128)S(1)}, u32[]{:S(2)}, u32[]{:S(2)}) async-start(f32[128,4,128]{2,1,0:T(4,128)} %bitcast.7), calls=%async_computation.1 | async-start | bytes 524288 | tf_op jit(solution)/shard_map/all_to_all | solution.py:317
  52.4 6.4 %collective-permute-start.5 = (f32[128,128]{1,0:T(8,128)S(1)}, f32[128,128]{1,0:T(8,128)S(1)}, u32[]{:S(2)}, u32[]{:S(2)}) collective-permute-start(f32[128,128]{1,0:T(8,128)S(1)} %get-tuple-element.40), channel_id=1, source_target_pairs={{0,16},{16,0},{1,17},{17,1},{2,18},{18,2},{3,19},{19,3},{4,20},{20... | collective-permute-start | bytes 196616 | tf_op jit(solution)/shard_map/ppermute | solution.py:314
  58.8 8.0 %copy-start.4 = (f32[128,128]{1,0:T(8,128)S(1)}, f32[128,128]{1,0:T(8,128)}, u32[]{:S(2)}) copy-start(f32[128,128]{1,0:T(8,128)} %w_ref.3) | copy-start | bytes 196612
